TPU v7x, 256 devices: a whole 4x4x8 slice. The times are simulated.
256 devices in a mesh: occ: 8 (over x, core), ao: 32 (over y, z).
Axes of the slice: x: 4, y: 4, z: 8, core: 2. Of those that a mesh axis runs over, the one named last changes fastest.
Arguments:
- amplitudes: bfloat16 [4096, 128, 128], P('occ', 'ao'), may hold values from -6 to 6
- blocks: bfloat16 [128, 96, 128, 128], P('ao', 'occ'), may hold values from -0.078125 to 0.078125
- kets: int32 [128, 96], P('ao', 'occ'), may hold values from 0 to 127, as said below
- counts: int32 [128], P('ao'), may hold values from 24 to 96, as said below
Outputs:
- ladder: bfloat16 [4096, 128, 128], P('occ', 'ao')
Inputs may be any that keep to these rules, and one draw needn't show every extreme that they name: `kets`: the ket tiles of one bra tile's slots are distinct. `counts`: some bra tile has all 96 slots live.
All inputs are finite; a program needn't handle non-finite values.
Results may differ from a plain program's by a relative error of at most 0.001.
Values may be sent and summed in bfloat16 or wider, within the bound.
No kernel may reach another device: no remote copies, remote signals or barrier semaphores. Data moves between devices by JAX's collectives and lax.ppermute only.
A program may use at most 192 MiB of HBM per device.

v0:
```python
import jax
import jax.numpy as jnp
from jax import lax
from jax.sharding import PartitionSpec as P


def tile_terms(whole, block, ket_row, count):
    rows = whole.shape[0]
    width = whole.shape[2]
    slots = ket_row.shape[0]
    live = jnp.arange(slots, dtype=jnp.int32) < count
    chosen = jnp.take(whole, ket_row, axis=1)
    masked = jnp.where(live[:, None, None], block, jnp.zeros_like(block))
    return jnp.dot(
        chosen.reshape(rows, slots * width),
        masked.reshape(slots * width, width),
        preferred_element_type=jnp.float32,
    )


def on_device(amplitudes, blocks, kets, counts):
    tiles = blocks.shape[0]
    whole = lax.all_gather(amplitudes, "ao", axis=1, tiled=True)
    all_blocks, all_kets = (
        lax.all_gather(blocks, "occ", axis=1, tiled=True),
        lax.all_gather(kets, "occ", axis=1, tiled=True),
    )
    parts = [tile_terms(whole, all_blocks[b], all_kets[b], counts[b]) for b in range(tiles)]
    total = jnp.stack(parts, axis=1)
    return total.astype(jnp.bfloat16)


def solution(mesh):
    placed = (P("occ", "ao", None), P("ao", "occ", None, None), P("ao", "occ"), P("ao"))
    return jax.shard_map(
        on_device, mesh=mesh, in_specs=placed, out_specs=P("occ", "ao", None), check_vma=False
    )
```

profile of v0, /device:TPU:96, one launch (start us, length us, event | category | flops | bytes accessed | tf_op | source)
XLA Modules:
  0.0 261.9 jit_solution(14570856816574903529)
XLA Ops:
  6.5 0.0 all-gather.4.cloned.1.call-start
  6.5 1.9 copy.14
  8.4 0.0 all-gather.4.cloned.1.call-update
  8.5 0.0 all-gather.6.cloned.1.call-start
  8.5 0.7 all-gather.6.cloned.1.call-update
  9.2 12.1 %all-gather = s32[8,12,4]{1,2,0:T(4,128)S(1)} all-gather(s32[1,12,4]{1,2,0:T(4,128)} %bitcast.137), channel_id=1, replica_groups=mesh['occ'=8,'ao'=32] {'occ'}, dimensions={0}, use_global_device_ids=true | all-gather | bytes 1728 | tf_op jit(solution)/shard_map/all_gather | solution.py:26
  21.3 0.1 reshape.66
  21.4 1.5 fusion.104
  22.8 0.6 iota_compare_fusion.3
  23.5 0.7 iota_compare_fusion.2
  24.2 0.6 iota_compare_fusion
  24.8 0.7 iota_compare_fusion.1
  25.6 126.3 %all-gather.4.cloned.1.call-done = bf16[512,128,128]{2,0,1:T(8,128)(2,1)} async-done(((bf16[512,4,128]{2,0,1:T(8,128)(2,1)}), bf16[512,128,128]{2,0,1:T(8,128)(2,1)}) %all-gather.4.cloned.1.call-update) | async-done | bytes 16777232 | tf_op jit(solution)/shard_map/all_gather | solution.py:23
  151.9 12.9 %gather_fusion.3 = bf16[96,512,128]{2,1,0:T(8,128)(2,1)} fusion(bf16[512,128,128]{2,0,1:T(8,128)(2,1)} %all-gather.4.cloned.1.call-done, s32[1024]{0:T(1024)S(1)} %get-tuple-element.24), kind=kCustom, calls=%fused_computation.3.clone | custom fusion | bytes 25166208 | tf_op jit(solution)/shard_map/jit(_take)/gather | solution.py:12
  164.8 13.9 %gather_fusion.2 = bf16[96,512,128]{2,1,0:T(8,128)(2,1)} fusion(bf16[512,128,128]{2,0,1:T(8,128)(2,1)} %all-gather.4.cloned.1.call-done, s32[1024]{0:T(1024)S(1)} %get-tuple-element.25), kind=kCustom, calls=%fused_computation.2.clone | custom fusion | bytes 25166208 | tf_op jit(solution)/shard_map/jit(_take)/gather | solution.py:12
  178.8 13.0 %gather_fusion.1 = bf16[96,512,128]{2,1,0:T(8,128)(2,1)} fusion(bf16[512,128,128]{2,0,1:T(8,128)(2,1)} %all-gather.4.cloned.1.call-done, s32[1024]{0:T(1024)S(1)} %get-tuple-element.26), kind=kCustom, calls=%fused_computation.1.clone | custom fusion | bytes 25166208 | tf_op jit(solution)/shard_map/jit(_take)/gather | solution.py:12
  191.7 13.0 %gather_fusion = bf16[96,512,128]{2,1,0:T(8,128)(2,1)} fusion(bf16[512,128,128]{2,0,1:T(8,128)(2,1)} %all-gather.4.cloned.1.call-done, s32[1024]{0:T(1024)S(1)} %get-tuple-element.27), kind=kCustom, calls=%fused_computation.clone | custom fusion | bytes 25166208 | tf_op jit(solution)/shard_map/jit(_take)/gather | solution.py:12
  204.8 16.4 %all-gather.6.cloned.1.call-done = bf16[4,96,128,128]{3,2,1,0:T(8,128)(2,1)} async-done(((bf16[4,12,128,128]{3,2,1,0:T(8,128)(2,1)}), bf16[4,96,128,128]{3,2,1,0:T(8,128)(2,1)}) %all-gather.6.cloned.1.call-update) | async-done | bytes 12582928 | tf_op jit(solution)/shard_map/all_gather | solution.py:25
  221.2 8.9 %fusion.91 = bf16[512,1,128]{2,0,1:T(8,128)(2,1)S(1)} fusion(bf16[4,96,128,128]{3,2,1,0:T(8,128)(2,1)} %all-gather.6.cloned.1.call-done, pred[96]{0:T(512)(128)(4,1)S(1)} %iota_compare_fusion, bf16[96,512,128]{2,1,0:T(8,128)(2,1)} %gather_fusion.3, pred[96]{0:T(512)(128)(4,1)S(1)} %get-tuple-element.14), kind=kOutput, calls=%fused_computation.51 | convolution fusion | flops 1618542592 | bytes 15859904 | tf_op jit(solution)/shard_map/dot_general | solution.py:14
  230.1 0.0 slice-start
  230.1 0.0 slice-start.1
  230.2 9.1 %fusion.86 = bf16[512,1,128]{2,0,1:T(8,128)(2,1)S(1)} fusion(bf16[4,96,128,128]{3,2,1,0:T(8,128)(2,1)} %all-gather.6.cloned.1.call-done, pred[96]{0:T(512)(128)(4,1)S(1)} %iota_compare_fusion.1, bf16[96,512,128]{2,1,0:T(8,128)(2,1)} %gather_fusion.2, pred[96]{0:T(512)(128)(4,1)S(1)} %get-tuple-element.16), kind=kOutput, calls=%fused_computation.50 | convolution fusion | flops 1618542592 | bytes 15859904 | tf_op jit(solution)/shard_map/dot_general | solution.py:14
  239.3 0.0 slice-start.2
  239.3 9.1 %fusion.81 = bf16[512,1,128]{2,0,1:T(8,128)(2,1)S(1)} fusion(bf16[4,96,128,128]{3,2,1,0:T(8,128)(2,1)} %all-gather.6.cloned.1.call-done, pred[96]{0:T(512)(128)(4,1)S(1)} %iota_compare_fusion.2, bf16[96,512,128]{2,1,0:T(8,128)(2,1)} %gather_fusion.1, pred[96]{0:T(512)(128)(4,1)S(1)} %get-tuple-element.18), kind=kOutput, calls=%fused_computation.49 | convolution fusion | flops 1618542592 | bytes 15859904 | tf_op jit(solution)/shard_map/dot_general | solution.py:14
  248.4 0.0 slice-done
  248.4 0.0 slice-done.1
  248.4 0.0 slice-done.2
  248.4 5.4 %fusion.76 = bf16[512,1,128]{2,0,1:T(8,128)(2,1)S(1)} fusion(bf16[4,96,128,128]{3,2,1,0:T(8,128)(2,1)} %all-gather.6.cloned.1.call-done, pred[96]{0:T(512)(128)(4,1)S(1)} %iota_compare_fusion.3, bf16[96,512,128]{2,1,0:T(8,128)(2,1)S(1)} %bitcast.135, pred[96]{0:T(512)(128)(4,1)S(1)} %get-tuple-element.6), kind=kOutput, calls=%fused_computation.48 | convolution fusion | flops 1618542592 | bytes 15859904 | tf_op jit(solution)/shard_map/dot_general | solution.py:14
  253.8 0.1 pad_maximum_fusion
  253.9 1.2 copy.15
  (5 shorter events, 0.0 us)
Async XLA Ops:
  6.5 145.3 %all-gather.4.cloned.1.call-start = ((), (), s32[]{:S(2)}) async-start(), calls=%async_computation | async-start | bytes 17301504 | tf_op jit(solution)/shard_map/all_gather | solution.py:23
  8.5 212.7 %all-gather.6.cloned.1.call-start = ((), (), s32[]{:S(2)}) async-start(), calls=%async_computation.1 | async-start | bytes 14155776 | tf_op jit(solution)/shard_map/all_gather | solution.py:25
  230.1 18.2 %slice-start = ((s8[12582912]{0:T(1024)(128)(4,1)}), s8[4194304]{0:T(1024)(128)(4,1)S(1)}, s32[]{:S(2)}) async-start(s8[12582912]{0:T(1024)(128)(4,1)} %bitcast.134), calls=%async_computation.2 | async-start | bytes 8388608
  230.1 18.2 %slice-start.1 = ((s8[12582912]{0:T(1024)(128)(4,1)}), s8[4194304]{0:T(1024)(128)(4,1)S(1)}, s32[]{:S(2)}) async-start(s8[12582912]{0:T(1024)(128)(4,1)} %bitcast.134), calls=%async_computation.3 | async-start | bytes 8388608
  239.3 9.1 %slice-start.2 = ((s8[12582912]{0:T(1024)(128)(4,1)}), s8[4194304]{0:T(1024)(128)(4,1)S(1)}, s32[]{:S(2)}) async-start(s8[12582912]{0:T(1024)(128)(4,1)} %bitcast.134), calls=%async_computation.4 | async-start | bytes 8388608
Sparse Core Ops, SparseCore 0:
  9.9 141.8 all-gather.3
  153.7 67.4 all-gather.5
where the time goes:
time: 265 us; the launch traced here: 262 us
  waiting for transfers between devices  143 us (54%)
  local copies, waits for them, and re-layouts  57.5 us (22%)
  matrix products  32.5 us (12%)
  between operations  13.5 us (5%)
  blocking collectives  12.1 us (5%)
  other arithmetic  2.75 us (1%)
    all_gather x1, waiting for transfers between devices, on_device(): whole = lax.all_gather(amplitudes, 'ao', axis=1, tiled=True)  126 us
    gather x4, local copies, waits for them, and re-layouts, tile_terms(): chosen = jnp.take(whole, ket_row, axis=1)  52.9 us
    dot_general x4, matrix products, tile_terms(): jnp.dot(chosen.reshape(rows, slots * width), masked.reshape(slots * width...  32.5 us
    all_gather x1, waiting for transfers between devices, on_device(): lax.all_gather(blocks, 'occ', axis=1, tiled=True)  16.4 us
    all_gather x1, blocking collectives, on_device(): lax.all_gather(kets, 'occ', axis=1, tiled=True)  12.1 us
  transfers between devices with their start and end apart: 2, of which 2 were waited for; matrix products, arithmetic and copies ran while one was open for 22% of the time, Pallas kernels for 0%

commit v1 on v0

v1 whole, which is shorter than its diff:
```python
import functools

import jax
import jax.numpy as jnp
from jax import lax
from jax.experimental import pallas as pl
from jax.experimental.pallas import tpu as pltpu
from jax.sharding import Mesh, PartitionSpec as P

AXES = ("x", "core", "y", "z")
NX, NC, NY, NZ = 4, 2, 4, 8
TILES, SLOTS, WIDTH = 4, 12, 128
BODY = TILES * SLOTS * WIDTH
VMEM = pl.BlockSpec(memory_space=pltpu.VMEM)
SMEM = pl.BlockSpec(memory_space=pltpu.SMEM)


def near(v):
    return pltpu.with_memory_space_constraint(v, pltpu.VMEM)


def pass_kernel(*refs):
    pass


class Order:
    def __init__(self):
        self.token = jnp.zeros((8, WIDTH), jnp.float32)

    def meet(self, *places):
        values = [near(v) for v in [self.token] + [a[k] for a, k in places]]
        held = pl.pallas_call(
            pass_kernel,
            out_shape=[pltpu.VMEM(v.shape, v.dtype) for v in values],
            in_specs=[VMEM] * len(values),
            out_specs=[VMEM] * len(values),
            input_output_aliases={i: i for i in range(len(values))},
            compiler_params=pltpu.CompilerParams(vmem_limit_bytes=1 << 20),
            cost_estimate=pl.CostEstimate(flops=0, bytes_accessed=0, transcendentals=0),
            name="meet",
        )(*values)
        self.token = held[0]
        for (a, k), value in zip(places, held[1:]):
            a[k] = value


def pack_kernel(first, second, out):
    rows = first.shape[0]

    def one(i, _):
        at = pl.multiple_of(i * 80, 16)
        out[pl.ds(at, 80), :] = first[pl.ds(at, 80), :]
        out[pl.ds(rows + at, 80), :] = second[pl.ds(at, 80), :]
        return 0

    lax.fori_loop(0, rows // 80, one, 0)


def pack(first, second):
    return pl.pallas_call(
        pack_kernel,
        out_shape=pltpu.VMEM((2 * first.shape[0], WIDTH), first.dtype),
        in_specs=[VMEM] * 2,
        out_specs=VMEM,
        compiler_params=pltpu.CompilerParams(vmem_limit_bytes=1 << 20),
        name="pack",
    )(near(first), near(second))


def pairs_of(move):
    pairs = []
    for x in range(NX):
        for c in range(NC):
            for y in range(NY):
                for z in range(NZ):
                    tx, tc, ty, tz = move(x, c, y, z)
                    to = ((tx % NX * NC + tc) * NY + ty) * NZ + tz % NZ
                    pairs.append((((x * NC + c) * NY + y) * NZ + z, to))
    return pairs


ALONG_X = pairs_of(lambda x, c, y, z: (x + 1 - 2 * c, c, y, z))
BACK_X = pairs_of(lambda x, c, y, z: (x - 1 + 2 * c, c, y, z))
ALONG_Z = pairs_of(lambda x, c, y, z: (x, c, y, z + 1 - 2 * c))
BACK_Z = pairs_of(lambda x, c, y, z: (x, c, y, z - 1 + 2 * c))
PARTNER = pairs_of(lambda x, c, y, z: (x, c, y ^ (1 + 2 * c), z))
CROSS = pairs_of(lambda x, c, y, z: (x, c, y ^ (3 - 2 * c), z))
OTHER_CORE = pairs_of(lambda x, c, y, z: (x, 1 - c, y, z))


def send(v, pairs, name):
    with jax.named_scope(name):
        return lax.ppermute(v, AXES, pairs)


def spread_kernel(fresh, steps, counts, *refs):
    dense, listed, kets = refs[-3:]
    shards = [
        ref.at[pl.ds(at, BODY + 16), :] for ref in refs[:-3 if fresh else -4] for at in range(0, ref.shape[0], BODY + 16)
    ]
    x, c, y, z = (lax.axis_index(a) for a in AXES)
    sign = 1 - 2 * c
    for i, shard in enumerate(shards):
        listed[...] = shard[BODY:BODY + 16, :].astype(jnp.float32).astype(jnp.int32)
        pltpu.sync_copy(listed, kets.at[i])
    if fresh:
        def wipe(i, _):
            dense[pl.ds(pl.multiple_of(i * 256, 256), 256), :] = jnp.zeros((256, dense.shape[1]), dense.dtype)
            return 0

        lax.fori_loop(0, dense.shape[0] // 256, wipe, 0)
    for i, (shard, (dx, own)) in enumerate(zip(shards, steps)):
        if own:
            source = ((x - sign * dx) & (NX - 1)) * NC + c
        else:
            source = ((x + sign * dx) & (NX - 1)) * NC + 1 - c

        def one(j, _, i=i, shard=shard, source=source):
            for b in range(TILES):
                k = kets[i, b, j]
                dz = (sign * (z - ((k >> 2) & 7))) & 7
                dy = y ^ (k >> 5)
                kind = jnp.where(dy == 0, 0, jnp.where(dy == 2, 3, jnp.where(dy == 1, 1 + c, 2 - c)))
                p = (dz * 4 + kind) * 4 + (k & 3)

                @pl.when(source * SLOTS + j < counts[b])
                def _():
                    block = shard[pl.ds(pl.multiple_of((b * SLOTS + j) * WIDTH, WIDTH), WIDTH), :]
                    dense[pl.ds(pl.multiple_of(p * WIDTH, WIDTH), WIDTH), b * WIDTH:(b + 1) * WIDTH] = block
            return 0

        lax.fori_loop(0, SLOTS, one, 0)


def spread(counts, shards, steps, dense=None):
    fresh = dense is None
    args = (counts,) + tuple(near(v) for v in tuple(shards) + (() if fresh else (dense,)))
    return pl.pallas_call(
        functools.partial(spread_kernel, fresh, steps),
        out_shape=pltpu.VMEM((NY * NZ * TILES * WIDTH, TILES * WIDTH), jnp.bfloat16),
        in_specs=[SMEM] + [VMEM] * (len(args) - 1),
        out_specs=VMEM,
        scratch_shapes=[pltpu.VMEM((16, WIDTH), jnp.int32), pltpu.SMEM((len(steps), 16, WIDTH), jnp.int32)],
        input_output_aliases={} if fresh else {len(args) - 1: 0},
        compiler_params=pltpu.CompilerParams(vmem_limit_bytes=4 << 20),
        cost_estimate=pl.CostEstimate(flops=0, bytes_accessed=6 << 20, transcendentals=0),
        name="spread",
    )(*args)


def terms_kernel(places, fresh, *refs):
    dense, out = refs[0], refs[-1]
    pieces = refs[1 if fresh else 2:-1]
    acc = None if fresh else refs[1][...]
    for piece, q in zip(pieces, places):
        left = jnp.concatenate([piece[t] for t in range(TILES)], axis=1)
        part = jnp.dot(left, dense[q * 512:(q + 1) * 512, :], preferred_element_type=jnp.float32)
        acc = part if acc is None else acc + part
    out[...] = acc.astype(out.dtype)


def add_terms(dense, total, pieces, dtype=jnp.float32):
    rows = pieces[0][0].shape[1]
    fresh = total is None
    args = (dense,) + (() if fresh else (total,)) + tuple(v for v, _ in pieces)
    return pl.pallas_call(
        functools.partial(terms_kernel, [q for _, q in pieces], fresh),
        out_shape=pltpu.VMEM((rows, TILES * WIDTH), dtype),
        in_specs=[VMEM] * len(args),
        out_specs=VMEM,
        compiler_params=pltpu.CompilerParams(vmem_limit_bytes=6 << 20),
        cost_estimate=pl.CostEstimate(
            flops=2 * rows * 512 * 512 * len(pieces), bytes_accessed=len(pieces) << 20, transcendentals=0
        ),
        name="terms",
    )(*(near(v) for v in args))


def on_device(amplitudes, blocks, kets, counts):
    own = jnp.transpose(amplitudes, (1, 0, 2))
    listed = jnp.pad(kets.astype(jnp.bfloat16), ((0, 16 - TILES), (0, WIDTH - SLOTS)))
    load = jnp.concatenate([blocks.reshape(BODY, WIDTH), listed], axis=0)

    s, q, u, v = {0: own}, {}, {}, {}
    bx, ox, dense = {0: load}, {}, {}
    order = Order()

    def along(a, k, name):
        a[k] = send(a[k - 1], ALONG_Z, name + str(k))

    def cross(a, b, k, name):
        b[k] = send(a[k], CROSS, name + str(k))

    along(s, 1, "s")
    q[0] = send(own, PARTNER, "q0")
    bx[1] = send(load, ALONG_X, "bx1")
    ox[0] = send(load, OTHER_CORE, "ox0")
    cross(s, u, 0, "u")

    order.meet((s, 1), (q, 0), (ox, 0))
    along(s, 2, "s")
    along(q, 1, "q")
    cross(s, u, 1, "u")
    dense[0] = spread(counts, [bx[0], ox[0]], [(0, True), (0, False)])
    order.meet((u, 0))
    cross(q, v, 0, "v")

    order.meet((s, 2), (u, 1), (bx, 1), (dense, 0))
    along(s, 3, "s")
    cross(s, u, 2, "u")
    bx[2] = send(bx[1], ALONG_X, "bx2")
    order.meet((q, 1), (v, 0))
    along(q, 2, "q")
    cross(q, v, 1, "v")
    dense[1] = spread(counts, [bx[1]], [(1, True)], dense[0])

    order.meet((s, 3), (u, 2), (dense, 1))
    along(s, 4, "s")
    cross(s, u, 3, "u")
    order.meet((q, 2), (v, 1))
    along(q, 3, "q")
    cross(q, v, 2, "v")

    order.meet((s, 4), (u, 3), (bx, 2))
    along(s, 5, "s")
    cross(s, u, 4, "u")
    both = pack(bx[1], bx[2])
    ox[1] = send(both, OTHER_CORE, "ox12")
    order.meet((q, 3), (v, 2))
    along(q, 4, "q")
    cross(q, v, 3, "v")
    dense[2] = spread(counts, [bx[2]], [(2, True)], dense[1])

    order.meet((s, 5), (u, 4), (ox, 1), (dense, 2))
    along(s, 6, "s")
    cross(s, u, 5, "u")
    bx[3] = send(bx[2], ALONG_X, "bx3")
    order.meet((q, 4), (v, 3))
    along(q, 5, "q")
    cross(q, v, 4, "v")
    dense[3] = spread(counts, [ox[1]], [(1, False), (2, False)], dense[2])

    order.meet((s, 6), (u, 5), (dense, 3))
    along(s, 7, "s")
    cross(s, u, 6, "u")
    order.meet((q, 5), (v, 4))
    along(q, 6, "q")
    cross(q, v, 5, "v")

    order.meet((s, 7), (u, 6), (bx, 3))
    cross(s, u, 7, "u")
    q[7] = send(q[0], BACK_Z, "q7")
    ox[3] = send(bx[3], OTHER_CORE, "ox3")
    dense[4] = spread(counts, [bx[3]], [(3, True)], dense[3])
    order.meet((q, 6), (v, 5), (dense, 4))
    cross(q, v, 6, "v")

    order.meet((u, 7), (q, 7), (ox, 3))
    cross(q, v, 7, "v")
    dense = spread(counts, [ox[3]], [(3, False)], dense[4])

    def terms(ks, names):
        return [(a[k], k * 4 + i) for k in ks for i, a in enumerate((s, q, u, v)) if "squv"[i] in names]

    total = add_terms(dense, None, terms(range(0, 3), "squv"))
    total = add_terms(dense, total, terms(range(3, 6), "squv"))
    total = add_terms(dense, total, terms((6,), "squv") + terms((7,), "squ"))
    out = add_terms(dense, total, terms((7,), "v"), jnp.bfloat16)
    return out.reshape(out.shape[0], TILES, WIDTH)


def solution(mesh):
    grid = Mesh(mesh.devices.reshape(NX, NC, NY, NZ), AXES)
    placed = (
        P(("x", "core"), ("y", "z"), None),
        P(("y", "z"), ("x", "core"), None, None),
        P(("y", "z"), ("x", "core")),
        P(("y", "z")),
    )
    return jax.shard_map(
        on_device, mesh=grid, in_specs=placed, out_specs=P(("x", "core"), ("y", "z"), None), check_vma=False
    )
```

time: 265 us -> 143 us (0.54)
  the two profiles are of different devices: /device:TPU:96 before, /device:TPU:6 now
where the time goes in v1:
time: 143 us; the launch traced here: 142 us
  waiting for transfers between devices  59.7 us (42%)
  starting transfers between devices  52.8 us (37%)
  Pallas kernels  26.4 us (18%)
  other arithmetic  2.27 us (2%)
    ppermute x37, waiting for transfers between devices, send(): return lax.ppermute(v, AXES, pairs)  59.7 us
    ppermute x37, starting transfers between devices, send(): return lax.ppermute(v, AXES, pairs)  52.8 us
    pallas_call x6, Pallas kernels, spread(): pl.pallas_call(functools.partial(spread_kernel, fresh, steps), out_shape=...  16.5 us
    pallas_call x4, Pallas kernels, add_terms(): pl.pallas_call(functools.partial(terms_kernel, [q for _, q in pieces], fr...  9.29 us
  transfers between devices with their start and end apart: 37, of which 21 were waited for; matrix products, arithmetic and copies ran while one was open for 0% of the time, Pallas kernels for 18%

profile of v1, /device:TPU:6, one launch (start us, length us, event | category | flops | bytes accessed | tf_op | source)
XLA Modules:
  0.0 142.3 jit_solution(1717136392875492916)
XLA Ops:
  2.4 2.3 %collective-permute-start.6 = (bf16[6160,128]{1,0:T(8,128)(2,1)S(1)}, bf16[6160,128]{1,0:T(8,128)(2,1)S(1)}, u32[]{:S(2)}, u32[]{:S(2)}) collective-permute-start(bf16[6160,128]{1,0:T(8,128)(2,1)S(1)} %fusion.1.refs_0_), channel_id=1, source_target_pairs={{0,64},{1,65},{2,66},{3,67},{4,68},{5,69},{6,70},{7,71},{8,72},{9,... | collective-permute-start | bytes 4730888 | tf_op jit(solution)/shard_map/bx1/ppermute | solution.py:93
  6.6 2.2 %collective-permute-start.3 = (bf16[4,512,128]{2,1,0:T(8,128)(2,1)S(1)}, bf16[4,512,128]{2,1,0:T(8,128)(2,1)S(1)}, u32[]{:S(2)}, u32[]{:S(2)}) collective-permute-start(bf16[4,512,128]{2,1,0:T(8,128)(2,1)S(1)} %bitcast.6), channel_id=1, source_target_pairs={{0,24},{1,25},{2,26},{3,27},{4,28},{5,29},{6,30},{7,31},{8,16},{9,... | collective-permute-start | bytes 1572872 | tf_op jit(solution)/shard_map/u0/ppermute | solution.py:93
  8.8 7.3 %collective-permute-done.refs_1_ = bf16[4,512,128]{2,1,0:T(8,128)(2,1)S(1)} collective-permute-done((bf16[4,512,128]{2,1,0:T(8,128)(2,1)S(1)}, bf16[4,512,128]{2,1,0:T(8,128)(2,1)S(1)}, u32[]{:S(2)}, u32[]{:S(2)}) %collective-permute-start) | collective-permute-done | bytes 524320 | tf_op jit(solution)/shard_map/s1/ppermute | solution.py:93
  16.1 5.2 %collective-permute-start.4 = (bf16[4,512,128]{2,1,0:T(8,128)(2,1)S(1)}, bf16[4,512,128]{2,1,0:T(8,128)(2,1)S(1)}, u32[]{:S(2)}, u32[]{:S(2)}) collective-permute-start(bf16[4,512,128]{2,1,0:T(8,128)(2,1)S(1)} %get-tuple-element.61.refs_5_), channel_id=1, source_target_pairs={{0,1},{1,2},{2,3},{3,4},{4,5},{5,6},{6,7},{7,0},{8,9},{9,10},{10,1... | collective-permute-start | bytes 1572872 | tf_op jit(solution)/shard_map/s2/ppermute | solution.py:93
  22.5 4.6 %spread.6.refs_4_ = bf16[16384,512]{1,0:T(8,128)(2,1)S(1)} custom-call(s32[4]{0:T(128)S(1)} %copy-done, bf16[6160,128]{1,0:T(8,128)(2,1)S(1)} %fusion.1.refs_0_, bf16[6160,128]{1,0:T(8,128)(2,1)S(1)} %get-tuple-element.62.refs_1_), custom_call_target="tpu_custom_call" | custom-call | bytes 6291456 | tf_op jit(solution)/shard_map/spread/pallas_call | solution.py:138
  28.4 3.3 %collective-permute-done.5.refs_2_ = bf16[4,512,128]{2,1,0:T(8,128)(2,1)S(1)} collective-permute-done((bf16[4,512,128]{2,1,0:T(8,128)(2,1)S(1)}, bf16[4,512,128]{2,1,0:T(8,128)(2,1)S(1)}, u32[]{:S(2)}, u32[]{:S(2)}) %collective-permute-start.5) | collective-permute-done | bytes 524320 | tf_op jit(solution)/shard_map/u1/ppermute | solution.py:93
  34.6 2.7 %collective-permute-start.8 = (bf16[4,512,128]{2,1,0:T(8,128)(2,1)S(1)}, bf16[4,512,128]{2,1,0:T(8,128)(2,1)S(1)}, u32[]{:S(2)}, u32[]{:S(2)}) collective-permute-start(bf16[4,512,128]{2,1,0:T(8,128)(2,1)S(1)} %get-tuple-element.64.refs_2_), channel_id=1, source_target_pairs={{0,24},{1,25},{2,26},{3,27},{4,28},{5,29},{6,30},{7,31},{8,16},{9,... | collective-permute-start | bytes 1572872 | tf_op jit(solution)/shard_map/v0/ppermute | solution.py:93
  37.8 4.0 %collective-permute-start.9 = (bf16[4,512,128]{2,1,0:T(8,128)(2,1)S(1)}, bf16[4,512,128]{2,1,0:T(8,128)(2,1)S(1)}, u32[]{:S(2)}, u32[]{:S(2)}) collective-permute-start(bf16[4,512,128]{2,1,0:T(8,128)(2,1)S(1)} %get-tuple-element.66.refs_9_), channel_id=1, source_target_pairs={{0,1},{1,2},{2,3},{3,4},{4,5},{5,6},{6,7},{7,0},{8,9},{9,10},{10,1... | collective-permute-start | bytes 1572872 | tf_op jit(solution)/shard_map/s3/ppermute | solution.py:93
  45.0 4.0 %collective-permute-start.11 = (bf16[4,512,128]{2,1,0:T(8,128)(2,1)S(1)}, bf16[4,512,128]{2,1,0:T(8,128)(2,1)S(1)}, u32[]{:S(2)}, u32[]{:S(2)}) collective-permute-start(bf16[4,512,128]{2,1,0:T(8,128)(2,1)S(1)} %get-tuple-element.70.refs_6_), channel_id=1, source_target_pairs={{0,1},{1,2},{2,3},{3,4},{4,5},{5,6},{6,7},{7,0},{8,9},{9,10},{10,1... | collective-permute-start | bytes 1572872 | tf_op jit(solution)/shard_map/q2/ppermute | solution.py:93
  49.6 2.0 %spread.7.refs_3_ = bf16[16384,512]{1,0:T(8,128)(2,1)S(1)} custom-call(s32[4]{0:T(128)S(1)} %copy-done, bf16[6160,128]{1,0:T(8,128)(2,1)S(1)} %get-tuple-element.67.refs_0_.first, bf16[16384,512]{1,0:T(8,128)(2,1)S(1)} %get-tuple-element.68.refs_1_), custom_call_target="tpu_custom_call", output_to_operand_aliasing={{}: (2, {})} | custom-call | bytes 6291456 | tf_op jit(solution)/shard_map/spread/pallas_call | solution.py:138
  51.6 3.3 %collective-permute-start.13 = (bf16[4,512,128]{2,1,0:T(8,128)(2,1)S(1)}, bf16[4,512,128]{2,1,0:T(8,128)(2,1)S(1)}, u32[]{:S(2)}, u32[]{:S(2)}) collective-permute-start(bf16[4,512,128]{2,1,0:T(8,128)(2,1)S(1)} %get-tuple-element.72.refs_2_), channel_id=1, source_target_pairs={{0,1},{1,2},{2,3},{3,4},{4,5},{5,6},{6,7},{7,0},{8,9},{9,10},{10,1... | collective-permute-start | bytes 1572872 | tf_op jit(solution)/shard_map/s4/ppermute | solution.py:93
  55.6 3.7 %collective-permute-done.12.refs_2_ = bf16[4,512,128]{2,1,0:T(8,128)(2,1)S(1)} collective-permute-done((bf16[4,512,128]{2,1,0:T(8,128)(2,1)S(1)}, bf16[4,512,128]{2,1,0:T(8,128)(2,1)S(1)}, u32[]{:S(2)}, u32[]{:S(2)}) %collective-permute-start.12) | collective-permute-done | bytes 524320 | tf_op jit(solution)/shard_map/v1/ppermute | solution.py:93
  59.3 2.8 %collective-permute-done.13.refs_1_ = bf16[4,512,128]{2,1,0:T(8,128)(2,1)S(1)} collective-permute-done((bf16[4,512,128]{2,1,0:T(8,128)(2,1)S(1)}, bf16[4,512,128]{2,1,0:T(8,128)(2,1)S(1)}, u32[]{:S(2)}, u32[]{:S(2)}) %collective-permute-start.13) | collective-permute-done | bytes 524320 | tf_op jit(solution)/shard_map/s4/ppermute | solution.py:93
  62.1 3.2 %collective-permute-done.14.refs_2_ = bf16[4,512,128]{2,1,0:T(8,128)(2,1)S(1)} collective-permute-done((bf16[4,512,128]{2,1,0:T(8,128)(2,1)S(1)}, bf16[4,512,128]{2,1,0:T(8,128)(2,1)S(1)}, u32[]{:S(2)}, u32[]{:S(2)}) %collective-permute-start.14) | collective-permute-done | bytes 524320 | tf_op jit(solution)/shard_map/u3/ppermute | solution.py:93
  70.9 5.7 %collective-permute-done.16.refs_1_ = bf16[4,512,128]{2,1,0:T(8,128)(2,1)S(1)} collective-permute-done((bf16[4,512,128]{2,1,0:T(8,128)(2,1)S(1)}, bf16[4,512,128]{2,1,0:T(8,128)(2,1)S(1)}, u32[]{:S(2)}, u32[]{:S(2)}) %collective-permute-start.16) | collective-permute-done | bytes 524320 | tf_op jit(solution)/shard_map/q3/ppermute | solution.py:93
  76.9 2.0 %collective-permute-done.17.refs_2_ = bf16[4,512,128]{2,1,0:T(8,128)(2,1)S(1)} collective-permute-done((bf16[4,512,128]{2,1,0:T(8,128)(2,1)S(1)}, bf16[4,512,128]{2,1,0:T(8,128)(2,1)S(1)}, u32[]{:S(2)}, u32[]{:S(2)}) %collective-permute-start.17) | collective-permute-done | bytes 524320 | tf_op jit(solution)/shard_map/v2/ppermute | solution.py:93
  79.7 2.5 %collective-permute-done.18.refs_1_ = bf16[4,512,128]{2,1,0:T(8,128)(2,1)S(1)} collective-permute-done((bf16[4,512,128]{2,1,0:T(8,128)(2,1)S(1)}, bf16[4,512,128]{2,1,0:T(8,128)(2,1)S(1)}, u32[]{:S(2)}, u32[]{:S(2)}) %collective-permute-start.18) | collective-permute-done | bytes 524320 | tf_op jit(solution)/shard_map/s5/ppermute | solution.py:93
  82.5 2.1 %spread.8.refs_4_ = bf16[16384,512]{1,0:T(8,128)(2,1)S(1)} custom-call(s32[4]{0:T(128)S(1)} %copy-done, bf16[6160,128]{1,0:T(8,128)(2,1)S(1)} %get-tuple-element.77.second.refs_0_, bf16[16384,512]{1,0:T(8,128)(2,1)S(1)} %get-tuple-element.78.refs_1_), custom_call_target="tpu_custom_call", output_to_operand_aliasing={{}: (2, {})} | custom-call | bytes 6291456 | tf_op jit(solution)/shard_map/spread/pallas_call | solution.py:138
  84.6 2.3 %collective-permute-done.19.refs_2_ = bf16[4,512,128]{2,1,0:T(8,128)(2,1)S(1)} collective-permute-done((bf16[4,512,128]{2,1,0:T(8,128)(2,1)S(1)}, bf16[4,512,128]{2,1,0:T(8,128)(2,1)S(1)}, u32[]{:S(2)}, u32[]{:S(2)}) %collective-permute-start.19) | collective-permute-done | bytes 524320 | tf_op jit(solution)/shard_map/u4/ppermute | solution.py:93
  87.0 2.2 %collective-permute-start.24 = (bf16[4,512,128]{2,1,0:T(8,128)(2,1)S(1)}, bf16[4,512,128]{2,1,0:T(8,128)(2,1)S(1)}, u32[]{:S(2)}, u32[]{:S(2)}) collective-permute-start(bf16[4,512,128]{2,1,0:T(8,128)(2,1)S(1)} %get-tuple-element.82.refs_10_), channel_id=1, source_target_pairs={{0,24},{1,25},{2,26},{3,27},{4,28},{5,29},{6,30},{7,31},{8,16},{9,... | collective-permute-start | bytes 1572872 | tf_op jit(solution)/shard_map/u5/ppermute | solution.py:93
  89.2 3.4 %collective-permute-done.22.refs_2_ = bf16[4,512,128]{2,1,0:T(8,128)(2,1)S(1)} collective-permute-done((bf16[4,512,128]{2,1,0:T(8,128)(2,1)S(1)}, bf16[4,512,128]{2,1,0:T(8,128)(2,1)S(1)}, u32[]{:S(2)}, u32[]{:S(2)}) %collective-permute-start.22) | collective-permute-done | bytes 524320 | tf_op jit(solution)/shard_map/v3/ppermute | solution.py:93
  92.6 2.2 %collective-permute-start.26 = (bf16[4,512,128]{2,1,0:T(8,128)(2,1)S(1)}, bf16[4,512,128]{2,1,0:T(8,128)(2,1)S(1)}, u32[]{:S(2)}, u32[]{:S(2)}) collective-permute-start(bf16[4,512,128]{2,1,0:T(8,128)(2,1)S(1)} %get-tuple-element.86.refs_7_), channel_id=1, source_target_pairs={{0,24},{1,25},{2,26},{3,27},{4,28},{5,29},{6,30},{7,31},{8,16},{9,... | collective-permute-start | bytes 1572872 | tf_op jit(solution)/shard_map/v4/ppermute | solution.py:93
  94.8 3.8 %spread.9.refs_3_ = bf16[16384,512]{1,0:T(8,128)(2,1)S(1)} custom-call(s32[4]{0:T(128)S(1)} %copy-done, bf16[12320,128]{1,0:T(8,128)(2,1)S(1)} %get-tuple-element.83.refs_0_, bf16[16384,512]{1,0:T(8,128)(2,1)S(1)} %get-tuple-element.84.refs_1_), custom_call_target="tpu_custom_call", output_to_operand_aliasing={{}: (2, {})} | custom-call | bytes 6291456 | tf_op jit(solution)/shard_map/spread/pallas_call | solution.py:138
  100.8 2.1 %collective-permute-done.25.refs_1_ = bf16[4,512,128]{2,1,0:T(8,128)(2,1)S(1)} collective-permute-done((bf16[4,512,128]{2,1,0:T(8,128)(2,1)S(1)}, bf16[4,512,128]{2,1,0:T(8,128)(2,1)S(1)}, u32[]{:S(2)}, u32[]{:S(2)}) %collective-permute-start.25) | collective-permute-done | bytes 524320 | tf_op jit(solution)/shard_map/q5/ppermute | solution.py:93
  103.8 5.3 %collective-permute-done.27.refs_1_ = bf16[4,512,128]{2,1,0:T(8,128)(2,1)S(1)} collective-permute-done((bf16[4,512,128]{2,1,0:T(8,128)(2,1)S(1)}, bf16[4,512,128]{2,1,0:T(8,128)(2,1)S(1)}, u32[]{:S(2)}, u32[]{:S(2)}) %collective-permute-start.27) | collective-permute-done | bytes 524320 | tf_op jit(solution)/shard_map/s7/ppermute | solution.py:93
  112.2 2.2 %collective-permute-start.33 = (bf16[4,512,128]{2,1,0:T(8,128)(2,1)S(1)}, bf16[4,512,128]{2,1,0:T(8,128)(2,1)S(1)}, u32[]{:S(2)}, u32[]{:S(2)}) collective-permute-start(bf16[4,512,128]{2,1,0:T(8,128)(2,1)S(1)} %get-tuple-element.64.refs_2_), channel_id=1, source_target_pairs={{0,7},{1,0},{2,1},{3,2},{4,3},{5,4},{6,5},{7,6},{8,15},{9,8},{10,9... | collective-permute-start | bytes 1572872 | tf_op jit(solution)/shard_map/q7/ppermute | solution.py:93
  114.5 2.3 %collective-permute-start.32 = (bf16[4,512,128]{2,1,0:T(8,128)(2,1)S(1)}, bf16[4,512,128]{2,1,0:T(8,128)(2,1)S(1)}, u32[]{:S(2)}, u32[]{:S(2)}) collective-permute-start(bf16[4,512,128]{2,1,0:T(8,128)(2,1)S(1)} %get-tuple-element.94.refs_6_), channel_id=1, source_target_pairs={{0,24},{1,25},{2,26},{3,27},{4,28},{5,29},{6,30},{7,31},{8,16},{9,... | collective-permute-start | bytes 1572872 | tf_op jit(solution)/shard_map/u7/ppermute | solution.py:93
  116.7 2.1 %spread.10.refs_3_ = bf16[16384,512]{1,0:T(8,128)(2,1)S(1)} custom-call(s32[4]{0:T(128)S(1)} %copy-done, bf16[6160,128]{1,0:T(8,128)(2,1)S(1)} %get-tuple-element.91.refs_0_, bf16[16384,512]{1,0:T(8,128)(2,1)S(1)} %get-tuple-element.92.refs_1_), custom_call_target="tpu_custom_call", output_to_operand_aliasing={{}: (2, {})} | custom-call | bytes 6291456 | tf_op jit(solution)/shard_map/spread/pallas_call | solution.py:138
  118.9 6.1 %collective-permute-done.30.refs_1_ = bf16[4,512,128]{2,1,0:T(8,128)(2,1)S(1)} collective-permute-done((bf16[4,512,128]{2,1,0:T(8,128)(2,1)S(1)}, bf16[4,512,128]{2,1,0:T(8,128)(2,1)S(1)}, u32[]{:S(2)}, u32[]{:S(2)}) %collective-permute-start.30) | collective-permute-done | bytes 524320 | tf_op jit(solution)/shard_map/q6/ppermute | solution.py:93
  130.5 3.4 %terms.4.refs_1_ = f32[512,512]{1,0:T(8,128)S(1)} custom-call(bf16[16384,512]{1,0:T(8,128)(2,1)S(1)} %spread.11.refs_0_, bf16[4,512,128]{2,1,0:T(8,128)(2,1)S(1)} %bitcast.7, bf16[4,512,128]{2,1,0:T(8,128)(2,1)S(1)} %get-tuple-element.64.refs_2_, bf16[4,512,128]{2,1,0:T(8,128)(2,1)S(1)} %get-tuple-element.97.refs_3_, ...), custom_call_target="tpu_custom_call" | custom-call | flops 3221225472 | bytes 12582912 | tf_op jit(solution)/shard_map/terms/pallas_call | solution.py:166
  133.9 3.4 %terms.5.refs_1_ = f32[512,512]{1,0:T(8,128)S(1)} custom-call(bf16[16384,512]{1,0:T(8,128)(2,1)S(1)} %spread.11.refs_0_, f32[512,512]{1,0:T(8,128)S(1)} %terms.4.refs_1_, bf16[4,512,128]{2,1,0:T(8,128)(2,1)S(1)} %get-tuple-element.72.refs_2_, bf16[4,512,128]{2,1,0:T(8,128)(2,1)S(1)} %get-tuple-element.80.refs_3_, ...), custom_call_target="tpu_custom_call" | custom-call | flops 3221225472 | bytes 12582912 | tf_op jit(solution)/shard_map/terms/pallas_call | solution.py:166
  137.3 2.1 %terms.6.refs_1_ = f32[512,512]{1,0:T(8,128)S(1)} custom-call(bf16[16384,512]{1,0:T(8,128)(2,1)S(1)} %spread.11.refs_0_, f32[512,512]{1,0:T(8,128)S(1)} %terms.5.refs_1_, bf16[4,512,128]{2,1,0:T(8,128)(2,1)S(1)} %get-tuple-element.88.refs_2_, bf16[4,512,128]{2,1,0:T(8,128)(2,1)S(1)} %get-tuple-element.109.refs_3_, ...), custom_call_target="tpu_custom_call" | custom-call | flops 1879048192 | bytes 7340032 | tf_op jit(solution)/shard_map/terms/pallas_call | solution.py:166
  (77 shorter events, 36.4 us)
Async XLA Ops:
  2.3 13.8 %collective-permute-start.2 = (bf16[6160,128]{1,0:T(8,128)(2,1)S(1)}, bf16[6160,128]{1,0:T(8,128)(2,1)S(1)}, u32[]{:S(2)}, u32[]{:S(2)}) collective-permute-start(bf16[6160,128]{1,0:T(8,128)(2,1)S(1)} %fusion.1.refs_0_), channel_id=1, source_target_pairs={{0,32},{1,33},{2,34},{3,35},{4,36},{5,37},{6,38},{7,39},{8,40},{9,... | collective-permute-start | bytes 4730888 | tf_op jit(solution)/shard_map/ox0/ppermute | solution.py:93
  2.4 24.8 %collective-permute-start.6 = (bf16[6160,128]{1,0:T(8,128)(2,1)S(1)}, bf16[6160,128]{1,0:T(8,128)(2,1)S(1)}, u32[]{:S(2)}, u32[]{:S(2)}) collective-permute-start(bf16[6160,128]{1,0:T(8,128)(2,1)S(1)} %fusion.1.refs_0_), channel_id=1, source_target_pairs={{0,64},{1,65},{2,66},{3,67},{4,68},{5,69},{6,70},{7,71},{8,72},{9,... | collective-permute-start | bytes 4730888 | tf_op jit(solution)/shard_map/bx1/ppermute | solution.py:93
  4.7 11.4 %collective-permute-start = (bf16[4,512,128]{2,1,0:T(8,128)(2,1)S(1)}, bf16[4,512,128]{2,1,0:T(8,128)(2,1)S(1)}, u32[]{:S(2)}, u32[]{:S(2)}) collective-permute-start(bf16[4,512,128]{2,1,0:T(8,128)(2,1)S(1)} %bitcast.4), channel_id=1, source_target_pairs={{0,1},{1,2},{2,3},{3,4},{4,5},{5,6},{6,7},{7,0},{8,9},{9,10},{10,1... | collective-permute-start | bytes 1572872 | tf_op jit(solution)/shard_map/s1/ppermute | solution.py:93
  5.0 11.1 %collective-permute-start.1 = (bf16[4,512,128]{2,1,0:T(8,128)(2,1)S(1)}, bf16[4,512,128]{2,1,0:T(8,128)(2,1)S(1)}, u32[]{:S(2)}, u32[]{:S(2)}) collective-permute-start(bf16[4,512,128]{2,1,0:T(8,128)(2,1)S(1)} %bitcast.5), channel_id=1, source_target_pairs={{0,8},{1,9},{2,10},{3,11},{4,12},{5,13},{6,14},{7,15},{8,0},{9,1},... | collective-permute-start | bytes 1572872 | tf_op jit(solution)/shard_map/q0/ppermute | solution.py:93
  6.6 20.6 %collective-permute-start.3 = (bf16[4,512,128]{2,1,0:T(8,128)(2,1)S(1)}, bf16[4,512,128]{2,1,0:T(8,128)(2,1)S(1)}, u32[]{:S(2)}, u32[]{:S(2)}) collective-permute-start(bf16[4,512,128]{2,1,0:T(8,128)(2,1)S(1)} %bitcast.6), channel_id=1, source_target_pairs={{0,24},{1,25},{2,26},{3,27},{4,28},{5,29},{6,30},{7,31},{8,16},{9,... | collective-permute-start | bytes 1572872 | tf_op jit(solution)/shard_map/u0/ppermute | solution.py:93
  16.1 12.3 %collective-permute-start.4 = (bf16[4,512,128]{2,1,0:T(8,128)(2,1)S(1)}, bf16[4,512,128]{2,1,0:T(8,128)(2,1)S(1)}, u32[]{:S(2)}, u32[]{:S(2)}) collective-permute-start(bf16[4,512,128]{2,1,0:T(8,128)(2,1)S(1)} %get-tuple-element.61.refs_5_), channel_id=1, source_target_pairs={{0,1},{1,2},{2,3},{3,4},{4,5},{5,6},{6,7},{7,0},{8,9},{9,10},{10,1... | collective-permute-start | bytes 1572872 | tf_op jit(solution)/shard_map/s2/ppermute | solution.py:93
  21.4 10.4 %collective-permute-start.5 = (bf16[4,512,128]{2,1,0:T(8,128)(2,1)S(1)}, bf16[4,512,128]{2,1,0:T(8,128)(2,1)S(1)}, u32[]{:S(2)}, u32[]{:S(2)}) collective-permute-start(bf16[4,512,128]{2,1,0:T(8,128)(2,1)S(1)} %get-tuple-element.61.refs_5_), channel_id=1, source_target_pairs={{0,24},{1,25},{2,26},{3,27},{4,28},{5,29},{6,30},{7,31},{8,16},{9,... | collective-permute-start | bytes 1572872 | tf_op jit(solution)/shard_map/u1/ppermute | solution.py:93
  31.8 33.5 %collective-permute-start.15 = (bf16[6160,128]{1,0:T(8,128)(2,1)S(1)}, bf16[6160,128]{1,0:T(8,128)(2,1)S(1)}, u32[]{:S(2)}, u32[]{:S(2)}) collective-permute-start(bf16[6160,128]{1,0:T(8,128)(2,1)S(1)} %get-tuple-element.67.refs_0_.first), channel_id=1, source_target_pairs={{0,64},{1,65},{2,66},{3,67},{4,68},{5,69},{6,70},{7,71},{8,72},{9,... | collective-permute-start | bytes 4730888 | tf_op jit(solution)/shard_map/bx2/ppermute | solution.py:93
  32.6 10.4 %collective-permute-start.7 = (bf16[4,512,128]{2,1,0:T(8,128)(2,1)S(1)}, bf16[4,512,128]{2,1,0:T(8,128)(2,1)S(1)}, u32[]{:S(2)}, u32[]{:S(2)}) collective-permute-start(bf16[4,512,128]{2,1,0:T(8,128)(2,1)S(1)} %get-tuple-element.64.refs_2_), channel_id=1, source_target_pairs={{0,1},{1,2},{2,3},{3,4},{4,5},{5,6},{6,7},{7,0},{8,9},{9,10},{10,1... | collective-permute-start | bytes 1572872 | tf_op jit(solution)/shard_map/q1/ppermute | solution.py:93
  34.6 10.4 %collective-permute-start.8 = (bf16[4,512,128]{2,1,0:T(8,128)(2,1)S(1)}, bf16[4,512,128]{2,1,0:T(8,128)(2,1)S(1)}, u32[]{:S(2)}, u32[]{:S(2)}) collective-permute-start(bf16[4,512,128]{2,1,0:T(8,128)(2,1)S(1)} %get-tuple-element.64.refs_2_), channel_id=1, source_target_pairs={{0,24},{1,25},{2,26},{3,27},{4,28},{5,29},{6,30},{7,31},{8,16},{9,... | collective-permute-start | bytes 1572872 | tf_op jit(solution)/shard_map/v0/ppermute | solution.py:93
  37.3 14.3 %collective-permute-start.10 = (bf16[4,512,128]{2,1,0:T(8,128)(2,1)S(1)}, bf16[4,512,128]{2,1,0:T(8,128)(2,1)S(1)}, u32[]{:S(2)}, u32[]{:S(2)}) collective-permute-start(bf16[4,512,128]{2,1,0:T(8,128)(2,1)S(1)} %get-tuple-element.66.refs_9_), channel_id=1, source_target_pairs={{0,24},{1,25},{2,26},{3,27},{4,28},{5,29},{6,30},{7,31},{8,16},{9,... | collective-permute-start | bytes 1572872 | tf_op jit(solution)/shard_map/u2/ppermute | solution.py:93
  37.8 13.8 %collective-permute-start.9 = (bf16[4,512,128]{2,1,0:T(8,128)(2,1)S(1)}, bf16[4,512,128]{2,1,0:T(8,128)(2,1)S(1)}, u32[]{:S(2)}, u32[]{:S(2)}) collective-permute-start(bf16[4,512,128]{2,1,0:T(8,128)(2,1)S(1)} %get-tuple-element.66.refs_9_), channel_id=1, source_target_pairs={{0,1},{1,2},{2,3},{3,4},{4,5},{5,6},{6,7},{7,0},{8,9},{9,10},{10,1... | collective-permute-start | bytes 1572872 | tf_op jit(solution)/shard_map/s3/ppermute | solution.py:93
  45.0 10.7 %collective-permute-start.11 = (bf16[4,512,128]{2,1,0:T(8,128)(2,1)S(1)}, bf16[4,512,128]{2,1,0:T(8,128)(2,1)S(1)}, u32[]{:S(2)}, u32[]{:S(2)}) collective-permute-start(bf16[4,512,128]{2,1,0:T(8,128)(2,1)S(1)} %get-tuple-element.70.refs_6_), channel_id=1, source_target_pairs={{0,1},{1,2},{2,3},{3,4},{4,5},{5,6},{6,7},{7,0},{8,9},{9,10},{10,1... | collective-permute-start | bytes 1572872 | tf_op jit(solution)/shard_map/q2/ppermute | solution.py:93
  48.9 10.4 %collective-permute-start.12 = (bf16[4,512,128]{2,1,0:T(8,128)(2,1)S(1)}, bf16[4,512,128]{2,1,0:T(8,128)(2,1)S(1)}, u32[]{:S(2)}, u32[]{:S(2)}) collective-permute-start(bf16[4,512,128]{2,1,0:T(8,128)(2,1)S(1)} %get-tuple-element.70.refs_6_), channel_id=1, source_target_pairs={{0,24},{1,25},{2,26},{3,27},{4,28},{5,29},{6,30},{7,31},{8,16},{9,... | collective-permute-start | bytes 1572872 | tf_op jit(solution)/shard_map/v1/ppermute | solution.py:93
  51.6 10.5 %collective-permute-start.13 = (bf16[4,512,128]{2,1,0:T(8,128)(2,1)S(1)}, bf16[4,512,128]{2,1,0:T(8,128)(2,1)S(1)}, u32[]{:S(2)}, u32[]{:S(2)}) collective-permute-start(bf16[4,512,128]{2,1,0:T(8,128)(2,1)S(1)} %get-tuple-element.72.refs_2_), channel_id=1, source_target_pairs={{0,1},{1,2},{2,3},{3,4},{4,5},{5,6},{6,7},{7,0},{8,9},{9,10},{10,1... | collective-permute-start | bytes 1572872 | tf_op jit(solution)/shard_map/s4/ppermute | solution.py:93
  54.9 10.4 %collective-permute-start.14 = (bf16[4,512,128]{2,1,0:T(8,128)(2,1)S(1)}, bf16[4,512,128]{2,1,0:T(8,128)(2,1)S(1)}, u32[]{:S(2)}, u32[]{:S(2)}) collective-permute-start(bf16[4,512,128]{2,1,0:T(8,128)(2,1)S(1)} %get-tuple-element.72.refs_2_), channel_id=1, source_target_pairs={{0,24},{1,25},{2,26},{3,27},{4,28},{5,29},{6,30},{7,31},{8,16},{9,... | collective-permute-start | bytes 1572872 | tf_op jit(solution)/shard_map/u3/ppermute | solution.py:93
  65.8 21.1 %collective-permute-start.20 = (bf16[12320,128]{1,0:T(8,128)(2,1)S(1)}, bf16[12320,128]{1,0:T(8,128)(2,1)S(1)}, u32[]{:S(2)}, u32[]{:S(2)}) collective-permute-start(bf16[12320,128]{1,0:T(8,128)(2,1)S(1)} %pack.1), channel_id=1, source_target_pairs={{0,32},{1,33},{2,34},{3,35},{4,36},{5,37},{6,38},{7,39},{8,40},{9,... | collective-permute-start | bytes 9461768 | tf_op jit(solution)/shard_map/ox12/ppermute | solution.py:93
  65.9 10.7 %collective-permute-start.16 = (bf16[4,512,128]{2,1,0:T(8,128)(2,1)S(1)}, bf16[4,512,128]{2,1,0:T(8,128)(2,1)S(1)}, u32[]{:S(2)}, u32[]{:S(2)}) collective-permute-start(bf16[4,512,128]{2,1,0:T(8,128)(2,1)S(1)} %get-tuple-element.74.refs_10_), channel_id=1, source_target_pairs={{0,1},{1,2},{2,3},{3,4},{4,5},{5,6},{6,7},{7,0},{8,9},{9,10},{10,1... | collective-permute-start | bytes 1572872 | tf_op jit(solution)/shard_map/q3/ppermute | solution.py:93
  67.3 36.5 %collective-permute-start.29 = (bf16[6160,128]{1,0:T(8,128)(2,1)S(1)}, bf16[6160,128]{1,0:T(8,128)(2,1)S(1)}, u32[]{:S(2)}, u32[]{:S(2)}) collective-permute-start(bf16[6160,128]{1,0:T(8,128)(2,1)S(1)} %get-tuple-element.77.second.refs_0_), channel_id=1, source_target_pairs={{0,64},{1,65},{2,66},{3,67},{4,68},{5,69},{6,70},{7,71},{8,72},{9,... | collective-permute-start | bytes 4730888 | tf_op jit(solution)/shard_map/bx3/ppermute | solution.py:93
  69.6 12.6 %collective-permute-start.18 = (bf16[4,512,128]{2,1,0:T(8,128)(2,1)S(1)}, bf16[4,512,128]{2,1,0:T(8,128)(2,1)S(1)}, u32[]{:S(2)}, u32[]{:S(2)}) collective-permute-start(bf16[4,512,128]{2,1,0:T(8,128)(2,1)S(1)} %get-tuple-element.76.refs_6_), channel_id=1, source_target_pairs={{0,1},{1,2},{2,3},{3,4},{4,5},{5,6},{6,7},{7,0},{8,9},{9,10},{10,1... | collective-permute-start | bytes 1572872 | tf_op jit(solution)/shard_map/s5/ppermute | solution.py:93
  87.0 11.6 %collective-permute-start.23 = (bf16[4,512,128]{2,1,0:T(8,128)(2,1)S(1)}, bf16[4,512,128]{2,1,0:T(8,128)(2,1)S(1)}, u32[]{:S(2)}, u32[]{:S(2)}) collective-permute-start(bf16[4,512,128]{2,1,0:T(8,128)(2,1)S(1)} %get-tuple-element.82.refs_10_), channel_id=1, source_target_pairs={{0,1},{1,2},{2,3},{3,4},{4,5},{5,6},{6,7},{7,0},{8,9},{9,10},{10,1... | collective-permute-start | bytes 1572872 | tf_op jit(solution)/shard_map/s6/ppermute | solution.py:93
  87.0 11.6 %collective-permute-start.24 = (bf16[4,512,128]{2,1,0:T(8,128)(2,1)S(1)}, bf16[4,512,128]{2,1,0:T(8,128)(2,1)S(1)}, u32[]{:S(2)}, u32[]{:S(2)}) collective-permute-start(bf16[4,512,128]{2,1,0:T(8,128)(2,1)S(1)} %get-tuple-element.82.refs_10_), channel_id=1, source_target_pairs={{0,24},{1,25},{2,26},{3,27},{4,28},{5,29},{6,30},{7,31},{8,16},{9,... | collective-permute-start | bytes 1572872 | tf_op jit(solution)/shard_map/u5/ppermute | solution.py:93
  92.6 10.4 %collective-permute-start.25 = (bf16[4,512,128]{2,1,0:T(8,128)(2,1)S(1)}, bf16[4,512,128]{2,1,0:T(8,128)(2,1)S(1)}, u32[]{:S(2)}, u32[]{:S(2)}) collective-permute-start(bf16[4,512,128]{2,1,0:T(8,128)(2,1)S(1)} %get-tuple-element.86.refs_7_), channel_id=1, source_target_pairs={{0,1},{1,2},{2,3},{3,4},{4,5},{5,6},{6,7},{7,0},{8,9},{9,10},{10,1... | collective-permute-start | bytes 1572872 | tf_op jit(solution)/shard_map/q5/ppermute | solution.py:93
  92.6 11.2 %collective-permute-start.26 = (bf16[4,512,128]{2,1,0:T(8,128)(2,1)S(1)}, bf16[4,512,128]{2,1,0:T(8,128)(2,1)S(1)}, u32[]{:S(2)}, u32[]{:S(2)}) collective-permute-start(bf16[4,512,128]{2,1,0:T(8,128)(2,1)S(1)} %get-tuple-element.86.refs_7_), channel_id=1, source_target_pairs={{0,24},{1,25},{2,26},{3,27},{4,28},{5,29},{6,30},{7,31},{8,16},{9,... | collective-permute-start | bytes 1572872 | tf_op jit(solution)/shard_map/v4/ppermute | solution.py:93
  98.6 10.5 %collective-permute-start.27 = (bf16[4,512,128]{2,1,0:T(8,128)(2,1)S(1)}, bf16[4,512,128]{2,1,0:T(8,128)(2,1)S(1)}, u32[]{:S(2)}, u32[]{:S(2)}) collective-permute-start(bf16[4,512,128]{2,1,0:T(8,128)(2,1)S(1)} %get-tuple-element.88.refs_2_), channel_id=1, source_target_pairs={{0,1},{1,2},{2,3},{3,4},{4,5},{5,6},{6,7},{7,0},{8,9},{9,10},{10,1... | collective-permute-start | bytes 1572872 | tf_op jit(solution)/shard_map/s7/ppermute | solution.py:93
  110.3 17.0 %collective-permute-start.34 = (bf16[6160,128]{1,0:T(8,128)(2,1)S(1)}, bf16[6160,128]{1,0:T(8,128)(2,1)S(1)}, u32[]{:S(2)}, u32[]{:S(2)}) collective-permute-start(bf16[6160,128]{1,0:T(8,128)(2,1)S(1)} %get-tuple-element.91.refs_0_), channel_id=1, source_target_pairs={{0,32},{1,33},{2,34},{3,35},{4,36},{5,37},{6,38},{7,39},{8,40},{9,... | collective-permute-start | bytes 4730888 | tf_op jit(solution)/shard_map/ox3/ppermute | solution.py:93
  110.3 14.7 %collective-permute-start.30 = (bf16[4,512,128]{2,1,0:T(8,128)(2,1)S(1)}, bf16[4,512,128]{2,1,0:T(8,128)(2,1)S(1)}, u32[]{:S(2)}, u32[]{:S(2)}) collective-permute-start(bf16[4,512,128]{2,1,0:T(8,128)(2,1)S(1)} %get-tuple-element.90.refs_11_), channel_id=1, source_target_pairs={{0,1},{1,2},{2,3},{3,4},{4,5},{5,6},{6,7},{7,0},{8,9},{9,10},{10,1... | collective-permute-start | bytes 1572872 | tf_op jit(solution)/shard_map/q6/ppermute | solution.py:93
  111.2 13.7 %collective-permute-start.31 = (bf16[4,512,128]{2,1,0:T(8,128)(2,1)S(1)}, bf16[4,512,128]{2,1,0:T(8,128)(2,1)S(1)}, u32[]{:S(2)}, u32[]{:S(2)}) collective-permute-start(bf16[4,512,128]{2,1,0:T(8,128)(2,1)S(1)} %get-tuple-element.90.refs_11_), channel_id=1, source_target_pairs={{0,24},{1,25},{2,26},{3,27},{4,28},{5,29},{6,30},{7,31},{8,16},{9,... | collective-permute-start | bytes 1572872 | tf_op jit(solution)/shard_map/v5/ppermute | solution.py:93
  112.2 13.5 %collective-permute-start.33 = (bf16[4,512,128]{2,1,0:T(8,128)(2,1)S(1)}, bf16[4,512,128]{2,1,0:T(8,128)(2,1)S(1)}, u32[]{:S(2)}, u32[]{:S(2)}) collective-permute-start(bf16[4,512,128]{2,1,0:T(8,128)(2,1)S(1)} %get-tuple-element.64.refs_2_), channel_id=1, source_target_pairs={{0,7},{1,0},{2,1},{3,2},{4,3},{5,4},{6,5},{7,6},{8,15},{9,8},{10,9... | collective-permute-start | bytes 1572872 | tf_op jit(solution)/shard_map/q7/ppermute | solution.py:93
  114.5 12.8 %collective-permute-start.32 = (bf16[4,512,128]{2,1,0:T(8,128)(2,1)S(1)}, bf16[4,512,128]{2,1,0:T(8,128)(2,1)S(1)}, u32[]{:S(2)}, u32[]{:S(2)}) collective-permute-start(bf16[4,512,128]{2,1,0:T(8,128)(2,1)S(1)} %get-tuple-element.94.refs_6_), channel_id=1, source_target_pairs={{0,24},{1,25},{2,26},{3,27},{4,28},{5,29},{6,30},{7,31},{8,16},{9,... | collective-permute-start | bytes 1572872 | tf_op jit(solution)/shard_map/u7/ppermute | solution.py:93
  124.9 12.3 %collective-permute-start.35 = (bf16[4,512,128]{2,1,0:T(8,128)(2,1)S(1)}, bf16[4,512,128]{2,1,0:T(8,128)(2,1)S(1)}, u32[]{:S(2)}, u32[]{:S(2)}) collective-permute-start(bf16[4,512,128]{2,1,0:T(8,128)(2,1)S(1)} %get-tuple-element.109.refs_3_), channel_id=1, source_target_pairs={{0,24},{1,25},{2,26},{3,27},{4,28},{5,29},{6,30},{7,31},{8,16},{9,... | collective-permute-start | bytes 1572872 | tf_op jit(solution)/shard_map/v6/ppermute | solution.py:93
  127.2 13.7 %collective-permute-start.36 = (bf16[4,512,128]{2,1,0:T(8,128)(2,1)S(1)}, bf16[4,512,128]{2,1,0:T(8,128)(2,1)S(1)}, u32[]{:S(2)}, u32[]{:S(2)}) collective-permute-start(bf16[4,512,128]{2,1,0:T(8,128)(2,1)S(1)} %get-tuple-element.111.refs_7_), channel_id=1, source_target_pairs={{0,24},{1,25},{2,26},{3,27},{4,28},{5,29},{6,30},{7,31},{8,16},{9,... | collective-permute-start | bytes 1572872 | tf_op jit(solution)/shard_map/v7/ppermute | solution.py:93
  (7 other events, 78.4 us)

commit v2 on v0

v2 whole, which is shorter than its diff:
```python
import functools

import jax
import jax.numpy as jnp
from jax import lax
from jax.experimental import pallas as pl
from jax.experimental.pallas import tpu as pltpu
from jax.sharding import Mesh, PartitionSpec as P

AXES = ("x", "core", "y", "z")
NX, NC, NY, NZ = 4, 2, 4, 8
TILES, SLOTS, WIDTH = 4, 12, 128
BODY = TILES * SLOTS * WIDTH
VMEM = pl.BlockSpec(memory_space=pltpu.VMEM)
SMEM = pl.BlockSpec(memory_space=pltpu.SMEM)
ANY = pl.BlockSpec(memory_space=pl.ANY)


def near(v):
    return pltpu.with_memory_space_constraint(v, pltpu.VMEM)


def pass_kernel(*refs):
    pass


class Order:
    def __init__(self):
        self.token = jnp.zeros((8, WIDTH), jnp.float32)

    def meet(self, *places):
        values = [self.token] + [a[k] for a, k in places]
        held = pl.pallas_call(
            pass_kernel,
            out_shape=[jax.ShapeDtypeStruct(v.shape, v.dtype) for v in values],
            in_specs=[ANY] * len(values),
            out_specs=[ANY] * len(values),
            input_output_aliases={i: i for i in range(len(values))},
            compiler_params=pltpu.CompilerParams(vmem_limit_bytes=1 << 20),
            cost_estimate=pl.CostEstimate(flops=0, bytes_accessed=0, transcendentals=0),
            name="meet",
        )(*values)
        self.token = held[0]
        for (a, k), value in zip(places, held[1:]):
            a[k] = value


def pairs_of(move):
    pairs = []
    for x in range(NX):
        for c in range(NC):
            for y in range(NY):
                for z in range(NZ):
                    tx, tc, ty, tz = move(x, c, y, z)
                    to = ((tx % NX * NC + tc) * NY + ty) * NZ + tz % NZ
                    pairs.append((((x * NC + c) * NY + y) * NZ + z, to))
    return pairs


ALONG_X = pairs_of(lambda x, c, y, z: (x + 1 - 2 * c, c, y, z))
BACK_X = pairs_of(lambda x, c, y, z: (x - 1 + 2 * c, c, y, z))
ALONG_Z = pairs_of(lambda x, c, y, z: (x, c, y, z + 1 - 2 * c))
BACK_Z = pairs_of(lambda x, c, y, z: (x, c, y, z - 1 + 2 * c))
PARTNER = pairs_of(lambda x, c, y, z: (x, c, y ^ (1 + 2 * c), z))
CROSS = pairs_of(lambda x, c, y, z: (x, c, y ^ (3 - 2 * c), z))
OTHER_CORE = pairs_of(lambda x, c, y, z: (x, 1 - c, y, z))


def send(v, pairs, name):
    with jax.named_scope(name):
        return lax.ppermute(v, AXES, pairs)


def load_kernel(blocks, kets, out, codes, sems):
    body = pltpu.make_async_copy(blocks, out.at[pl.ds(0, BODY), :], sems.at[0])
    body.start()
    codes[...] = jnp.zeros(codes.shape, codes.dtype)
    codes[0:TILES, 0:SLOTS] = kets[...].astype(jnp.float32)
    half = codes[...].astype(jnp.bfloat16)
    pl.run_scoped(functools.partial(put_codes, half, out, sems), pltpu.VMEM((16, WIDTH), jnp.bfloat16))
    body.wait()


def put_codes(half, out, sems, narrow):
    narrow[...] = half
    tail = pltpu.make_async_copy(narrow, out.at[pl.ds(BODY, 16), :], sems.at[1])
    tail.start()
    tail.wait()


def make_load(blocks, kets):
    return pl.pallas_call(
        load_kernel,
        out_shape=pltpu.HBM((BODY + 16, WIDTH), jnp.bfloat16),
        in_specs=[VMEM, VMEM],
        out_specs=pl.BlockSpec(memory_space=pltpu.HBM),
        scratch_shapes=[pltpu.VMEM((16, WIDTH), jnp.float32), pltpu.SemaphoreType.DMA((2,))],
        compiler_params=pltpu.CompilerParams(vmem_limit_bytes=1 << 20),
        cost_estimate=pl.CostEstimate(flops=0, bytes_accessed=0, transcendentals=0),
        name="load",
    )(near(blocks.reshape(BODY, WIDTH)), kets)


def spread_kernel(tiles, counts, loads, dense, held, codes, listed, kets, sems):
    c, y, z = (lax.axis_index(a) for a in AXES[1:])
    sign = 1 - 2 * c
    rows, span = BODY + 16, SLOTS * WIDTH
    shards = loads.shape[0] // rows
    spare = dense.shape[0] // WIDTH - 1

    code_moves, block_moves = [], []
    for i in range(shards):
        code_moves.append(pltpu.make_async_copy(loads.at[pl.ds(i * rows + BODY, 16), :], codes.at[i], sems.at[i]))
        here = loads.at[pl.ds(i * rows + tiles[0] * span, len(tiles) * span), :]
        block_moves.append(pltpu.make_async_copy(here, held.at[i], sems.at[shards + i]))
    for move in code_moves + block_moves:
        move.start()

    def wipe(i, _):
        dense[pl.ds(pl.multiple_of(i * 512, 512), 512), :] = jnp.zeros((512, dense.shape[1]), dense.dtype)
        return 0

    lax.fori_loop(0, dense.shape[0] // 512, wipe, 0)
    for move in code_moves:
        move.wait()
    for i in range(shards):
        listed[i * 16:(i + 1) * 16, :] = codes[i].astype(jnp.float32).astype(jnp.int32)
    last = pltpu.make_async_copy(listed, kets, sems.at[2 * shards])
    last.start()
    last.wait()
    limits = [counts[t] for t in tiles]

    def place(i, n, j):
        k = kets[i * 16 + tiles[n], j]
        dz = (sign * (z - ((k >> 2) & 7))) & 7
        dy = y ^ (k >> 5)
        kind = jnp.where(dy == 0, 0, jnp.where(dy == 2, 3, jnp.where(dy == 1, 1 + c, 2 - c)))
        return jnp.where(i * SLOTS + j < limits[n], (dz * 4 + kind) * 4 + (k & 3), spare)

    for i in range(shards):
        block_moves[i].wait()

        def some(g, _, i=i):
            picks = [(n, g * 2 + d) for n in range(len(tiles)) for d in range(2)]
            spots = [place(i, n, j) for n, j in picks]
            blocks = [held[i, pl.ds(pl.multiple_of((n * SLOTS + j) * WIDTH, WIDTH), WIDTH), :] for n, j in picks]
            for (n, _), p, block in zip(picks, spots, blocks):
                dense[pl.ds(pl.multiple_of(p * WIDTH, WIDTH), WIDTH), n * WIDTH:(n + 1) * WIDTH] = block
            return 0

        lax.fori_loop(0, SLOTS // 2, some, 0, unroll=True)


def spread(counts, loads, tiles):
    shards = NX * NC
    return pl.pallas_call(
        functools.partial(spread_kernel, tiles),
        out_shape=pltpu.VMEM((NY * NZ * TILES * WIDTH + 512, len(tiles) * WIDTH), jnp.bfloat16),
        in_specs=[SMEM, pl.BlockSpec(memory_space=pltpu.HBM)],
        out_specs=VMEM,
        scratch_shapes=[
            pltpu.VMEM((shards, len(tiles) * SLOTS * WIDTH, WIDTH), jnp.bfloat16),
            pltpu.VMEM((shards, 16, WIDTH), jnp.bfloat16),
            pltpu.VMEM((shards * 16, WIDTH), jnp.int32),
            pltpu.SMEM((shards * 16, WIDTH), jnp.int32),
            pltpu.SemaphoreType.DMA((2 * shards + 1,)),
        ],
        compiler_params=pltpu.CompilerParams(vmem_limit_bytes=10 << 20),
        cost_estimate=pl.CostEstimate(flops=0, bytes_accessed=0, transcendentals=0),
        name="spread",
    )(counts, pltpu.with_memory_space_constraint(loads, pltpu.HBM))


def terms_kernel(places, fresh, *refs):
    dense, out = refs[:2], refs[-1]
    pieces = refs[2 if fresh else 3:-1]
    acc = None if fresh else refs[2][...]
    for piece, q in zip(pieces, places):
        left = jnp.concatenate([piece[t] for t in range(TILES)], axis=1)
        right = jnp.concatenate([d[q * 512:(q + 1) * 512, :] for d in dense], axis=1)
        part = jnp.dot(left, right, preferred_element_type=jnp.float32)
        acc = part if acc is None else acc + part
    out[...] = acc.astype(out.dtype)


def add_terms(dense, total, pieces, dtype=jnp.float32):
    rows = pieces[0][0].shape[1]
    fresh = total is None
    args = (dense[0], dense[1]) + (() if fresh else (total,)) + tuple(v for v, _ in pieces)
    return pl.pallas_call(
        functools.partial(terms_kernel, [q for _, q in pieces], fresh),
        out_shape=pltpu.VMEM((rows, TILES * WIDTH), dtype),
        in_specs=[VMEM] * len(args),
        out_specs=VMEM,
        compiler_params=pltpu.CompilerParams(vmem_limit_bytes=8 << 20),
        cost_estimate=pl.CostEstimate(flops=0, bytes_accessed=0, transcendentals=0),
        name="terms",
    )(*(near(v) for v in args))


def on_device(amplitudes, blocks, kets, counts):
    own = jnp.transpose(amplitudes, (1, 0, 2))
    load = make_load(blocks, kets)

    s, q, u, v = {0: own}, {}, {}, {}
    with jax.named_scope("loads"):
        everything = lax.all_gather(load, ("x", "core"), axis=0, tiled=True)
    order = Order()

    def along(a, k, name):
        a[k] = send(a[k - 1], ALONG_Z, name + str(k))

    def cross(a, b, k, name):
        b[k] = send(a[k], CROSS, name + str(k))

    def turn(k, more_s=(), more_u=(), more_q=(), more_v=()):
        order.meet((s, k), *more_s)
        if k + 1 < NZ:
            along(s, k + 1, "s")
        order.meet((u, k - 1), *more_u)
        cross(s, u, k, "u")
        order.meet((q, k - 1), *more_q)
        if k < NZ - 1:
            along(q, k, "q")
        order.meet((v, k - 2), *more_v)
        cross(q, v, k - 1, "v")

    along(s, 1, "s")
    q[0] = send(own, PARTNER, "q0")
    cross(s, u, 0, "u")
    s[7] = send(own, BACK_Z, "s7")
    order.meet((s, 1))
    along(s, 2, "s")
    cross(s, u, 1, "u")
    order.meet((q, 0))
    along(q, 1, "q")
    cross(q, v, 0, "v")
    order.meet((u, 0))
    order.meet((s, 7))
    for k in range(2, 6):
        turn(k)
    dense = {0: spread(counts, everything, (0, 1))}
    order.meet((s, 6), (dense, 0), (v, 0))
    cross(s, u, 6, "u")
    v[7] = send(v[0], BACK_Z, "v7")
    dense[1] = spread(counts, everything, (2, 3))
    order.meet((u, 5), (q, 5), (dense, 1))
    along(q, 6, "q")
    cross(q, v, 5, "v")

    def terms(ks, names):
        return [(a[k], k * 4 + i) for k in ks for i, a in enumerate((s, q, u, v)) if "squv"[i] in names]

    total = {0: add_terms(dense, None, terms(range(0, 3), "squv"))}
    order.meet((v, 4), (u, 6), (total, 0), (s, 7), (q, 0))
    cross(s, u, 7, "u")
    q[7] = send(q[0], BACK_Z, "q7")
    total[1] = add_terms(dense, total[0], terms((3,), "squv") + terms((4,), "squv") + terms((5,), "squ"))
    order.meet((q, 6), (v, 5), (total, 1))
    cross(q, v, 6, "v")
    total = add_terms(dense, total[1], terms((5,), "v") + terms((6,), "squ") + terms((7,), "suv"))
    out = add_terms(dense, total, terms((7,), "q") + terms((6,), "v"), jnp.bfloat16)
    return out.reshape(out.shape[0], TILES, WIDTH)


def solution(mesh):
    grid = Mesh(mesh.devices.reshape(NX, NC, NY, NZ), AXES)
    placed = (
        P(("x", "core"), ("y", "z"), None),
        P(("y", "z"), ("x", "core"), None, None),
        P(("y", "z"), ("x", "core")),
        P(("y", "z")),
    )
    return jax.shard_map(
        on_device, mesh=grid, in_specs=placed, out_specs=P(("x", "core"), ("y", "z"), None), check_vma=False
    )
```

time: 265 us -> 130 us (0.49)
  waiting for transfers between devices: 143 us -> 20.5 us
  starting transfers between devices: 0.04 us -> 68.3 us
  local copies, waits for them, and re-layouts: 57.5 us -> 5.22 us
  matrix products: 32.5 us -> 0 us
  Pallas kernels: 0 us -> 21 us
  blocking collectives: 12.1 us -> 0 us
  other arithmetic: 2.75 us -> 0 us
    all_gather x2 -> x1, waiting for transfers between devices: 143 us -> 0.01 us  [on_device(): everything = lax.all_gather(load, ('x', 'core'), axis=0, tiled=True)]
    ppermute x0 -> x31, starting transfers between devices: none -> 68.3 us  [send(): return lax.ppermute(v, AXES, pairs)]
    gather x4 -> x0, local copies, waits for them, and re-layouts: 52.9 us -> none  [tile_terms(): chosen = jnp.take(whole, ket_row, axis=1)]
    dot_general x4 -> x0, matrix products: 32.5 us -> none  [tile_terms(): jnp.dot(chosen.reshape(rows, slots * width), masked.reshape(slots * width...]
    pallas_call x0 -> x31, Pallas kernels: none -> 21 us  [the longest x4 10.7 us: add_terms(): pl.pallas_call(functools.partial(terms_kernel, [q for _, q in pieces], fr...]
    ppermute x0 -> x31, waiting for transfers between devices: none -> 20.4 us  [send(): return lax.ppermute(v, AXES, pairs)]
    all_gather x1 -> x0, blocking collectives: 12.1 us -> none  [on_device(): lax.all_gather(kets, 'occ', axis=1, tiled=True)]
  transfers between devices with their start and end apart: 2 -> 32, of which waited for: 2 -> 7; matrix products, arithmetic and copies ran while one was open for 22% -> 1% of each run, Pallas kernels for 0% -> 15%
where the time goes in v2:
time: 130 us; the launch traced here: 129 us
  starting transfers between devices  68.3 us (53%)
  Pallas kernels  21 us (16%)
  waiting for transfers between devices  20.5 us (16%)
  between operations  14 us (11%)
  local copies, waits for them, and re-layouts  5.22 us (4%)
    ppermute x31, starting transfers between devices, send(): return lax.ppermute(v, AXES, pairs)  68.3 us
    ppermute x31, waiting for transfers between devices, send(): return lax.ppermute(v, AXES, pairs)  20.4 us
    pallas_call x4, Pallas kernels, add_terms(): pl.pallas_call(functools.partial(terms_kernel, [q for _, q in pieces], fr...  10.7 us
    pallas_call x2, Pallas kernels, spread(): pl.pallas_call(functools.partial(spread_kernel, tiles), out_shape=pltpu.V...  9.14 us
    unnamed x71, local copies, waits for them, and re-layouts  4.3 us
  transfers between devices with their start and end apart: 32, of which 7 were waited for; matrix products, arithmetic and copies ran while one was open for 1% of the time, Pallas kernels for 15%

profile of v2, /device:TPU:96, one launch (start us, length us, event | category | flops | bytes accessed | tf_op | source)
XLA Modules:
  0.0 128.9 jit_solution(7642803164881538277)
XLA Ops:
  6.5 1.4 %copy-done.32 = bf16[4,12,128,128]{3,2,1,0:T(8,128)(2,1)S(1)} copy-done((bf16[4,12,128,128]{3,2,1,0:T(8,128)(2,1)S(1)}, bf16[4,12,128,128]{3,2,1,0:T(8,128)(2,1)}, u32[]{:S(2)}) %copy-start.32) | copy-done | bytes 1572888
  11.0 3.2 %collective-permute-start = (bf16[4,512,128]{2,1,0:T(8,128)(2,1)S(1)}, bf16[4,512,128]{2,1,0:T(8,128)(2,1)S(1)}, u32[]{:S(2)}, u32[]{:S(2)}) collective-permute-start(bf16[4,512,128]{2,1,0:T(8,128)(2,1)S(1)} %bitcast.4), channel_id=1, source_target_pairs={{0,1},{1,2},{2,3},{3,4},{4,5},{5,6},{6,7},{7,0},{8,9},{9,10},{10,1... | collective-permute-start | bytes 1572872 | tf_op jit(solution)/shard_map/s1/ppermute | solution.py:71
  14.2 1.6 %collective-permute-start.1 = (bf16[4,512,128]{2,1,0:T(8,128)(2,1)S(1)}, bf16[4,512,128]{2,1,0:T(8,128)(2,1)S(1)}, u32[]{:S(2)}, u32[]{:S(2)}) collective-permute-start(bf16[4,512,128]{2,1,0:T(8,128)(2,1)S(1)} %bitcast.5), channel_id=1, source_target_pairs={{0,8},{1,9},{2,10},{3,11},{4,12},{5,13},{6,14},{7,15},{8,0},{9,1},... | collective-permute-start | bytes 1572872 | tf_op jit(solution)/shard_map/q0/ppermute | solution.py:71
  15.7 2.2 %collective-permute-start.2 = (bf16[4,512,128]{2,1,0:T(8,128)(2,1)S(1)}, bf16[4,512,128]{2,1,0:T(8,128)(2,1)S(1)}, u32[]{:S(2)}, u32[]{:S(2)}) collective-permute-start(bf16[4,512,128]{2,1,0:T(8,128)(2,1)S(1)} %bitcast.6), channel_id=1, source_target_pairs={{0,24},{1,25},{2,26},{3,27},{4,28},{5,29},{6,30},{7,31},{8,16},{9,... | collective-permute-start | bytes 1572872 | tf_op jit(solution)/shard_map/u0/ppermute | solution.py:71
  17.9 6.8 %collective-permute-done.refs_1_ = bf16[4,512,128]{2,1,0:T(8,128)(2,1)S(1)} collective-permute-done((bf16[4,512,128]{2,1,0:T(8,128)(2,1)S(1)}, bf16[4,512,128]{2,1,0:T(8,128)(2,1)S(1)}, u32[]{:S(2)}, u32[]{:S(2)}) %collective-permute-start) | collective-permute-done | bytes 524320 | tf_op jit(solution)/shard_map/s1/ppermute | solution.py:71
  24.7 3.7 %collective-permute-start.4 = (bf16[4,512,128]{2,1,0:T(8,128)(2,1)S(1)}, bf16[4,512,128]{2,1,0:T(8,128)(2,1)S(1)}, u32[]{:S(2)}, u32[]{:S(2)}) collective-permute-start(bf16[4,512,128]{2,1,0:T(8,128)(2,1)S(1)} %get-tuple-element.66.refs_6_), channel_id=1, source_target_pairs={{0,1},{1,2},{2,3},{3,4},{4,5},{5,6},{6,7},{7,0},{8,9},{9,10},{10,1... | collective-permute-start | bytes 1572872 | tf_op jit(solution)/shard_map/s2/ppermute | solution.py:71
  28.4 4.4 %collective-permute-start.5 = (bf16[4,512,128]{2,1,0:T(8,128)(2,1)S(1)}, bf16[4,512,128]{2,1,0:T(8,128)(2,1)S(1)}, u32[]{:S(2)}, u32[]{:S(2)}) collective-permute-start(bf16[4,512,128]{2,1,0:T(8,128)(2,1)S(1)} %get-tuple-element.66.refs_6_), channel_id=1, source_target_pairs={{0,24},{1,25},{2,26},{3,27},{4,28},{5,29},{6,30},{7,31},{8,16},{9,... | collective-permute-start | bytes 1572872 | tf_op jit(solution)/shard_map/u1/ppermute | solution.py:71
  33.0 2.1 %collective-permute-done.4.refs_1_ = bf16[4,512,128]{2,1,0:T(8,128)(2,1)S(1)} collective-permute-done((bf16[4,512,128]{2,1,0:T(8,128)(2,1)S(1)}, bf16[4,512,128]{2,1,0:T(8,128)(2,1)S(1)}, u32[]{:S(2)}, u32[]{:S(2)}) %collective-permute-start.4) | collective-permute-done | bytes 524320 | tf_op jit(solution)/shard_map/s2/ppermute | solution.py:71
  35.1 3.7 %collective-permute-start.8 = (bf16[4,512,128]{2,1,0:T(8,128)(2,1)S(1)}, bf16[4,512,128]{2,1,0:T(8,128)(2,1)S(1)}, u32[]{:S(2)}, u32[]{:S(2)}) collective-permute-start(bf16[4,512,128]{2,1,0:T(8,128)(2,1)S(1)} %get-tuple-element.72.refs_10_), channel_id=1, source_target_pairs={{0,1},{1,2},{2,3},{3,4},{4,5},{5,6},{6,7},{7,0},{8,9},{9,10},{10,1... | collective-permute-start | bytes 1572872 | tf_op jit(solution)/shard_map/s3/ppermute | solution.py:71
  38.8 4.4 %collective-permute-start.9 = (bf16[4,512,128]{2,1,0:T(8,128)(2,1)S(1)}, bf16[4,512,128]{2,1,0:T(8,128)(2,1)S(1)}, u32[]{:S(2)}, u32[]{:S(2)}) collective-permute-start(bf16[4,512,128]{2,1,0:T(8,128)(2,1)S(1)} %get-tuple-element.72.refs_10_), channel_id=1, source_target_pairs={{0,24},{1,25},{2,26},{3,27},{4,28},{5,29},{6,30},{7,31},{8,16},{9,... | collective-permute-start | bytes 1572872 | tf_op jit(solution)/shard_map/u2/ppermute | solution.py:71
  43.2 1.2 collective-permute-start.10
  44.4 4.4 %collective-permute-start.11 = (bf16[4,512,128]{2,1,0:T(8,128)(2,1)S(1)}, bf16[4,512,128]{2,1,0:T(8,128)(2,1)S(1)}, u32[]{:S(2)}, u32[]{:S(2)}) collective-permute-start(bf16[4,512,128]{2,1,0:T(8,128)(2,1)S(1)} %get-tuple-element.75.refs_7_), channel_id=1, source_target_pairs={{0,24},{1,25},{2,26},{3,27},{4,28},{5,29},{6,30},{7,31},{8,16},{9,... | collective-permute-start | bytes 1572872 | tf_op jit(solution)/shard_map/v1/ppermute | solution.py:71
  48.8 1.2 collective-permute-start.12
  50.0 4.4 %collective-permute-start.13 = (bf16[4,512,128]{2,1,0:T(8,128)(2,1)S(1)}, bf16[4,512,128]{2,1,0:T(8,128)(2,1)S(1)}, u32[]{:S(2)}, u32[]{:S(2)}) collective-permute-start(bf16[4,512,128]{2,1,0:T(8,128)(2,1)S(1)} %get-tuple-element.78.refs_3_), channel_id=1, source_target_pairs={{0,24},{1,25},{2,26},{3,27},{4,28},{5,29},{6,30},{7,31},{8,16},{9,... | collective-permute-start | bytes 1572872 | tf_op jit(solution)/shard_map/u3/ppermute | solution.py:71
  54.5 1.2 collective-permute-start.14
  55.7 4.4 %collective-permute-start.15 = (bf16[4,512,128]{2,1,0:T(8,128)(2,1)S(1)}, bf16[4,512,128]{2,1,0:T(8,128)(2,1)S(1)}, u32[]{:S(2)}, u32[]{:S(2)}) collective-permute-start(bf16[4,512,128]{2,1,0:T(8,128)(2,1)S(1)} %get-tuple-element.81.refs_11_), channel_id=1, source_target_pairs={{0,24},{1,25},{2,26},{3,27},{4,28},{5,29},{6,30},{7,31},{8,16},{9,... | collective-permute-start | bytes 1572872 | tf_op jit(solution)/shard_map/v2/ppermute | solution.py:71
  60.1 1.2 collective-permute-start.16
  61.3 4.4 %collective-permute-start.17 = (bf16[4,512,128]{2,1,0:T(8,128)(2,1)S(1)}, bf16[4,512,128]{2,1,0:T(8,128)(2,1)S(1)}, u32[]{:S(2)}, u32[]{:S(2)}) collective-permute-start(bf16[4,512,128]{2,1,0:T(8,128)(2,1)S(1)} %get-tuple-element.84.refs_7_), channel_id=1, source_target_pairs={{0,24},{1,25},{2,26},{3,27},{4,28},{5,29},{6,30},{7,31},{8,16},{9,... | collective-permute-start | bytes 1572872 | tf_op jit(solution)/shard_map/u4/ppermute | solution.py:71
  66.9 4.4 %collective-permute-start.19 = (bf16[4,512,128]{2,1,0:T(8,128)(2,1)S(1)}, bf16[4,512,128]{2,1,0:T(8,128)(2,1)S(1)}, u32[]{:S(2)}, u32[]{:S(2)}) collective-permute-start(bf16[4,512,128]{2,1,0:T(8,128)(2,1)S(1)} %get-tuple-element.87.refs_4_), channel_id=1, source_target_pairs={{0,24},{1,25},{2,26},{3,27},{4,28},{5,29},{6,30},{7,31},{8,16},{9,... | collective-permute-start | bytes 1572872 | tf_op jit(solution)/shard_map/v3/ppermute | solution.py:71
  71.3 1.3 %collective-permute-start.20 = (bf16[4,512,128]{2,1,0:T(8,128)(2,1)}, bf16[4,512,128]{2,1,0:T(8,128)(2,1)S(1)}, u32[]{:S(2)}, u32[]{:S(2)}) collective-permute-start(bf16[4,512,128]{2,1,0:T(8,128)(2,1)} %get-tuple-element.90.refs_11_), channel_id=1, source_target_pairs={{0,1},{1,2},{2,3},{3,4},{4,5},{5,6},{6,7},{7,0},{8,9},{9,10},{10,1... | collective-permute-start | bytes 1572872 | tf_op jit(solution)/shard_map/s6/ppermute | solution.py:71
  73.7 2.1 %collective-permute-done.18.refs_1_ = bf16[4,512,128]{2,1,0:T(8,128)(2,1)} collective-permute-done((bf16[4,512,128]{2,1,0:T(8,128)(2,1)S(1)}, bf16[4,512,128]{2,1,0:T(8,128)(2,1)}, u32[]{:S(2)}, u32[]{:S(2)}) %collective-permute-start.18) | collective-permute-done | bytes 524320 | tf_op jit(solution)/shard_map/q4/ppermute | solution.py:71
  75.8 2.4 %collective-permute-start.22 = (bf16[4,512,128]{2,1,0:T(8,128)(2,1)}, bf16[4,512,128]{2,1,0:T(8,128)(2,1)S(1)}, u32[]{:S(2)}, u32[]{:S(2)}) collective-permute-start(bf16[4,512,128]{2,1,0:T(8,128)(2,1)} %get-tuple-element.94.refs_8_), channel_id=1, source_target_pairs={{0,1},{1,2},{2,3},{3,4},{4,5},{5,6},{6,7},{7,0},{8,9},{9,10},{10,1... | collective-permute-start | bytes 1572872 | tf_op jit(solution)/shard_map/q5/ppermute | solution.py:71
  78.2 4.4 %collective-permute-start.21 = (bf16[4,512,128]{2,1,0:T(8,128)(2,1)}, bf16[4,512,128]{2,1,0:T(8,128)(2,1)S(1)}, u32[]{:S(2)}, u32[]{:S(2)}) collective-permute-start(bf16[4,512,128]{2,1,0:T(8,128)(2,1)} %get-tuple-element.90.refs_11_), channel_id=1, source_target_pairs={{0,24},{1,25},{2,26},{3,27},{4,28},{5,29},{6,30},{7,31},{8,16},{9,... | collective-permute-start | bytes 1572872 | tf_op jit(solution)/shard_map/u5/ppermute | solution.py:71
  83.6 4.6 %spread.2.refs_2_ = bf16[16896,256]{1,0:T(8,128)(2,1)S(1)} custom-call(s32[4]{0:T(128)S(1)} %copy-done.33, bf16[49280,128]{1,0:T(8,128)(2,1)} %all-gather.2.cloned.1.call-done.loads), custom_call_target="tpu_custom_call" | custom-call | tf_op jit(solution)/shard_map/spread/pallas_call | solution.py:156
  88.2 3.3 %collective-permute-start.24 = (bf16[4,512,128]{2,1,0:T(8,128)(2,1)S(1)}, bf16[4,512,128]{2,1,0:T(8,128)(2,1)S(1)}, u32[]{:S(2)}, u32[]{:S(2)}) collective-permute-start(bf16[4,512,128]{2,1,0:T(8,128)(2,1)S(1)} %get-tuple-element.97.refs_4_), channel_id=1, source_target_pairs={{0,24},{1,25},{2,26},{3,27},{4,28},{5,29},{6,30},{7,31},{8,16},{9,... | collective-permute-start | bytes 1572872 | tf_op jit(solution)/shard_map/u6/ppermute | solution.py:71
  91.5 4.6 %spread.3.refs_3_ = bf16[16896,256]{1,0:T(8,128)(2,1)S(1)} custom-call(s32[4]{0:T(128)S(1)} %copy-done.33, bf16[49280,128]{1,0:T(8,128)(2,1)} %all-gather.2.cloned.1.call-done.loads), custom_call_target="tpu_custom_call" | custom-call | tf_op jit(solution)/shard_map/spread/pallas_call | solution.py:156
  98.6 3.4 %terms.4.refs_3_ = f32[512,512]{1,0:T(8,128)S(1)} custom-call(bf16[16896,256]{1,0:T(8,128)(2,1)S(1)} %get-tuple-element.92.refs_0_, bf16[16896,256]{1,0:T(8,128)(2,1)S(1)} %get-tuple-element.95.refs_1_, bf16[4,512,128]{2,1,0:T(8,128)(2,1)S(1)} %bitcast.8, bf16[4,512,128]{2,1,0:T(8,128)(2,1)S(1)} %get-tuple-element.69.refs_3_.refs_5_, ...), custom_call_target="tpu_custom_call" | custom-call | tf_op jit(solution)/shard_map/terms/pallas_call | solution.py:190
  102.0 3.2 %collective-permute-start.27 = (bf16[4,512,128]{2,1,0:T(8,128)(2,1)S(1)}, bf16[4,512,128]{2,1,0:T(8,128)(2,1)S(1)}, u32[]{:S(2)}, u32[]{:S(2)}) collective-permute-start(bf16[4,512,128]{2,1,0:T(8,128)(2,1)S(1)} %get-tuple-element.117.refs_7_), channel_id=1, source_target_pairs={{0,24},{1,25},{2,26},{3,27},{4,28},{5,29},{6,30},{7,31},{8,16},{9,... | collective-permute-start | bytes 1572872 | tf_op jit(solution)/shard_map/u7/ppermute | solution.py:71
  105.2 4.5 %terms.5.refs_3_ = f32[512,512]{1,0:T(8,128)S(1)} custom-call(bf16[16896,256]{1,0:T(8,128)(2,1)S(1)} %get-tuple-element.92.refs_0_, bf16[16896,256]{1,0:T(8,128)(2,1)S(1)} %get-tuple-element.95.refs_1_, f32[512,512]{1,0:T(8,128)S(1)} %get-tuple-element.107.refs_2_, bf16[4,512,128]{2,1,0:T(8,128)(2,1)S(1)} %copy-done.23, bf16[4,512,128]{2,1,0:T(8,128)(2,1)S(1)} %copy-done.29, ...), custom_call_target="tpu_custom_call" | custom-call | tf_op jit(solution)/shard_map/terms/pallas_call | solution.py:190
  110.1 2.8 %collective-permute-done.27.refs_8_ = bf16[4,512,128]{2,1,0:T(8,128)(2,1)S(1)} collective-permute-done((bf16[4,512,128]{2,1,0:T(8,128)(2,1)S(1)}, bf16[4,512,128]{2,1,0:T(8,128)(2,1)S(1)}, u32[]{:S(2)}, u32[]{:S(2)}) %collective-permute-start.27) | collective-permute-done | bytes 524320 | tf_op jit(solution)/shard_map/u7/ppermute | solution.py:71
  112.9 2.1 %terms.6.refs_2_ = f32[512,512]{1,0:T(8,128)S(1)} custom-call(bf16[16896,256]{1,0:T(8,128)(2,1)S(1)} %get-tuple-element.92.refs_0_, bf16[16896,256]{1,0:T(8,128)(2,1)S(1)} %get-tuple-element.95.refs_1_, f32[512,512]{1,0:T(8,128)S(1)} %get-tuple-element.113.refs_2_, bf16[4,512,128]{2,1,0:T(8,128)(2,1)S(1)} %get-tuple-element.114.refs_3_, ...), custom_call_target="tpu_custom_call" | custom-call | tf_op jit(solution)/shard_map/terms/pallas_call | solution.py:190
  114.9 5.3 %collective-permute-done.30.refs_4_ = bf16[4,512,128]{2,1,0:T(8,128)(2,1)S(1)} collective-permute-done((bf16[4,512,128]{2,1,0:T(8,128)(2,1)S(1)}, bf16[4,512,128]{2,1,0:T(8,128)(2,1)S(1)}, u32[]{:S(2)}, u32[]{:S(2)}) %collective-permute-start.30) | collective-permute-done | bytes 524320 | tf_op jit(solution)/shard_map/v6/ppermute | solution.py:71
  (137 shorter events, 10.9 us)
Async XLA Ops:
  6.5 77.1 %all-gather.2.cloned.1.call-start = ((), (), s32[]{:S(2)}) async-start(), calls=%async_computation | async-start | bytes 14192640 | tf_op jit(solution)/shard_map/loads/all_gather | solution.py:207
  11.0 13.8 %collective-permute-start = (bf16[4,512,128]{2,1,0:T(8,128)(2,1)S(1)}, bf16[4,512,128]{2,1,0:T(8,128)(2,1)S(1)}, u32[]{:S(2)}, u32[]{:S(2)}) collective-permute-start(bf16[4,512,128]{2,1,0:T(8,128)(2,1)S(1)} %bitcast.4), channel_id=1, source_target_pairs={{0,1},{1,2},{2,3},{3,4},{4,5},{5,6},{6,7},{7,0},{8,9},{9,10},{10,1... | collective-permute-start | bytes 1572872 | tf_op jit(solution)/shard_map/s1/ppermute | solution.py:71
  14.2 18.6 %collective-permute-start.1 = (bf16[4,512,128]{2,1,0:T(8,128)(2,1)S(1)}, bf16[4,512,128]{2,1,0:T(8,128)(2,1)S(1)}, u32[]{:S(2)}, u32[]{:S(2)}) collective-permute-start(bf16[4,512,128]{2,1,0:T(8,128)(2,1)S(1)} %bitcast.5), channel_id=1, source_target_pairs={{0,8},{1,9},{2,10},{3,11},{4,12},{5,13},{6,14},{7,15},{8,0},{9,1},... | collective-permute-start | bytes 1572872 | tf_op jit(solution)/shard_map/q0/ppermute | solution.py:71
  15.7 17.2 %collective-permute-start.2 = (bf16[4,512,128]{2,1,0:T(8,128)(2,1)S(1)}, bf16[4,512,128]{2,1,0:T(8,128)(2,1)S(1)}, u32[]{:S(2)}, u32[]{:S(2)}) collective-permute-start(bf16[4,512,128]{2,1,0:T(8,128)(2,1)S(1)} %bitcast.6), channel_id=1, source_target_pairs={{0,24},{1,25},{2,26},{3,27},{4,28},{5,29},{6,30},{7,31},{8,16},{9,... | collective-permute-start | bytes 1572872 | tf_op jit(solution)/shard_map/u0/ppermute | solution.py:71
  17.9 15.1 %collective-permute-start.3 = (bf16[4,512,128]{2,1,0:T(8,128)(2,1)S(1)}, bf16[4,512,128]{2,1,0:T(8,128)(2,1)S(1)}, u32[]{:S(2)}, u32[]{:S(2)}) collective-permute-start(bf16[4,512,128]{2,1,0:T(8,128)(2,1)S(1)} %bitcast.7), channel_id=1, source_target_pairs={{0,7},{1,0},{2,1},{3,2},{4,3},{5,4},{6,5},{7,6},{8,15},{9,8},{10,9... | collective-permute-start | bytes 1572872 | tf_op jit(solution)/shard_map/s7/ppermute | solution.py:71
  24.7 10.4 %collective-permute-start.4 = (bf16[4,512,128]{2,1,0:T(8,128)(2,1)S(1)}, bf16[4,512,128]{2,1,0:T(8,128)(2,1)S(1)}, u32[]{:S(2)}, u32[]{:S(2)}) collective-permute-start(bf16[4,512,128]{2,1,0:T(8,128)(2,1)S(1)} %get-tuple-element.66.refs_6_), channel_id=1, source_target_pairs={{0,1},{1,2},{2,3},{3,4},{4,5},{5,6},{6,7},{7,0},{8,9},{9,10},{10,1... | collective-permute-start | bytes 1572872 | tf_op jit(solution)/shard_map/s2/ppermute | solution.py:71
  28.4 14.8 %collective-permute-start.5 = (bf16[4,512,128]{2,1,0:T(8,128)(2,1)S(1)}, bf16[4,512,128]{2,1,0:T(8,128)(2,1)S(1)}, u32[]{:S(2)}, u32[]{:S(2)}) collective-permute-start(bf16[4,512,128]{2,1,0:T(8,128)(2,1)S(1)} %get-tuple-element.66.refs_6_), channel_id=1, source_target_pairs={{0,24},{1,25},{2,26},{3,27},{4,28},{5,29},{6,30},{7,31},{8,16},{9,... | collective-permute-start | bytes 1572872 | tf_op jit(solution)/shard_map/u1/ppermute | solution.py:71
  32.8 10.4 %collective-permute-start.6 = (bf16[4,512,128]{2,1,0:T(8,128)(2,1)S(1)}, bf16[4,512,128]{2,1,0:T(8,128)(2,1)S(1)}, u32[]{:S(2)}, u32[]{:S(2)}) collective-permute-start(bf16[4,512,128]{2,1,0:T(8,128)(2,1)S(1)} %get-tuple-element.69.refs_3_.refs_5_), channel_id=1, source_target_pairs={{0,1},{1,2},{2,3},{3,4},{4,5},{5,6},{6,7},{7,0},{8,9},{9,10},{10,1... | collective-permute-start | bytes 1572872 | tf_op jit(solution)/shard_map/q1/ppermute | solution.py:71
  32.9 15.9 %collective-permute-start.7 = (bf16[4,512,128]{2,1,0:T(8,128)(2,1)S(1)}, bf16[4,512,128]{2,1,0:T(8,128)(2,1)S(1)}, u32[]{:S(2)}, u32[]{:S(2)}) collective-permute-start(bf16[4,512,128]{2,1,0:T(8,128)(2,1)S(1)} %get-tuple-element.69.refs_3_.refs_5_), channel_id=1, source_target_pairs={{0,24},{1,25},{2,26},{3,27},{4,28},{5,29},{6,30},{7,31},{8,16},{9,... | collective-permute-start | bytes 1572872 | tf_op jit(solution)/shard_map/v0/ppermute | solution.py:71
  35.1 13.7 %collective-permute-start.8 = (bf16[4,512,128]{2,1,0:T(8,128)(2,1)S(1)}, bf16[4,512,128]{2,1,0:T(8,128)(2,1)S(1)}, u32[]{:S(2)}, u32[]{:S(2)}) collective-permute-start(bf16[4,512,128]{2,1,0:T(8,128)(2,1)S(1)} %get-tuple-element.72.refs_10_), channel_id=1, source_target_pairs={{0,1},{1,2},{2,3},{3,4},{4,5},{5,6},{6,7},{7,0},{8,9},{9,10},{10,1... | collective-permute-start | bytes 1572872 | tf_op jit(solution)/shard_map/s3/ppermute | solution.py:71
  38.8 15.6 %collective-permute-start.9 = (bf16[4,512,128]{2,1,0:T(8,128)(2,1)S(1)}, bf16[4,512,128]{2,1,0:T(8,128)(2,1)S(1)}, u32[]{:S(2)}, u32[]{:S(2)}) collective-permute-start(bf16[4,512,128]{2,1,0:T(8,128)(2,1)S(1)} %get-tuple-element.72.refs_10_), channel_id=1, source_target_pairs={{0,24},{1,25},{2,26},{3,27},{4,28},{5,29},{6,30},{7,31},{8,16},{9,... | collective-permute-start | bytes 1572872 | tf_op jit(solution)/shard_map/u2/ppermute | solution.py:71
  43.2 11.2 %collective-permute-start.10 = (bf16[4,512,128]{2,1,0:T(8,128)(2,1)S(1)}, bf16[4,512,128]{2,1,0:T(8,128)(2,1)S(1)}, u32[]{:S(2)}, u32[]{:S(2)}) collective-permute-start(bf16[4,512,128]{2,1,0:T(8,128)(2,1)S(1)} %get-tuple-element.75.refs_7_), channel_id=1, source_target_pairs={{0,1},{1,2},{2,3},{3,4},{4,5},{5,6},{6,7},{7,0},{8,9},{9,10},{10,1... | collective-permute-start | bytes 1572872 | tf_op jit(solution)/shard_map/q2/ppermute | solution.py:71
  44.4 15.6 %collective-permute-start.11 = (bf16[4,512,128]{2,1,0:T(8,128)(2,1)S(1)}, bf16[4,512,128]{2,1,0:T(8,128)(2,1)S(1)}, u32[]{:S(2)}, u32[]{:S(2)}) collective-permute-start(bf16[4,512,128]{2,1,0:T(8,128)(2,1)S(1)} %get-tuple-element.75.refs_7_), channel_id=1, source_target_pairs={{0,24},{1,25},{2,26},{3,27},{4,28},{5,29},{6,30},{7,31},{8,16},{9,... | collective-permute-start | bytes 1572872 | tf_op jit(solution)/shard_map/v1/ppermute | solution.py:71
  48.8 11.2 %collective-permute-start.12 = (bf16[4,512,128]{2,1,0:T(8,128)(2,1)S(1)}, bf16[4,512,128]{2,1,0:T(8,128)(2,1)S(1)}, u32[]{:S(2)}, u32[]{:S(2)}) collective-permute-start(bf16[4,512,128]{2,1,0:T(8,128)(2,1)S(1)} %get-tuple-element.78.refs_3_), channel_id=1, source_target_pairs={{0,1},{1,2},{2,3},{3,4},{4,5},{5,6},{6,7},{7,0},{8,9},{9,10},{10,1... | collective-permute-start | bytes 1572872 | tf_op jit(solution)/shard_map/s4/ppermute | solution.py:71
  50.0 15.6 %collective-permute-start.13 = (bf16[4,512,128]{2,1,0:T(8,128)(2,1)S(1)}, bf16[4,512,128]{2,1,0:T(8,128)(2,1)S(1)}, u32[]{:S(2)}, u32[]{:S(2)}) collective-permute-start(bf16[4,512,128]{2,1,0:T(8,128)(2,1)S(1)} %get-tuple-element.78.refs_3_), channel_id=1, source_target_pairs={{0,24},{1,25},{2,26},{3,27},{4,28},{5,29},{6,30},{7,31},{8,16},{9,... | collective-permute-start | bytes 1572872 | tf_op jit(solution)/shard_map/u3/ppermute | solution.py:71
  54.5 11.2 %collective-permute-start.14 = (bf16[4,512,128]{2,1,0:T(8,128)(2,1)S(1)}, bf16[4,512,128]{2,1,0:T(8,128)(2,1)S(1)}, u32[]{:S(2)}, u32[]{:S(2)}) collective-permute-start(bf16[4,512,128]{2,1,0:T(8,128)(2,1)S(1)} %get-tuple-element.81.refs_11_), channel_id=1, source_target_pairs={{0,1},{1,2},{2,3},{3,4},{4,5},{5,6},{6,7},{7,0},{8,9},{9,10},{10,1... | collective-permute-start | bytes 1572872 | tf_op jit(solution)/shard_map/q3/ppermute | solution.py:71
  55.7 15.6 %collective-permute-start.15 = (bf16[4,512,128]{2,1,0:T(8,128)(2,1)S(1)}, bf16[4,512,128]{2,1,0:T(8,128)(2,1)S(1)}, u32[]{:S(2)}, u32[]{:S(2)}) collective-permute-start(bf16[4,512,128]{2,1,0:T(8,128)(2,1)S(1)} %get-tuple-element.81.refs_11_), channel_id=1, source_target_pairs={{0,24},{1,25},{2,26},{3,27},{4,28},{5,29},{6,30},{7,31},{8,16},{9,... | collective-permute-start | bytes 1572872 | tf_op jit(solution)/shard_map/v2/ppermute | solution.py:71
  60.1 11.2 %collective-permute-start.16 = (bf16[4,512,128]{2,1,0:T(8,128)(2,1)S(1)}, bf16[4,512,128]{2,1,0:T(8,128)(2,1)}, u32[]{:S(2)}, u32[]{:S(2)}) collective-permute-start(bf16[4,512,128]{2,1,0:T(8,128)(2,1)S(1)} %get-tuple-element.84.refs_7_), channel_id=1, source_target_pairs={{0,1},{1,2},{2,3},{3,4},{4,5},{5,6},{6,7},{7,0},{8,9},{9,10},{10,1... | collective-permute-start | bytes 1572872 | tf_op jit(solution)/shard_map/s5/ppermute | solution.py:71
  61.3 12.4 %collective-permute-start.17 = (bf16[4,512,128]{2,1,0:T(8,128)(2,1)S(1)}, bf16[4,512,128]{2,1,0:T(8,128)(2,1)S(1)}, u32[]{:S(2)}, u32[]{:S(2)}) collective-permute-start(bf16[4,512,128]{2,1,0:T(8,128)(2,1)S(1)} %get-tuple-element.84.refs_7_), channel_id=1, source_target_pairs={{0,24},{1,25},{2,26},{3,27},{4,28},{5,29},{6,30},{7,31},{8,16},{9,... | collective-permute-start | bytes 1572872 | tf_op jit(solution)/shard_map/u4/ppermute | solution.py:71
  65.7 10.1 %collective-permute-start.18 = (bf16[4,512,128]{2,1,0:T(8,128)(2,1)S(1)}, bf16[4,512,128]{2,1,0:T(8,128)(2,1)}, u32[]{:S(2)}, u32[]{:S(2)}) collective-permute-start(bf16[4,512,128]{2,1,0:T(8,128)(2,1)S(1)} %get-tuple-element.87.refs_4_), channel_id=1, source_target_pairs={{0,1},{1,2},{2,3},{3,4},{4,5},{5,6},{6,7},{7,0},{8,9},{9,10},{10,1... | collective-permute-start | bytes 1572872 | tf_op jit(solution)/shard_map/q4/ppermute | solution.py:71
  66.9 15.8 %collective-permute-start.19 = (bf16[4,512,128]{2,1,0:T(8,128)(2,1)S(1)}, bf16[4,512,128]{2,1,0:T(8,128)(2,1)S(1)}, u32[]{:S(2)}, u32[]{:S(2)}) collective-permute-start(bf16[4,512,128]{2,1,0:T(8,128)(2,1)S(1)} %get-tuple-element.87.refs_4_), channel_id=1, source_target_pairs={{0,24},{1,25},{2,26},{3,27},{4,28},{5,29},{6,30},{7,31},{8,16},{9,... | collective-permute-start | bytes 1572872 | tf_op jit(solution)/shard_map/v3/ppermute | solution.py:71
  71.3 16.9 %collective-permute-start.20 = (bf16[4,512,128]{2,1,0:T(8,128)(2,1)}, bf16[4,512,128]{2,1,0:T(8,128)(2,1)S(1)}, u32[]{:S(2)}, u32[]{:S(2)}) collective-permute-start(bf16[4,512,128]{2,1,0:T(8,128)(2,1)} %get-tuple-element.90.refs_11_), channel_id=1, source_target_pairs={{0,1},{1,2},{2,3},{3,4},{4,5},{5,6},{6,7},{7,0},{8,9},{9,10},{10,1... | collective-permute-start | bytes 1572872 | tf_op jit(solution)/shard_map/s6/ppermute | solution.py:71
  75.8 20.4 %collective-permute-start.22 = (bf16[4,512,128]{2,1,0:T(8,128)(2,1)}, bf16[4,512,128]{2,1,0:T(8,128)(2,1)S(1)}, u32[]{:S(2)}, u32[]{:S(2)}) collective-permute-start(bf16[4,512,128]{2,1,0:T(8,128)(2,1)} %get-tuple-element.94.refs_8_), channel_id=1, source_target_pairs={{0,1},{1,2},{2,3},{3,4},{4,5},{5,6},{6,7},{7,0},{8,9},{9,10},{10,1... | collective-permute-start | bytes 1572872 | tf_op jit(solution)/shard_map/q5/ppermute | solution.py:71
  78.2 17.9 %collective-permute-start.21 = (bf16[4,512,128]{2,1,0:T(8,128)(2,1)}, bf16[4,512,128]{2,1,0:T(8,128)(2,1)S(1)}, u32[]{:S(2)}, u32[]{:S(2)}) collective-permute-start(bf16[4,512,128]{2,1,0:T(8,128)(2,1)} %get-tuple-element.90.refs_11_), channel_id=1, source_target_pairs={{0,24},{1,25},{2,26},{3,27},{4,28},{5,29},{6,30},{7,31},{8,16},{9,... | collective-permute-start | bytes 1572872 | tf_op jit(solution)/shard_map/u5/ppermute | solution.py:71
  82.6 19.4 %collective-permute-start.23 = (bf16[4,512,128]{2,1,0:T(8,128)(2,1)}, bf16[4,512,128]{2,1,0:T(8,128)(2,1)}, u32[]{:S(2)}, u32[]{:S(2)}) collective-permute-start(bf16[4,512,128]{2,1,0:T(8,128)(2,1)} %get-tuple-element.94.refs_8_), channel_id=1, source_target_pairs={{0,24},{1,25},{2,26},{3,27},{4,28},{5,29},{6,30},{7,31},{8,16},{9,... | collective-permute-start | bytes 1572872 | tf_op jit(solution)/shard_map/v4/ppermute | solution.py:71
  88.2 13.8 %collective-permute-start.24 = (bf16[4,512,128]{2,1,0:T(8,128)(2,1)S(1)}, bf16[4,512,128]{2,1,0:T(8,128)(2,1)S(1)}, u32[]{:S(2)}, u32[]{:S(2)}) collective-permute-start(bf16[4,512,128]{2,1,0:T(8,128)(2,1)S(1)} %get-tuple-element.97.refs_4_), channel_id=1, source_target_pairs={{0,24},{1,25},{2,26},{3,27},{4,28},{5,29},{6,30},{7,31},{8,16},{9,... | collective-permute-start | bytes 1572872 | tf_op jit(solution)/shard_map/u6/ppermute | solution.py:71
  96.2 13.5 %collective-permute-start.25 = (bf16[4,512,128]{2,1,0:T(8,128)(2,1)S(1)}, bf16[4,512,128]{2,1,0:T(8,128)(2,1)S(1)}, u32[]{:S(2)}, u32[]{:S(2)}) collective-permute-start(bf16[4,512,128]{2,1,0:T(8,128)(2,1)S(1)} %get-tuple-element.106.refs_12_), channel_id=1, source_target_pairs={{0,1},{1,2},{2,3},{3,4},{4,5},{5,6},{6,7},{7,0},{8,9},{9,10},{10,1... | collective-permute-start | bytes 1572872 | tf_op jit(solution)/shard_map/q6/ppermute | solution.py:71
  96.9 12.9 %collective-permute-start.26 = (bf16[4,512,128]{2,1,0:T(8,128)(2,1)S(1)}, bf16[4,512,128]{2,1,0:T(8,128)(2,1)S(1)}, u32[]{:S(2)}, u32[]{:S(2)}) collective-permute-start(bf16[4,512,128]{2,1,0:T(8,128)(2,1)S(1)} %get-tuple-element.106.refs_12_), channel_id=1, source_target_pairs={{0,24},{1,25},{2,26},{3,27},{4,28},{5,29},{6,30},{7,31},{8,16},{9,... | collective-permute-start | bytes 1572872 | tf_op jit(solution)/shard_map/v5/ppermute | solution.py:71
  97.4 12.7 %collective-permute-start.28 = (bf16[4,512,128]{2,1,0:T(8,128)(2,1)S(1)}, bf16[4,512,128]{2,1,0:T(8,128)(2,1)S(1)}, u32[]{:S(2)}, u32[]{:S(2)}) collective-permute-start(bf16[4,512,128]{2,1,0:T(8,128)(2,1)S(1)} %get-tuple-element.99.refs_5_), channel_id=1, source_target_pairs={{0,7},{1,0},{2,1},{3,2},{4,3},{5,4},{6,5},{7,6},{8,15},{9,8},{10,9... | collective-permute-start | bytes 1572872 | tf_op jit(solution)/shard_map/v7/ppermute | solution.py:71
  102.0 10.8 %collective-permute-start.27 = (bf16[4,512,128]{2,1,0:T(8,128)(2,1)S(1)}, bf16[4,512,128]{2,1,0:T(8,128)(2,1)S(1)}, u32[]{:S(2)}, u32[]{:S(2)}) collective-permute-start(bf16[4,512,128]{2,1,0:T(8,128)(2,1)S(1)} %get-tuple-element.117.refs_7_), channel_id=1, source_target_pairs={{0,24},{1,25},{2,26},{3,27},{4,28},{5,29},{6,30},{7,31},{8,16},{9,... | collective-permute-start | bytes 1572872 | tf_op jit(solution)/shard_map/u7/ppermute | solution.py:71
  109.8 10.5 %collective-permute-start.30 = (bf16[4,512,128]{2,1,0:T(8,128)(2,1)S(1)}, bf16[4,512,128]{2,1,0:T(8,128)(2,1)S(1)}, u32[]{:S(2)}, u32[]{:S(2)}) collective-permute-start(bf16[4,512,128]{2,1,0:T(8,128)(2,1)S(1)} %get-tuple-element.115.refs_5_), channel_id=1, source_target_pairs={{0,24},{1,25},{2,26},{3,27},{4,28},{5,29},{6,30},{7,31},{8,16},{9,... | collective-permute-start | bytes 1572872 | tf_op jit(solution)/shard_map/v6/ppermute | solution.py:71
  110.1 10.4 %collective-permute-start.29 = (bf16[4,512,128]{2,1,0:T(8,128)(2,1)S(1)}, bf16[4,512,128]{2,1,0:T(8,128)(2,1)S(1)}, u32[]{:S(2)}, u32[]{:S(2)}) collective-permute-start(bf16[4,512,128]{2,1,0:T(8,128)(2,1)S(1)} %get-tuple-element.118), channel_id=1, source_target_pairs={{0,7},{1,0},{2,1},{3,2},{4,3},{5,4},{6,5},{7,6},{8,15},{9,8},{10,9... | collective-permute-start | bytes 1572872 | tf_op jit(solution)/shard_map/q7/ppermute | solution.py:71
  (35 other events, 554.0 us)
Sparse Core Ops, SparseCore 0:
  10.0 71.8 all-gather.1

commit v3 on v2

--- a/solution.py
+++ b/solution.py
@@ -240,24 +240,25 @@
     for k in range(2, 6):
         turn(k)
     dense = {0: spread(counts, everything, (0, 1))}
-    order.meet((s, 6), (dense, 0), (v, 0))
+    order.meet((s, 6), (dense, 0))
     cross(s, u, 6, "u")
-    v[7] = send(v[0], BACK_Z, "v7")
-    dense[1] = spread(counts, everything, (2, 3))
-    order.meet((u, 5), (q, 5), (dense, 1))
+    order.meet((u, 5))
+    order.meet((q, 5))
     along(q, 6, "q")
     cross(q, v, 5, "v")
+    dense[1] = spread(counts, everything, (2, 3))
 
     def terms(ks, names):
         return [(a[k], k * 4 + i) for k in ks for i, a in enumerate((s, q, u, v)) if "squv"[i] in names]
 
     total = {0: add_terms(dense, None, terms(range(0, 3), "squv"))}
-    order.meet((v, 4), (u, 6), (total, 0), (s, 7), (q, 0))
+    order.meet((v, 4), (u, 6), (total, 0), (s, 7), (v, 0), (q, 0))
     cross(s, u, 7, "u")
     q[7] = send(q[0], BACK_Z, "q7")
+    v[7] = send(v[0], BACK_Z, "v7")
+    order.meet((q, 6), (v, 5))
+    cross(q, v, 6, "v")
     total[1] = add_terms(dense, total[0], terms((3,), "squv") + terms((4,), "squv") + terms((5,), "squ"))
-    order.meet((q, 6), (v, 5), (total, 1))
-    cross(q, v, 6, "v")
     total = add_terms(dense, total[1], terms((5,), "v") + terms((6,), "squ") + terms((7,), "suv"))
     out = add_terms(dense, total, terms((7,), "q") + terms((6,), "v"), jnp.bfloat16)
     return out.reshape(out.shape[0], TILES, WIDTH)

time: 130 us -> 128 us (0.985)
  waiting for transfers between devices: 20.5 us -> 16.7 us
  starting transfers between devices: 68.3 us -> 71.4 us
    ppermute x31, waiting for transfers between devices: 20.4 us -> 16.6 us  [send(): return lax.ppermute(v, AXES, pairs)]
    ppermute x31, starting transfers between devices: 68.3 us -> 71.4 us  [send(): return lax.ppermute(v, AXES, pairs)]
    unnamed x71 -> x67, local copies, waits for them, and re-layouts: 4.3 us -> 4.15 us
where the time goes in v3:
time: 128 us
  starting transfers between devices  71.4 us (56%)
  Pallas kernels  21.1 us (16%)
  waiting for transfers between devices  16.7 us (13%)
  between operations  14 us (11%)
  local copies, waits for them, and re-layouts  5.07 us (4%)
    ppermute x31, starting transfers between devices, send(): return lax.ppermute(v, AXES, pairs)  71.4 us
    ppermute x31, waiting for transfers between devices, send(): return lax.ppermute(v, AXES, pairs)  16.6 us
    pallas_call x4, Pallas kernels, add_terms(): pl.pallas_call(functools.partial(terms_kernel, [q for _, q in pieces], fr...  10.8 us
    pallas_call x2, Pallas kernels, spread(): pl.pallas_call(functools.partial(spread_kernel, tiles), out_shape=pltpu.V...  9.12 us
    unnamed x67, local copies, waits for them, and re-layouts  4.15 us
  transfers between devices with their start and end apart: 32, of which 7 were waited for; matrix products, arithmetic and copies ran while one was open for 1% of the time, Pallas kernels for 15%

profile of v3, /device:TPU:96, one launch (start us, length us, event | category | flops | bytes accessed | tf_op | source)
XLA Modules:
  0.0 128.2 jit_solution(5030096110355337006)
XLA Ops:
  6.5 1.4 %copy-done.30 = bf16[4,12,128,128]{3,2,1,0:T(8,128)(2,1)S(1)} copy-done((bf16[4,12,128,128]{3,2,1,0:T(8,128)(2,1)S(1)}, bf16[4,12,128,128]{3,2,1,0:T(8,128)(2,1)}, u32[]{:S(2)}) %copy-start.30) | copy-done | bytes 1572888
  11.0 3.2 %collective-permute-start = (bf16[4,512,128]{2,1,0:T(8,128)(2,1)S(1)}, bf16[4,512,128]{2,1,0:T(8,128)(2,1)S(1)}, u32[]{:S(2)}, u32[]{:S(2)}) collective-permute-start(bf16[4,512,128]{2,1,0:T(8,128)(2,1)S(1)} %bitcast.4), channel_id=1, source_target_pairs={{0,1},{1,2},{2,3},{3,4},{4,5},{5,6},{6,7},{7,0},{8,9},{9,10},{10,1... | collective-permute-start | bytes 1572872 | tf_op jit(solution)/shard_map/s1/ppermute | solution.py:71
  14.2 1.6 %collective-permute-start.1 = (bf16[4,512,128]{2,1,0:T(8,128)(2,1)S(1)}, bf16[4,512,128]{2,1,0:T(8,128)(2,1)S(1)}, u32[]{:S(2)}, u32[]{:S(2)}) collective-permute-start(bf16[4,512,128]{2,1,0:T(8,128)(2,1)S(1)} %bitcast.5), channel_id=1, source_target_pairs={{0,8},{1,9},{2,10},{3,11},{4,12},{5,13},{6,14},{7,15},{8,0},{9,1},... | collective-permute-start | bytes 1572872 | tf_op jit(solution)/shard_map/q0/ppermute | solution.py:71
  15.7 2.2 %collective-permute-start.2 = (bf16[4,512,128]{2,1,0:T(8,128)(2,1)S(1)}, bf16[4,512,128]{2,1,0:T(8,128)(2,1)S(1)}, u32[]{:S(2)}, u32[]{:S(2)}) collective-permute-start(bf16[4,512,128]{2,1,0:T(8,128)(2,1)S(1)} %bitcast.6), channel_id=1, source_target_pairs={{0,24},{1,25},{2,26},{3,27},{4,28},{5,29},{6,30},{7,31},{8,16},{9,... | collective-permute-start | bytes 1572872 | tf_op jit(solution)/shard_map/u0/ppermute | solution.py:71
  17.9 6.8 %collective-permute-done.refs_1_ = bf16[4,512,128]{2,1,0:T(8,128)(2,1)S(1)} collective-permute-done((bf16[4,512,128]{2,1,0:T(8,128)(2,1)S(1)}, bf16[4,512,128]{2,1,0:T(8,128)(2,1)S(1)}, u32[]{:S(2)}, u32[]{:S(2)}) %collective-permute-start) | collective-permute-done | bytes 524320 | tf_op jit(solution)/shard_map/s1/ppermute | solution.py:71
  24.7 3.7 %collective-permute-start.4 = (bf16[4,512,128]{2,1,0:T(8,128)(2,1)S(1)}, bf16[4,512,128]{2,1,0:T(8,128)(2,1)S(1)}, u32[]{:S(2)}, u32[]{:S(2)}) collective-permute-start(bf16[4,512,128]{2,1,0:T(8,128)(2,1)S(1)} %get-tuple-element.65.refs_6_), channel_id=1, source_target_pairs={{0,1},{1,2},{2,3},{3,4},{4,5},{5,6},{6,7},{7,0},{8,9},{9,10},{10,1... | collective-permute-start | bytes 1572872 | tf_op jit(solution)/shard_map/s2/ppermute | solution.py:71
  28.4 4.4 %collective-permute-start.5 = (bf16[4,512,128]{2,1,0:T(8,128)(2,1)S(1)}, bf16[4,512,128]{2,1,0:T(8,128)(2,1)S(1)}, u32[]{:S(2)}, u32[]{:S(2)}) collective-permute-start(bf16[4,512,128]{2,1,0:T(8,128)(2,1)S(1)} %get-tuple-element.65.refs_6_), channel_id=1, source_target_pairs={{0,24},{1,25},{2,26},{3,27},{4,28},{5,29},{6,30},{7,31},{8,16},{9,... | collective-permute-start | bytes 1572872 | tf_op jit(solution)/shard_map/u1/ppermute | solution.py:71
  33.0 2.1 %collective-permute-done.4.refs_1_ = bf16[4,512,128]{2,1,0:T(8,128)(2,1)S(1)} collective-permute-done((bf16[4,512,128]{2,1,0:T(8,128)(2,1)S(1)}, bf16[4,512,128]{2,1,0:T(8,128)(2,1)S(1)}, u32[]{:S(2)}, u32[]{:S(2)}) %collective-permute-start.4) | collective-permute-done | bytes 524320 | tf_op jit(solution)/shard_map/s2/ppermute | solution.py:71
  35.1 3.7 %collective-permute-start.8 = (bf16[4,512,128]{2,1,0:T(8,128)(2,1)S(1)}, bf16[4,512,128]{2,1,0:T(8,128)(2,1)S(1)}, u32[]{:S(2)}, u32[]{:S(2)}) collective-permute-start(bf16[4,512,128]{2,1,0:T(8,128)(2,1)S(1)} %get-tuple-element.71.refs_10_), channel_id=1, source_target_pairs={{0,1},{1,2},{2,3},{3,4},{4,5},{5,6},{6,7},{7,0},{8,9},{9,10},{10,1... | collective-permute-start | bytes 1572872 | tf_op jit(solution)/shard_map/s3/ppermute | solution.py:71
  38.8 4.4 %collective-permute-start.9 = (bf16[4,512,128]{2,1,0:T(8,128)(2,1)S(1)}, bf16[4,512,128]{2,1,0:T(8,128)(2,1)S(1)}, u32[]{:S(2)}, u32[]{:S(2)}) collective-permute-start(bf16[4,512,128]{2,1,0:T(8,128)(2,1)S(1)} %get-tuple-element.71.refs_10_), channel_id=1, source_target_pairs={{0,24},{1,25},{2,26},{3,27},{4,28},{5,29},{6,30},{7,31},{8,16},{9,... | collective-permute-start | bytes 1572872 | tf_op jit(solution)/shard_map/u2/ppermute | solution.py:71
  44.4 4.4 %collective-permute-start.11 = (bf16[4,512,128]{2,1,0:T(8,128)(2,1)S(1)}, bf16[4,512,128]{2,1,0:T(8,128)(2,1)S(1)}, u32[]{:S(2)}, u32[]{:S(2)}) collective-permute-start(bf16[4,512,128]{2,1,0:T(8,128)(2,1)S(1)} %get-tuple-element.74.refs_7_), channel_id=1, source_target_pairs={{0,24},{1,25},{2,26},{3,27},{4,28},{5,29},{6,30},{7,31},{8,16},{9,... | collective-permute-start | bytes 1572872 | tf_op jit(solution)/shard_map/v1/ppermute | solution.py:71
  48.8 1.2 collective-permute-start.12
  50.0 4.4 %collective-permute-start.13 = (bf16[4,512,128]{2,1,0:T(8,128)(2,1)S(1)}, bf16[4,512,128]{2,1,0:T(8,128)(2,1)S(1)}, u32[]{:S(2)}, u32[]{:S(2)}) collective-permute-start(bf16[4,512,128]{2,1,0:T(8,128)(2,1)S(1)} %get-tuple-element.77.refs_3_), channel_id=1, source_target_pairs={{0,24},{1,25},{2,26},{3,27},{4,28},{5,29},{6,30},{7,31},{8,16},{9,... | collective-permute-start | bytes 1572872 | tf_op jit(solution)/shard_map/u3/ppermute | solution.py:71
  55.7 4.4 %collective-permute-start.15 = (bf16[4,512,128]{2,1,0:T(8,128)(2,1)S(1)}, bf16[4,512,128]{2,1,0:T(8,128)(2,1)S(1)}, u32[]{:S(2)}, u32[]{:S(2)}) collective-permute-start(bf16[4,512,128]{2,1,0:T(8,128)(2,1)S(1)} %get-tuple-element.80.refs_11_), channel_id=1, source_target_pairs={{0,24},{1,25},{2,26},{3,27},{4,28},{5,29},{6,30},{7,31},{8,16},{9,... | collective-permute-start | bytes 1572872 | tf_op jit(solution)/shard_map/v2/ppermute | solution.py:71
  61.3 4.4 %collective-permute-start.17 = (bf16[4,512,128]{2,1,0:T(8,128)(2,1)S(1)}, bf16[4,512,128]{2,1,0:T(8,128)(2,1)S(1)}, u32[]{:S(2)}, u32[]{:S(2)}) collective-permute-start(bf16[4,512,128]{2,1,0:T(8,128)(2,1)S(1)} %get-tuple-element.83.refs_7_), channel_id=1, source_target_pairs={{0,24},{1,25},{2,26},{3,27},{4,28},{5,29},{6,30},{7,31},{8,16},{9,... | collective-permute-start | bytes 1572872 | tf_op jit(solution)/shard_map/u4/ppermute | solution.py:71
  66.9 4.4 %collective-permute-start.19 = (bf16[4,512,128]{2,1,0:T(8,128)(2,1)S(1)}, bf16[4,512,128]{2,1,0:T(8,128)(2,1)S(1)}, u32[]{:S(2)}, u32[]{:S(2)}) collective-permute-start(bf16[4,512,128]{2,1,0:T(8,128)(2,1)S(1)} %get-tuple-element.86.refs_4_), channel_id=1, source_target_pairs={{0,24},{1,25},{2,26},{3,27},{4,28},{5,29},{6,30},{7,31},{8,16},{9,... | collective-permute-start | bytes 1572872 | tf_op jit(solution)/shard_map/v3/ppermute | solution.py:71
  71.3 1.3 %collective-permute-start.20 = (bf16[4,512,128]{2,1,0:T(8,128)(2,1)}, bf16[4,512,128]{2,1,0:T(8,128)(2,1)S(1)}, u32[]{:S(2)}, u32[]{:S(2)}) collective-permute-start(bf16[4,512,128]{2,1,0:T(8,128)(2,1)} %get-tuple-element.89.refs_11_), channel_id=1, source_target_pairs={{0,1},{1,2},{2,3},{3,4},{4,5},{5,6},{6,7},{7,0},{8,9},{9,10},{10,1... | collective-permute-start | bytes 1572872 | tf_op jit(solution)/shard_map/s6/ppermute | solution.py:71
  72.6 4.4 %collective-permute-start.21 = (bf16[4,512,128]{2,1,0:T(8,128)(2,1)}, bf16[4,512,128]{2,1,0:T(8,128)(2,1)S(1)}, u32[]{:S(2)}, u32[]{:S(2)}) collective-permute-start(bf16[4,512,128]{2,1,0:T(8,128)(2,1)} %get-tuple-element.89.refs_11_), channel_id=1, source_target_pairs={{0,24},{1,25},{2,26},{3,27},{4,28},{5,29},{6,30},{7,31},{8,16},{9,... | collective-permute-start | bytes 1572872 | tf_op jit(solution)/shard_map/u5/ppermute | solution.py:71
  78.2 4.4 %collective-permute-start.23 = (bf16[4,512,128]{2,1,0:T(8,128)(2,1)}, bf16[4,512,128]{2,1,0:T(8,128)(2,1)}, u32[]{:S(2)}, u32[]{:S(2)}) collective-permute-start(bf16[4,512,128]{2,1,0:T(8,128)(2,1)} %get-tuple-element.93.refs_8_), channel_id=1, source_target_pairs={{0,24},{1,25},{2,26},{3,27},{4,28},{5,29},{6,30},{7,31},{8,16},{9,... | collective-permute-start | bytes 1572872 | tf_op jit(solution)/shard_map/v4/ppermute | solution.py:71
  83.5 4.6 %spread.2.refs_2_ = bf16[16896,256]{1,0:T(8,128)(2,1)S(1)} custom-call(s32[4]{0:T(128)S(1)} %copy-done.31, bf16[49280,128]{1,0:T(8,128)(2,1)} %all-gather.2.cloned.1.call-done.loads), custom_call_target="tpu_custom_call" | custom-call | tf_op jit(solution)/shard_map/spread/pallas_call | solution.py:156
  89.4 2.8 %collective-permute-start.25 = (bf16[4,512,128]{2,1,0:T(8,128)(2,1)}, bf16[4,512,128]{2,1,0:T(8,128)(2,1)S(1)}, u32[]{:S(2)}, u32[]{:S(2)}) collective-permute-start(bf16[4,512,128]{2,1,0:T(8,128)(2,1)} %get-tuple-element.108.refs_12_), channel_id=1, source_target_pairs={{0,1},{1,2},{2,3},{3,4},{4,5},{5,6},{6,7},{7,0},{8,9},{9,10},{10,1... | collective-permute-start | bytes 1572872 | tf_op jit(solution)/shard_map/q6/ppermute | solution.py:71
  92.2 1.7 %collective-permute-start.26 = (bf16[4,512,128]{2,1,0:T(8,128)(2,1)}, bf16[4,512,128]{2,1,0:T(8,128)(2,1)S(1)}, u32[]{:S(2)}, u32[]{:S(2)}) collective-permute-start(bf16[4,512,128]{2,1,0:T(8,128)(2,1)} %get-tuple-element.108.refs_12_), channel_id=1, source_target_pairs={{0,24},{1,25},{2,26},{3,27},{4,28},{5,29},{6,30},{7,31},{8,16},{9,... | collective-permute-start | bytes 1572872 | tf_op jit(solution)/shard_map/v5/ppermute | solution.py:71
  94.0 4.6 %spread.3.refs_1_ = bf16[16896,256]{1,0:T(8,128)(2,1)S(1)} custom-call(s32[4]{0:T(128)S(1)} %copy-done.31, bf16[49280,128]{1,0:T(8,128)(2,1)} %all-gather.2.cloned.1.call-done.loads), custom_call_target="tpu_custom_call" | custom-call | tf_op jit(solution)/shard_map/spread/pallas_call | solution.py:156
  98.7 3.4 %terms.4.refs_3_ = f32[512,512]{1,0:T(8,128)S(1)} custom-call(bf16[16896,256]{1,0:T(8,128)(2,1)S(1)} %get-tuple-element.90.refs_0_, bf16[16896,256]{1,0:T(8,128)(2,1)S(1)} %spread.3.refs_1_, bf16[4,512,128]{2,1,0:T(8,128)(2,1)S(1)} %bitcast.8, bf16[4,512,128]{2,1,0:T(8,128)(2,1)S(1)} %get-tuple-element.68.refs_3_.refs_6_, ...), custom_call_target="tpu_custom_call" | custom-call | tf_op jit(solution)/shard_map/terms/pallas_call | solution.py:190
  102.2 1.6 %collective-permute-start.27 = (bf16[4,512,128]{2,1,0:T(8,128)(2,1)S(1)}, bf16[4,512,128]{2,1,0:T(8,128)(2,1)S(1)}, u32[]{:S(2)}, u32[]{:S(2)}) collective-permute-start(bf16[4,512,128]{2,1,0:T(8,128)(2,1)S(1)} %get-tuple-element.114.refs_7_), channel_id=1, source_target_pairs={{0,24},{1,25},{2,26},{3,27},{4,28},{5,29},{6,30},{7,31},{8,16},{9,... | collective-permute-start | bytes 1572872 | tf_op jit(solution)/shard_map/u7/ppermute | solution.py:71
  104.2 1.4 %collective-permute-start.30 = (bf16[4,512,128]{2,1,0:T(8,128)(2,1)S(1)}, bf16[4,512,128]{2,1,0:T(8,128)(2,1)S(1)}, u32[]{:S(2)}, u32[]{:S(2)}) collective-permute-start(bf16[4,512,128]{2,1,0:T(8,128)(2,1)S(1)} %get-tuple-element.112.refs_5_), channel_id=1, source_target_pairs={{0,24},{1,25},{2,26},{3,27},{4,28},{5,29},{6,30},{7,31},{8,16},{9,... | collective-permute-start | bytes 1572872 | tf_op jit(solution)/shard_map/v6/ppermute | solution.py:71
  105.8 4.7 %terms.5.refs_2_ = f32[512,512]{1,0:T(8,128)S(1)} custom-call(bf16[16896,256]{1,0:T(8,128)(2,1)S(1)} %get-tuple-element.90.refs_0_, bf16[16896,256]{1,0:T(8,128)(2,1)S(1)} %spread.3.refs_1_, f32[512,512]{1,0:T(8,128)S(1)} %get-tuple-element.103.refs_2_, bf16[4,512,128]{2,1,0:T(8,128)(2,1)S(1)} %copy-done.21, bf16[4,512,128]{2,1,0:T(8,128)(2,1)S(1)} %copy-done.27, ...), custom_call_target="tpu_custom_call" | custom-call | tf_op jit(solution)/shard_map/terms/pallas_call | solution.py:190
  110.5 2.2 %collective-permute-done.27.refs_8_ = bf16[4,512,128]{2,1,0:T(8,128)(2,1)S(1)} collective-permute-done((bf16[4,512,128]{2,1,0:T(8,128)(2,1)S(1)}, bf16[4,512,128]{2,1,0:T(8,128)(2,1)S(1)}, u32[]{:S(2)}, u32[]{:S(2)}) %collective-permute-start.27) | collective-permute-done | bytes 524320 | tf_op jit(solution)/shard_map/u7/ppermute | solution.py:71
  112.6 1.5 %collective-permute-done.28.refs_9_ = bf16[4,512,128]{2,1,0:T(8,128)(2,1)S(1)} collective-permute-done((bf16[4,512,128]{2,1,0:T(8,128)(2,1)S(1)}, bf16[4,512,128]{2,1,0:T(8,128)(2,1)S(1)}, u32[]{:S(2)}, u32[]{:S(2)}) %collective-permute-start.28) | collective-permute-done | bytes 524320 | tf_op jit(solution)/shard_map/v7/ppermute | solution.py:71
  114.1 2.1 %terms.6.refs_2_ = f32[512,512]{1,0:T(8,128)S(1)} custom-call(bf16[16896,256]{1,0:T(8,128)(2,1)S(1)} %get-tuple-element.90.refs_0_, bf16[16896,256]{1,0:T(8,128)(2,1)S(1)} %spread.3.refs_1_, f32[512,512]{1,0:T(8,128)S(1)} %terms.5.refs_2_, bf16[4,512,128]{2,1,0:T(8,128)(2,1)S(1)} %get-tuple-element.111.refs_3_, ...), custom_call_target="tpu_custom_call" | custom-call | tf_op jit(solution)/shard_map/terms/pallas_call | solution.py:190
  116.2 2.1 %collective-permute-done.30.refs_4_ = bf16[4,512,128]{2,1,0:T(8,128)(2,1)S(1)} collective-permute-done((bf16[4,512,128]{2,1,0:T(8,128)(2,1)S(1)}, bf16[4,512,128]{2,1,0:T(8,128)(2,1)S(1)}, u32[]{:S(2)}, u32[]{:S(2)}) %collective-permute-start.30) | collective-permute-done | bytes 524320 | tf_op jit(solution)/shard_map/v6/ppermute | solution.py:71
  118.2 1.5 %collective-permute-done.29.refs_3_ = bf16[4,512,128]{2,1,0:T(8,128)(2,1)S(1)} collective-permute-done((bf16[4,512,128]{2,1,0:T(8,128)(2,1)S(1)}, bf16[4,512,128]{2,1,0:T(8,128)(2,1)S(1)}, u32[]{:S(2)}, u32[]{:S(2)}) %collective-permute-start.29) | collective-permute-done | bytes 524320 | tf_op jit(solution)/shard_map/q7/ppermute | solution.py:71
  (134 shorter events, 13.7 us)
Async XLA Ops:
  6.5 77.0 %all-gather.2.cloned.1.call-start = ((), (), s32[]{:S(2)}) async-start(), calls=%async_computation | async-start | bytes 14192640 | tf_op jit(solution)/shard_map/loads/all_gather | solution.py:207
  11.0 13.8 %collective-permute-start = (bf16[4,512,128]{2,1,0:T(8,128)(2,1)S(1)}, bf16[4,512,128]{2,1,0:T(8,128)(2,1)S(1)}, u32[]{:S(2)}, u32[]{:S(2)}) collective-permute-start(bf16[4,512,128]{2,1,0:T(8,128)(2,1)S(1)} %bitcast.4), channel_id=1, source_target_pairs={{0,1},{1,2},{2,3},{3,4},{4,5},{5,6},{6,7},{7,0},{8,9},{9,10},{10,1... | collective-permute-start | bytes 1572872 | tf_op jit(solution)/shard_map/s1/ppermute | solution.py:71
  14.2 18.6 %collective-permute-start.1 = (bf16[4,512,128]{2,1,0:T(8,128)(2,1)S(1)}, bf16[4,512,128]{2,1,0:T(8,128)(2,1)S(1)}, u32[]{:S(2)}, u32[]{:S(2)}) collective-permute-start(bf16[4,512,128]{2,1,0:T(8,128)(2,1)S(1)} %bitcast.5), channel_id=1, source_target_pairs={{0,8},{1,9},{2,10},{3,11},{4,12},{5,13},{6,14},{7,15},{8,0},{9,1},... | collective-permute-start | bytes 1572872 | tf_op jit(solution)/shard_map/q0/ppermute | solution.py:71
  15.7 17.2 %collective-permute-start.2 = (bf16[4,512,128]{2,1,0:T(8,128)(2,1)S(1)}, bf16[4,512,128]{2,1,0:T(8,128)(2,1)S(1)}, u32[]{:S(2)}, u32[]{:S(2)}) collective-permute-start(bf16[4,512,128]{2,1,0:T(8,128)(2,1)S(1)} %bitcast.6), channel_id=1, source_target_pairs={{0,24},{1,25},{2,26},{3,27},{4,28},{5,29},{6,30},{7,31},{8,16},{9,... | collective-permute-start | bytes 1572872 | tf_op jit(solution)/shard_map/u0/ppermute | solution.py:71
  17.9 15.1 %collective-permute-start.3 = (bf16[4,512,128]{2,1,0:T(8,128)(2,1)S(1)}, bf16[4,512,128]{2,1,0:T(8,128)(2,1)S(1)}, u32[]{:S(2)}, u32[]{:S(2)}) collective-permute-start(bf16[4,512,128]{2,1,0:T(8,128)(2,1)S(1)} %bitcast.7), channel_id=1, source_target_pairs={{0,7},{1,0},{2,1},{3,2},{4,3},{5,4},{6,5},{7,6},{8,15},{9,8},{10,9... | collective-permute-start | bytes 1572872 | tf_op jit(solution)/shard_map/s7/ppermute | solution.py:71
  24.7 10.4 %collective-permute-start.4 = (bf16[4,512,128]{2,1,0:T(8,128)(2,1)S(1)}, bf16[4,512,128]{2,1,0:T(8,128)(2,1)S(1)}, u32[]{:S(2)}, u32[]{:S(2)}) collective-permute-start(bf16[4,512,128]{2,1,0:T(8,128)(2,1)S(1)} %get-tuple-element.65.refs_6_), channel_id=1, source_target_pairs={{0,1},{1,2},{2,3},{3,4},{4,5},{5,6},{6,7},{7,0},{8,9},{9,10},{10,1... | collective-permute-start | bytes 1572872 | tf_op jit(solution)/shard_map/s2/ppermute | solution.py:71
  28.4 14.8 %collective-permute-start.5 = (bf16[4,512,128]{2,1,0:T(8,128)(2,1)S(1)}, bf16[4,512,128]{2,1,0:T(8,128)(2,1)S(1)}, u32[]{:S(2)}, u32[]{:S(2)}) collective-permute-start(bf16[4,512,128]{2,1,0:T(8,128)(2,1)S(1)} %get-tuple-element.65.refs_6_), channel_id=1, source_target_pairs={{0,24},{1,25},{2,26},{3,27},{4,28},{5,29},{6,30},{7,31},{8,16},{9,... | collective-permute-start | bytes 1572872 | tf_op jit(solution)/shard_map/u1/ppermute | solution.py:71
  32.8 10.4 %collective-permute-start.6 = (bf16[4,512,128]{2,1,0:T(8,128)(2,1)S(1)}, bf16[4,512,128]{2,1,0:T(8,128)(2,1)S(1)}, u32[]{:S(2)}, u32[]{:S(2)}) collective-permute-start(bf16[4,512,128]{2,1,0:T(8,128)(2,1)S(1)} %get-tuple-element.68.refs_3_.refs_6_), channel_id=1, source_target_pairs={{0,1},{1,2},{2,3},{3,4},{4,5},{5,6},{6,7},{7,0},{8,9},{9,10},{10,1... | collective-permute-start | bytes 1572872 | tf_op jit(solution)/shard_map/q1/ppermute | solution.py:71
  32.9 15.9 %collective-permute-start.7 = (bf16[4,512,128]{2,1,0:T(8,128)(2,1)S(1)}, bf16[4,512,128]{2,1,0:T(8,128)(2,1)S(1)}, u32[]{:S(2)}, u32[]{:S(2)}) collective-permute-start(bf16[4,512,128]{2,1,0:T(8,128)(2,1)S(1)} %get-tuple-element.68.refs_3_.refs_6_), channel_id=1, source_target_pairs={{0,24},{1,25},{2,26},{3,27},{4,28},{5,29},{6,30},{7,31},{8,16},{9,... | collective-permute-start | bytes 1572872 | tf_op jit(solution)/shard_map/v0/ppermute | solution.py:71
  35.1 13.7 %collective-permute-start.8 = (bf16[4,512,128]{2,1,0:T(8,128)(2,1)S(1)}, bf16[4,512,128]{2,1,0:T(8,128)(2,1)S(1)}, u32[]{:S(2)}, u32[]{:S(2)}) collective-permute-start(bf16[4,512,128]{2,1,0:T(8,128)(2,1)S(1)} %get-tuple-element.71.refs_10_), channel_id=1, source_target_pairs={{0,1},{1,2},{2,3},{3,4},{4,5},{5,6},{6,7},{7,0},{8,9},{9,10},{10,1... | collective-permute-start | bytes 1572872 | tf_op jit(solution)/shard_map/s3/ppermute | solution.py:71
  38.8 15.6 %collective-permute-start.9 = (bf16[4,512,128]{2,1,0:T(8,128)(2,1)S(1)}, bf16[4,512,128]{2,1,0:T(8,128)(2,1)S(1)}, u32[]{:S(2)}, u32[]{:S(2)}) collective-permute-start(bf16[4,512,128]{2,1,0:T(8,128)(2,1)S(1)} %get-tuple-element.71.refs_10_), channel_id=1, source_target_pairs={{0,24},{1,25},{2,26},{3,27},{4,28},{5,29},{6,30},{7,31},{8,16},{9,... | collective-permute-start | bytes 1572872 | tf_op jit(solution)/shard_map/u2/ppermute | solution.py:71
  43.2 11.2 %collective-permute-start.10 = (bf16[4,512,128]{2,1,0:T(8,128)(2,1)S(1)}, bf16[4,512,128]{2,1,0:T(8,128)(2,1)S(1)}, u32[]{:S(2)}, u32[]{:S(2)}) collective-permute-start(bf16[4,512,128]{2,1,0:T(8,128)(2,1)S(1)} %get-tuple-element.74.refs_7_), channel_id=1, source_target_pairs={{0,1},{1,2},{2,3},{3,4},{4,5},{5,6},{6,7},{7,0},{8,9},{9,10},{10,1... | collective-permute-start | bytes 1572872 | tf_op jit(solution)/shard_map/q2/ppermute | solution.py:71
  44.4 15.6 %collective-permute-start.11 = (bf16[4,512,128]{2,1,0:T(8,128)(2,1)S(1)}, bf16[4,512,128]{2,1,0:T(8,128)(2,1)S(1)}, u32[]{:S(2)}, u32[]{:S(2)}) collective-permute-start(bf16[4,512,128]{2,1,0:T(8,128)(2,1)S(1)} %get-tuple-element.74.refs_7_), channel_id=1, source_target_pairs={{0,24},{1,25},{2,26},{3,27},{4,28},{5,29},{6,30},{7,31},{8,16},{9,... | collective-permute-start | bytes 1572872 | tf_op jit(solution)/shard_map/v1/ppermute | solution.py:71
  48.8 11.2 %collective-permute-start.12 = (bf16[4,512,128]{2,1,0:T(8,128)(2,1)S(1)}, bf16[4,512,128]{2,1,0:T(8,128)(2,1)S(1)}, u32[]{:S(2)}, u32[]{:S(2)}) collective-permute-start(bf16[4,512,128]{2,1,0:T(8,128)(2,1)S(1)} %get-tuple-element.77.refs_3_), channel_id=1, source_target_pairs={{0,1},{1,2},{2,3},{3,4},{4,5},{5,6},{6,7},{7,0},{8,9},{9,10},{10,1... | collective-permute-start | bytes 1572872 | tf_op jit(solution)/shard_map/s4/ppermute | solution.py:71
  50.0 15.6 %collective-permute-start.13 = (bf16[4,512,128]{2,1,0:T(8,128)(2,1)S(1)}, bf16[4,512,128]{2,1,0:T(8,128)(2,1)S(1)}, u32[]{:S(2)}, u32[]{:S(2)}) collective-permute-start(bf16[4,512,128]{2,1,0:T(8,128)(2,1)S(1)} %get-tuple-element.77.refs_3_), channel_id=1, source_target_pairs={{0,24},{1,25},{2,26},{3,27},{4,28},{5,29},{6,30},{7,31},{8,16},{9,... | collective-permute-start | bytes 1572872 | tf_op jit(solution)/shard_map/u3/ppermute | solution.py:71
  54.5 11.2 %collective-permute-start.14 = (bf16[4,512,128]{2,1,0:T(8,128)(2,1)S(1)}, bf16[4,512,128]{2,1,0:T(8,128)(2,1)S(1)}, u32[]{:S(2)}, u32[]{:S(2)}) collective-permute-start(bf16[4,512,128]{2,1,0:T(8,128)(2,1)S(1)} %get-tuple-element.80.refs_11_), channel_id=1, source_target_pairs={{0,1},{1,2},{2,3},{3,4},{4,5},{5,6},{6,7},{7,0},{8,9},{9,10},{10,1... | collective-permute-start | bytes 1572872 | tf_op jit(solution)/shard_map/q3/ppermute | solution.py:71
  55.7 15.6 %collective-permute-start.15 = (bf16[4,512,128]{2,1,0:T(8,128)(2,1)S(1)}, bf16[4,512,128]{2,1,0:T(8,128)(2,1)S(1)}, u32[]{:S(2)}, u32[]{:S(2)}) collective-permute-start(bf16[4,512,128]{2,1,0:T(8,128)(2,1)S(1)} %get-tuple-element.80.refs_11_), channel_id=1, source_target_pairs={{0,24},{1,25},{2,26},{3,27},{4,28},{5,29},{6,30},{7,31},{8,16},{9,... | collective-permute-start | bytes 1572872 | tf_op jit(solution)/shard_map/v2/ppermute | solution.py:71
  60.1 11.2 %collective-permute-start.16 = (bf16[4,512,128]{2,1,0:T(8,128)(2,1)S(1)}, bf16[4,512,128]{2,1,0:T(8,128)(2,1)}, u32[]{:S(2)}, u32[]{:S(2)}) collective-permute-start(bf16[4,512,128]{2,1,0:T(8,128)(2,1)S(1)} %get-tuple-element.83.refs_7_), channel_id=1, source_target_pairs={{0,1},{1,2},{2,3},{3,4},{4,5},{5,6},{6,7},{7,0},{8,9},{9,10},{10,1... | collective-permute-start | bytes 1572872 | tf_op jit(solution)/shard_map/s5/ppermute | solution.py:71
  61.3 15.7 %collective-permute-start.17 = (bf16[4,512,128]{2,1,0:T(8,128)(2,1)S(1)}, bf16[4,512,128]{2,1,0:T(8,128)(2,1)S(1)}, u32[]{:S(2)}, u32[]{:S(2)}) collective-permute-start(bf16[4,512,128]{2,1,0:T(8,128)(2,1)S(1)} %get-tuple-element.83.refs_7_), channel_id=1, source_target_pairs={{0,24},{1,25},{2,26},{3,27},{4,28},{5,29},{6,30},{7,31},{8,16},{9,... | collective-permute-start | bytes 1572872 | tf_op jit(solution)/shard_map/u4/ppermute | solution.py:71
  65.7 11.3 %collective-permute-start.18 = (bf16[4,512,128]{2,1,0:T(8,128)(2,1)S(1)}, bf16[4,512,128]{2,1,0:T(8,128)(2,1)}, u32[]{:S(2)}, u32[]{:S(2)}) collective-permute-start(bf16[4,512,128]{2,1,0:T(8,128)(2,1)S(1)} %get-tuple-element.86.refs_4_), channel_id=1, source_target_pairs={{0,1},{1,2},{2,3},{3,4},{4,5},{5,6},{6,7},{7,0},{8,9},{9,10},{10,1... | collective-permute-start | bytes 1572872 | tf_op jit(solution)/shard_map/q4/ppermute | solution.py:71
  66.9 15.7 %collective-permute-start.19 = (bf16[4,512,128]{2,1,0:T(8,128)(2,1)S(1)}, bf16[4,512,128]{2,1,0:T(8,128)(2,1)S(1)}, u32[]{:S(2)}, u32[]{:S(2)}) collective-permute-start(bf16[4,512,128]{2,1,0:T(8,128)(2,1)S(1)} %get-tuple-element.86.refs_4_), channel_id=1, source_target_pairs={{0,24},{1,25},{2,26},{3,27},{4,28},{5,29},{6,30},{7,31},{8,16},{9,... | collective-permute-start | bytes 1572872 | tf_op jit(solution)/shard_map/v3/ppermute | solution.py:71
  71.3 16.8 %collective-permute-start.20 = (bf16[4,512,128]{2,1,0:T(8,128)(2,1)}, bf16[4,512,128]{2,1,0:T(8,128)(2,1)S(1)}, u32[]{:S(2)}, u32[]{:S(2)}) collective-permute-start(bf16[4,512,128]{2,1,0:T(8,128)(2,1)} %get-tuple-element.89.refs_11_), channel_id=1, source_target_pairs={{0,1},{1,2},{2,3},{3,4},{4,5},{5,6},{6,7},{7,0},{8,9},{9,10},{10,1... | collective-permute-start | bytes 1572872 | tf_op jit(solution)/shard_map/s6/ppermute | solution.py:71
  72.6 16.7 %collective-permute-start.21 = (bf16[4,512,128]{2,1,0:T(8,128)(2,1)}, bf16[4,512,128]{2,1,0:T(8,128)(2,1)S(1)}, u32[]{:S(2)}, u32[]{:S(2)}) collective-permute-start(bf16[4,512,128]{2,1,0:T(8,128)(2,1)} %get-tuple-element.89.refs_11_), channel_id=1, source_target_pairs={{0,24},{1,25},{2,26},{3,27},{4,28},{5,29},{6,30},{7,31},{8,16},{9,... | collective-permute-start | bytes 1572872 | tf_op jit(solution)/shard_map/u5/ppermute | solution.py:71
  77.0 12.3 %collective-permute-start.22 = (bf16[4,512,128]{2,1,0:T(8,128)(2,1)}, bf16[4,512,128]{2,1,0:T(8,128)(2,1)}, u32[]{:S(2)}, u32[]{:S(2)}) collective-permute-start(bf16[4,512,128]{2,1,0:T(8,128)(2,1)} %get-tuple-element.93.refs_8_), channel_id=1, source_target_pairs={{0,1},{1,2},{2,3},{3,4},{4,5},{5,6},{6,7},{7,0},{8,9},{9,10},{10,1... | collective-permute-start | bytes 1572872 | tf_op jit(solution)/shard_map/q5/ppermute | solution.py:71
  78.2 23.9 %collective-permute-start.23 = (bf16[4,512,128]{2,1,0:T(8,128)(2,1)}, bf16[4,512,128]{2,1,0:T(8,128)(2,1)}, u32[]{:S(2)}, u32[]{:S(2)}) collective-permute-start(bf16[4,512,128]{2,1,0:T(8,128)(2,1)} %get-tuple-element.93.refs_8_), channel_id=1, source_target_pairs={{0,24},{1,25},{2,26},{3,27},{4,28},{5,29},{6,30},{7,31},{8,16},{9,... | collective-permute-start | bytes 1572872 | tf_op jit(solution)/shard_map/v4/ppermute | solution.py:71
  88.1 14.0 %collective-permute-start.24 = (bf16[4,512,128]{2,1,0:T(8,128)(2,1)S(1)}, bf16[4,512,128]{2,1,0:T(8,128)(2,1)S(1)}, u32[]{:S(2)}, u32[]{:S(2)}) collective-permute-start(bf16[4,512,128]{2,1,0:T(8,128)(2,1)S(1)} %get-tuple-element.95.refs_4_), channel_id=1, source_target_pairs={{0,24},{1,25},{2,26},{3,27},{4,28},{5,29},{6,30},{7,31},{8,16},{9,... | collective-permute-start | bytes 1572872 | tf_op jit(solution)/shard_map/u6/ppermute | solution.py:71
  89.4 14.3 %collective-permute-start.25 = (bf16[4,512,128]{2,1,0:T(8,128)(2,1)}, bf16[4,512,128]{2,1,0:T(8,128)(2,1)S(1)}, u32[]{:S(2)}, u32[]{:S(2)}) collective-permute-start(bf16[4,512,128]{2,1,0:T(8,128)(2,1)} %get-tuple-element.108.refs_12_), channel_id=1, source_target_pairs={{0,1},{1,2},{2,3},{3,4},{4,5},{5,6},{6,7},{7,0},{8,9},{9,10},{10,1... | collective-permute-start | bytes 1572872 | tf_op jit(solution)/shard_map/q6/ppermute | solution.py:71
  92.2 12.0 %collective-permute-start.26 = (bf16[4,512,128]{2,1,0:T(8,128)(2,1)}, bf16[4,512,128]{2,1,0:T(8,128)(2,1)S(1)}, u32[]{:S(2)}, u32[]{:S(2)}) collective-permute-start(bf16[4,512,128]{2,1,0:T(8,128)(2,1)} %get-tuple-element.108.refs_12_), channel_id=1, source_target_pairs={{0,24},{1,25},{2,26},{3,27},{4,28},{5,29},{6,30},{7,31},{8,16},{9,... | collective-permute-start | bytes 1572872 | tf_op jit(solution)/shard_map/v5/ppermute | solution.py:71
  102.2 10.5 %collective-permute-start.27 = (bf16[4,512,128]{2,1,0:T(8,128)(2,1)S(1)}, bf16[4,512,128]{2,1,0:T(8,128)(2,1)S(1)}, u32[]{:S(2)}, u32[]{:S(2)}) collective-permute-start(bf16[4,512,128]{2,1,0:T(8,128)(2,1)S(1)} %get-tuple-element.114.refs_7_), channel_id=1, source_target_pairs={{0,24},{1,25},{2,26},{3,27},{4,28},{5,29},{6,30},{7,31},{8,16},{9,... | collective-permute-start | bytes 1572872 | tf_op jit(solution)/shard_map/u7/ppermute | solution.py:71
  103.7 10.4 %collective-permute-start.28 = (bf16[4,512,128]{2,1,0:T(8,128)(2,1)S(1)}, bf16[4,512,128]{2,1,0:T(8,128)(2,1)S(1)}, u32[]{:S(2)}, u32[]{:S(2)}) collective-permute-start(bf16[4,512,128]{2,1,0:T(8,128)(2,1)S(1)} %get-tuple-element.115), channel_id=1, source_target_pairs={{0,7},{1,0},{2,1},{3,2},{4,3},{5,4},{6,5},{7,6},{8,15},{9,8},{10,9... | collective-permute-start | bytes 1572872 | tf_op jit(solution)/shard_map/v7/ppermute | solution.py:71
  104.2 14.0 %collective-permute-start.30 = (bf16[4,512,128]{2,1,0:T(8,128)(2,1)S(1)}, bf16[4,512,128]{2,1,0:T(8,128)(2,1)S(1)}, u32[]{:S(2)}, u32[]{:S(2)}) collective-permute-start(bf16[4,512,128]{2,1,0:T(8,128)(2,1)S(1)} %get-tuple-element.112.refs_5_), channel_id=1, source_target_pairs={{0,24},{1,25},{2,26},{3,27},{4,28},{5,29},{6,30},{7,31},{8,16},{9,... | collective-permute-start | bytes 1572872 | tf_op jit(solution)/shard_map/v6/ppermute | solution.py:71
  105.6 14.2 %collective-permute-start.29 = (bf16[4,512,128]{2,1,0:T(8,128)(2,1)S(1)}, bf16[4,512,128]{2,1,0:T(8,128)(2,1)S(1)}, u32[]{:S(2)}, u32[]{:S(2)}) collective-permute-start(bf16[4,512,128]{2,1,0:T(8,128)(2,1)S(1)} %get-tuple-element.116), channel_id=1, source_target_pairs={{0,7},{1,0},{2,1},{3,2},{4,3},{5,4},{6,5},{7,6},{8,15},{9,8},{10,9... | collective-permute-start | bytes 1572872 | tf_op jit(solution)/shard_map/q7/ppermute | solution.py:71
  (33 other events, 547.3 us)
Sparse Core Ops, SparseCore 0:
  10.0 71.8 all-gather.1

commit v4 on v3

--- a/solution.py
+++ b/solution.py
@@ -71,14 +71,22 @@
         return lax.ppermute(v, AXES, pairs)
 
 
-def load_kernel(blocks, kets, out, codes, sems):
-    body = pltpu.make_async_copy(blocks, out.at[pl.ds(0, BODY), :], sems.at[0])
-    body.start()
+def load_kernel(blocks, kets, out, codes, held, sems):
+    part = BODY // 4
+    spans = [pl.ds(i * part, part) for i in range(4)]
+    reads = [pltpu.make_async_copy(blocks.at[d, :], held.at[d, :], sems.at[2 + i]) for i, d in enumerate(spans)]
+    writes = [pltpu.make_async_copy(held.at[d, :], out.at[d, :], sems.at[6 + i]) for i, d in enumerate(spans)]
+    for move in reads:
+        move.start()
+    for read, write in zip(reads, writes):
+        read.wait()
+        write.start()
     codes[...] = jnp.zeros(codes.shape, codes.dtype)
     codes[0:TILES, 0:SLOTS] = kets[...].astype(jnp.float32)
     half = codes[...].astype(jnp.bfloat16)
     pl.run_scoped(functools.partial(put_codes, half, out, sems), pltpu.VMEM((16, WIDTH), jnp.bfloat16))
-    body.wait()
+    for move in writes:
+        move.wait()
 
 
 def put_codes(half, out, sems, narrow):
@@ -92,13 +100,17 @@
     return pl.pallas_call(
         load_kernel,
         out_shape=pltpu.HBM((BODY + 16, WIDTH), jnp.bfloat16),
-        in_specs=[VMEM, VMEM],
+        in_specs=[pl.BlockSpec(memory_space=pltpu.HBM), VMEM],
         out_specs=pl.BlockSpec(memory_space=pltpu.HBM),
-        scratch_shapes=[pltpu.VMEM((16, WIDTH), jnp.float32), pltpu.SemaphoreType.DMA((2,))],
-        compiler_params=pltpu.CompilerParams(vmem_limit_bytes=1 << 20),
+        scratch_shapes=[
+            pltpu.VMEM((16, WIDTH), jnp.float32),
+            pltpu.VMEM((BODY, WIDTH), jnp.bfloat16),
+            pltpu.SemaphoreType.DMA((10,)),
+        ],
+        compiler_params=pltpu.CompilerParams(vmem_limit_bytes=4 << 20),
         cost_estimate=pl.CostEstimate(flops=0, bytes_accessed=0, transcendentals=0),
         name="load",
-    )(near(blocks.reshape(BODY, WIDTH)), kets)
+    )(pltpu.with_memory_space_constraint(blocks.reshape(BODY, WIDTH), pltpu.HBM), kets)
 
 
 def spread_kernel(tiles, counts, loads, dense, held, codes, listed, kets, sems):

time: 128 us -> 128 us (level)
  local copies, waits for them, and re-layouts: 5.07 us -> 3.65 us
    unnamed x67 -> x65, local copies, waits for them, and re-layouts: 4.15 us -> 2.73 us
where the time goes in v4:
time: 128 us
  starting transfers between devices  71.4 us (56%)
  Pallas kernels  22.2 us (17%)
  waiting for transfers between devices  16.6 us (13%)
  between operations  14 us (11%)
  local copies, waits for them, and re-layouts  3.65 us (3%)
    ppermute x31, starting transfers between devices, send(): return lax.ppermute(v, AXES, pairs)  71.4 us
    ppermute x31, waiting for transfers between devices, send(): return lax.ppermute(v, AXES, pairs)  16.6 us
    pallas_call x4, Pallas kernels, add_terms(): pl.pallas_call(functools.partial(terms_kernel, [q for _, q in pieces], fr...  10.8 us
    pallas_call x2, Pallas kernels, spread(): pl.pallas_call(functools.partial(spread_kernel, tiles), out_shape=pltpu.V...  9.15 us
    unnamed x65, local copies, waits for them, and re-layouts  2.73 us
  transfers between devices with their start and end apart: 32, of which 7 were waited for; matrix products, arithmetic and copies ran while one was open for 1% of the time, Pallas kernels for 15%

profile of v4, /device:TPU:96, one launch (start us, length us, event | category | flops | bytes accessed | tf_op | source)
XLA Modules:
  0.0 127.9 jit_solution(13274184276695603682)
XLA Ops:
  7.2 2.2 %load.1 = bf16[6160,128]{1,0:T(8,128)(2,1)} custom-call(bf16[6144,128]{1,0:T(8,128)(2,1)} %bitcast.9, s32[4,12]{1,0:T(4,128)S(1)} %copy-done.31), custom_call_target="tpu_custom_call" | custom-call | tf_op jit(solution)/shard_map/load/pallas_call | solution.py:100
  10.6 3.2 %collective-permute-start = (bf16[4,512,128]{2,1,0:T(8,128)(2,1)S(1)}, bf16[4,512,128]{2,1,0:T(8,128)(2,1)S(1)}, u32[]{:S(2)}, u32[]{:S(2)}) collective-permute-start(bf16[4,512,128]{2,1,0:T(8,128)(2,1)S(1)} %bitcast.4), channel_id=1, source_target_pairs={{0,1},{1,2},{2,3},{3,4},{4,5},{5,6},{6,7},{7,0},{8,9},{9,10},{10,1... | collective-permute-start | bytes 1572872 | tf_op jit(solution)/shard_map/s1/ppermute | solution.py:71
  13.8 1.6 %collective-permute-start.1 = (bf16[4,512,128]{2,1,0:T(8,128)(2,1)S(1)}, bf16[4,512,128]{2,1,0:T(8,128)(2,1)S(1)}, u32[]{:S(2)}, u32[]{:S(2)}) collective-permute-start(bf16[4,512,128]{2,1,0:T(8,128)(2,1)S(1)} %bitcast.5), channel_id=1, source_target_pairs={{0,8},{1,9},{2,10},{3,11},{4,12},{5,13},{6,14},{7,15},{8,0},{9,1},... | collective-permute-start | bytes 1572872 | tf_op jit(solution)/shard_map/q0/ppermute | solution.py:71
  15.4 2.2 %collective-permute-start.2 = (bf16[4,512,128]{2,1,0:T(8,128)(2,1)S(1)}, bf16[4,512,128]{2,1,0:T(8,128)(2,1)S(1)}, u32[]{:S(2)}, u32[]{:S(2)}) collective-permute-start(bf16[4,512,128]{2,1,0:T(8,128)(2,1)S(1)} %bitcast.6), channel_id=1, source_target_pairs={{0,24},{1,25},{2,26},{3,27},{4,28},{5,29},{6,30},{7,31},{8,16},{9,... | collective-permute-start | bytes 1572872 | tf_op jit(solution)/shard_map/u0/ppermute | solution.py:71
  17.6 6.8 %collective-permute-done.refs_1_ = bf16[4,512,128]{2,1,0:T(8,128)(2,1)S(1)} collective-permute-done((bf16[4,512,128]{2,1,0:T(8,128)(2,1)S(1)}, bf16[4,512,128]{2,1,0:T(8,128)(2,1)S(1)}, u32[]{:S(2)}, u32[]{:S(2)}) %collective-permute-start) | collective-permute-done | bytes 524320 | tf_op jit(solution)/shard_map/s1/ppermute | solution.py:71
  24.4 3.7 %collective-permute-start.4 = (bf16[4,512,128]{2,1,0:T(8,128)(2,1)S(1)}, bf16[4,512,128]{2,1,0:T(8,128)(2,1)S(1)}, u32[]{:S(2)}, u32[]{:S(2)}) collective-permute-start(bf16[4,512,128]{2,1,0:T(8,128)(2,1)S(1)} %get-tuple-element.65.refs_6_), channel_id=1, source_target_pairs={{0,1},{1,2},{2,3},{3,4},{4,5},{5,6},{6,7},{7,0},{8,9},{9,10},{10,1... | collective-permute-start | bytes 1572872 | tf_op jit(solution)/shard_map/s2/ppermute | solution.py:71
  28.1 4.4 %collective-permute-start.5 = (bf16[4,512,128]{2,1,0:T(8,128)(2,1)S(1)}, bf16[4,512,128]{2,1,0:T(8,128)(2,1)S(1)}, u32[]{:S(2)}, u32[]{:S(2)}) collective-permute-start(bf16[4,512,128]{2,1,0:T(8,128)(2,1)S(1)} %get-tuple-element.65.refs_6_), channel_id=1, source_target_pairs={{0,24},{1,25},{2,26},{3,27},{4,28},{5,29},{6,30},{7,31},{8,16},{9,... | collective-permute-start | bytes 1572872 | tf_op jit(solution)/shard_map/u1/ppermute | solution.py:71
  32.7 2.1 %collective-permute-done.4.refs_1_ = bf16[4,512,128]{2,1,0:T(8,128)(2,1)S(1)} collective-permute-done((bf16[4,512,128]{2,1,0:T(8,128)(2,1)S(1)}, bf16[4,512,128]{2,1,0:T(8,128)(2,1)S(1)}, u32[]{:S(2)}, u32[]{:S(2)}) %collective-permute-start.4) | collective-permute-done | bytes 524320 | tf_op jit(solution)/shard_map/s2/ppermute | solution.py:71
  34.8 3.7 %collective-permute-start.8 = (bf16[4,512,128]{2,1,0:T(8,128)(2,1)S(1)}, bf16[4,512,128]{2,1,0:T(8,128)(2,1)S(1)}, u32[]{:S(2)}, u32[]{:S(2)}) collective-permute-start(bf16[4,512,128]{2,1,0:T(8,128)(2,1)S(1)} %get-tuple-element.71.refs_10_), channel_id=1, source_target_pairs={{0,1},{1,2},{2,3},{3,4},{4,5},{5,6},{6,7},{7,0},{8,9},{9,10},{10,1... | collective-permute-start | bytes 1572872 | tf_op jit(solution)/shard_map/s3/ppermute | solution.py:71
  38.4 4.4 %collective-permute-start.9 = (bf16[4,512,128]{2,1,0:T(8,128)(2,1)S(1)}, bf16[4,512,128]{2,1,0:T(8,128)(2,1)S(1)}, u32[]{:S(2)}, u32[]{:S(2)}) collective-permute-start(bf16[4,512,128]{2,1,0:T(8,128)(2,1)S(1)} %get-tuple-element.71.refs_10_), channel_id=1, source_target_pairs={{0,24},{1,25},{2,26},{3,27},{4,28},{5,29},{6,30},{7,31},{8,16},{9,... | collective-permute-start | bytes 1572872 | tf_op jit(solution)/shard_map/u2/ppermute | solution.py:71
  44.1 4.4 %collective-permute-start.11 = (bf16[4,512,128]{2,1,0:T(8,128)(2,1)S(1)}, bf16[4,512,128]{2,1,0:T(8,128)(2,1)S(1)}, u32[]{:S(2)}, u32[]{:S(2)}) collective-permute-start(bf16[4,512,128]{2,1,0:T(8,128)(2,1)S(1)} %get-tuple-element.74.refs_7_), channel_id=1, source_target_pairs={{0,24},{1,25},{2,26},{3,27},{4,28},{5,29},{6,30},{7,31},{8,16},{9,... | collective-permute-start | bytes 1572872 | tf_op jit(solution)/shard_map/v1/ppermute | solution.py:71
  48.5 1.2 collective-permute-start.12
  49.7 4.4 %collective-permute-start.13 = (bf16[4,512,128]{2,1,0:T(8,128)(2,1)S(1)}, bf16[4,512,128]{2,1,0:T(8,128)(2,1)S(1)}, u32[]{:S(2)}, u32[]{:S(2)}) collective-permute-start(bf16[4,512,128]{2,1,0:T(8,128)(2,1)S(1)} %get-tuple-element.77.refs_3_), channel_id=1, source_target_pairs={{0,24},{1,25},{2,26},{3,27},{4,28},{5,29},{6,30},{7,31},{8,16},{9,... | collective-permute-start | bytes 1572872 | tf_op jit(solution)/shard_map/u3/ppermute | solution.py:71
  55.3 4.4 %collective-permute-start.15 = (bf16[4,512,128]{2,1,0:T(8,128)(2,1)S(1)}, bf16[4,512,128]{2,1,0:T(8,128)(2,1)S(1)}, u32[]{:S(2)}, u32[]{:S(2)}) collective-permute-start(bf16[4,512,128]{2,1,0:T(8,128)(2,1)S(1)} %get-tuple-element.80.refs_11_), channel_id=1, source_target_pairs={{0,24},{1,25},{2,26},{3,27},{4,28},{5,29},{6,30},{7,31},{8,16},{9,... | collective-permute-start | bytes 1572872 | tf_op jit(solution)/shard_map/v2/ppermute | solution.py:71
  60.9 4.4 %collective-permute-start.17 = (bf16[4,512,128]{2,1,0:T(8,128)(2,1)S(1)}, bf16[4,512,128]{2,1,0:T(8,128)(2,1)S(1)}, u32[]{:S(2)}, u32[]{:S(2)}) collective-permute-start(bf16[4,512,128]{2,1,0:T(8,128)(2,1)S(1)} %get-tuple-element.83.refs_7_), channel_id=1, source_target_pairs={{0,24},{1,25},{2,26},{3,27},{4,28},{5,29},{6,30},{7,31},{8,16},{9,... | collective-permute-start | bytes 1572872 | tf_op jit(solution)/shard_map/u4/ppermute | solution.py:71
  66.5 4.4 %collective-permute-start.19 = (bf16[4,512,128]{2,1,0:T(8,128)(2,1)S(1)}, bf16[4,512,128]{2,1,0:T(8,128)(2,1)S(1)}, u32[]{:S(2)}, u32[]{:S(2)}) collective-permute-start(bf16[4,512,128]{2,1,0:T(8,128)(2,1)S(1)} %get-tuple-element.86.refs_4_), channel_id=1, source_target_pairs={{0,24},{1,25},{2,26},{3,27},{4,28},{5,29},{6,30},{7,31},{8,16},{9,... | collective-permute-start | bytes 1572872 | tf_op jit(solution)/shard_map/v3/ppermute | solution.py:71
  71.0 1.3 %collective-permute-start.20 = (bf16[4,512,128]{2,1,0:T(8,128)(2,1)}, bf16[4,512,128]{2,1,0:T(8,128)(2,1)S(1)}, u32[]{:S(2)}, u32[]{:S(2)}) collective-permute-start(bf16[4,512,128]{2,1,0:T(8,128)(2,1)} %get-tuple-element.89.refs_11_), channel_id=1, source_target_pairs={{0,1},{1,2},{2,3},{3,4},{4,5},{5,6},{6,7},{7,0},{8,9},{9,10},{10,1... | collective-permute-start | bytes 1572872 | tf_op jit(solution)/shard_map/s6/ppermute | solution.py:71
  72.3 4.4 %collective-permute-start.21 = (bf16[4,512,128]{2,1,0:T(8,128)(2,1)}, bf16[4,512,128]{2,1,0:T(8,128)(2,1)S(1)}, u32[]{:S(2)}, u32[]{:S(2)}) collective-permute-start(bf16[4,512,128]{2,1,0:T(8,128)(2,1)} %get-tuple-element.89.refs_11_), channel_id=1, source_target_pairs={{0,24},{1,25},{2,26},{3,27},{4,28},{5,29},{6,30},{7,31},{8,16},{9,... | collective-permute-start | bytes 1572872 | tf_op jit(solution)/shard_map/u5/ppermute | solution.py:71
  77.9 4.4 %collective-permute-start.23 = (bf16[4,512,128]{2,1,0:T(8,128)(2,1)}, bf16[4,512,128]{2,1,0:T(8,128)(2,1)}, u32[]{:S(2)}, u32[]{:S(2)}) collective-permute-start(bf16[4,512,128]{2,1,0:T(8,128)(2,1)} %get-tuple-element.93.refs_8_), channel_id=1, source_target_pairs={{0,24},{1,25},{2,26},{3,27},{4,28},{5,29},{6,30},{7,31},{8,16},{9,... | collective-permute-start | bytes 1572872 | tf_op jit(solution)/shard_map/v4/ppermute | solution.py:71
  83.2 4.6 %spread.2.refs_2_ = bf16[16896,256]{1,0:T(8,128)(2,1)S(1)} custom-call(s32[4]{0:T(128)S(1)} %copy-done.30, bf16[49280,128]{1,0:T(8,128)(2,1)} %all-gather.2.cloned.1.call-done.loads), custom_call_target="tpu_custom_call" | custom-call | tf_op jit(solution)/shard_map/spread/pallas_call | solution.py:168
  89.1 2.8 %collective-permute-start.25 = (bf16[4,512,128]{2,1,0:T(8,128)(2,1)}, bf16[4,512,128]{2,1,0:T(8,128)(2,1)S(1)}, u32[]{:S(2)}, u32[]{:S(2)}) collective-permute-start(bf16[4,512,128]{2,1,0:T(8,128)(2,1)} %get-tuple-element.108.refs_12_), channel_id=1, source_target_pairs={{0,1},{1,2},{2,3},{3,4},{4,5},{5,6},{6,7},{7,0},{8,9},{9,10},{10,1... | collective-permute-start | bytes 1572872 | tf_op jit(solution)/shard_map/q6/ppermute | solution.py:71
  91.9 1.7 %collective-permute-start.26 = (bf16[4,512,128]{2,1,0:T(8,128)(2,1)}, bf16[4,512,128]{2,1,0:T(8,128)(2,1)S(1)}, u32[]{:S(2)}, u32[]{:S(2)}) collective-permute-start(bf16[4,512,128]{2,1,0:T(8,128)(2,1)} %get-tuple-element.108.refs_12_), channel_id=1, source_target_pairs={{0,24},{1,25},{2,26},{3,27},{4,28},{5,29},{6,30},{7,31},{8,16},{9,... | collective-permute-start | bytes 1572872 | tf_op jit(solution)/shard_map/v5/ppermute | solution.py:71
  93.6 4.6 %spread.3.refs_1_ = bf16[16896,256]{1,0:T(8,128)(2,1)S(1)} custom-call(s32[4]{0:T(128)S(1)} %copy-done.30, bf16[49280,128]{1,0:T(8,128)(2,1)} %all-gather.2.cloned.1.call-done.loads), custom_call_target="tpu_custom_call" | custom-call | tf_op jit(solution)/shard_map/spread/pallas_call | solution.py:168
  98.4 3.4 %terms.4.refs_3_ = f32[512,512]{1,0:T(8,128)S(1)} custom-call(bf16[16896,256]{1,0:T(8,128)(2,1)S(1)} %get-tuple-element.90.refs_0_, bf16[16896,256]{1,0:T(8,128)(2,1)S(1)} %spread.3.refs_1_, bf16[4,512,128]{2,1,0:T(8,128)(2,1)S(1)} %bitcast.8, bf16[4,512,128]{2,1,0:T(8,128)(2,1)S(1)} %get-tuple-element.68.refs_3_.refs_6_, ...), custom_call_target="tpu_custom_call" | custom-call | tf_op jit(solution)/shard_map/terms/pallas_call | solution.py:202
  101.8 1.6 %collective-permute-start.27 = (bf16[4,512,128]{2,1,0:T(8,128)(2,1)S(1)}, bf16[4,512,128]{2,1,0:T(8,128)(2,1)S(1)}, u32[]{:S(2)}, u32[]{:S(2)}) collective-permute-start(bf16[4,512,128]{2,1,0:T(8,128)(2,1)S(1)} %get-tuple-element.114.refs_7_), channel_id=1, source_target_pairs={{0,24},{1,25},{2,26},{3,27},{4,28},{5,29},{6,30},{7,31},{8,16},{9,... | collective-permute-start | bytes 1572872 | tf_op jit(solution)/shard_map/u7/ppermute | solution.py:71
  103.9 1.4 %collective-permute-start.30 = (bf16[4,512,128]{2,1,0:T(8,128)(2,1)S(1)}, bf16[4,512,128]{2,1,0:T(8,128)(2,1)S(1)}, u32[]{:S(2)}, u32[]{:S(2)}) collective-permute-start(bf16[4,512,128]{2,1,0:T(8,128)(2,1)S(1)} %get-tuple-element.112.refs_5_), channel_id=1, source_target_pairs={{0,24},{1,25},{2,26},{3,27},{4,28},{5,29},{6,30},{7,31},{8,16},{9,... | collective-permute-start | bytes 1572872 | tf_op jit(solution)/shard_map/v6/ppermute | solution.py:71
  105.5 4.7 %terms.5.refs_2_ = f32[512,512]{1,0:T(8,128)S(1)} custom-call(bf16[16896,256]{1,0:T(8,128)(2,1)S(1)} %get-tuple-element.90.refs_0_, bf16[16896,256]{1,0:T(8,128)(2,1)S(1)} %spread.3.refs_1_, f32[512,512]{1,0:T(8,128)S(1)} %get-tuple-element.103.refs_2_, bf16[4,512,128]{2,1,0:T(8,128)(2,1)S(1)} %copy-done.21, bf16[4,512,128]{2,1,0:T(8,128)(2,1)S(1)} %copy-done.27, ...), custom_call_target="tpu_custom_call" | custom-call | tf_op jit(solution)/shard_map/terms/pallas_call | solution.py:202
  110.1 2.2 %collective-permute-done.27.refs_8_ = bf16[4,512,128]{2,1,0:T(8,128)(2,1)S(1)} collective-permute-done((bf16[4,512,128]{2,1,0:T(8,128)(2,1)S(1)}, bf16[4,512,128]{2,1,0:T(8,128)(2,1)S(1)}, u32[]{:S(2)}, u32[]{:S(2)}) %collective-permute-start.27) | collective-permute-done | bytes 524320 | tf_op jit(solution)/shard_map/u7/ppermute | solution.py:71
  112.3 1.5 %collective-permute-done.28.refs_9_ = bf16[4,512,128]{2,1,0:T(8,128)(2,1)S(1)} collective-permute-done((bf16[4,512,128]{2,1,0:T(8,128)(2,1)S(1)}, bf16[4,512,128]{2,1,0:T(8,128)(2,1)S(1)}, u32[]{:S(2)}, u32[]{:S(2)}) %collective-permute-start.28) | collective-permute-done | bytes 524320 | tf_op jit(solution)/shard_map/v7/ppermute | solution.py:71
  113.8 2.1 %terms.6.refs_2_ = f32[512,512]{1,0:T(8,128)S(1)} custom-call(bf16[16896,256]{1,0:T(8,128)(2,1)S(1)} %get-tuple-element.90.refs_0_, bf16[16896,256]{1,0:T(8,128)(2,1)S(1)} %spread.3.refs_1_, f32[512,512]{1,0:T(8,128)S(1)} %terms.5.refs_2_, bf16[4,512,128]{2,1,0:T(8,128)(2,1)S(1)} %get-tuple-element.111.refs_3_, ...), custom_call_target="tpu_custom_call" | custom-call | tf_op jit(solution)/shard_map/terms/pallas_call | solution.py:202
  115.9 2.1 %collective-permute-done.30.refs_4_ = bf16[4,512,128]{2,1,0:T(8,128)(2,1)S(1)} collective-permute-done((bf16[4,512,128]{2,1,0:T(8,128)(2,1)S(1)}, bf16[4,512,128]{2,1,0:T(8,128)(2,1)S(1)}, u32[]{:S(2)}, u32[]{:S(2)}) %collective-permute-start.30) | collective-permute-done | bytes 524320 | tf_op jit(solution)/shard_map/v6/ppermute | solution.py:71
  117.9 1.5 %collective-permute-done.29.refs_3_ = bf16[4,512,128]{2,1,0:T(8,128)(2,1)S(1)} collective-permute-done((bf16[4,512,128]{2,1,0:T(8,128)(2,1)S(1)}, bf16[4,512,128]{2,1,0:T(8,128)(2,1)S(1)}, u32[]{:S(2)}, u32[]{:S(2)}) %collective-permute-start.29) | collective-permute-done | bytes 524320 | tf_op jit(solution)/shard_map/q7/ppermute | solution.py:71
  (132 shorter events, 12.5 us)
Async XLA Ops:
  6.5 76.6 %all-gather.2.cloned.1.call-start = ((), (), s32[]{:S(2)}) async-start(), calls=%async_computation | async-start | bytes 14192640 | tf_op jit(solution)/shard_map/loads/all_gather | solution.py:219
  10.6 13.8 %collective-permute-start = (bf16[4,512,128]{2,1,0:T(8,128)(2,1)S(1)}, bf16[4,512,128]{2,1,0:T(8,128)(2,1)S(1)}, u32[]{:S(2)}, u32[]{:S(2)}) collective-permute-start(bf16[4,512,128]{2,1,0:T(8,128)(2,1)S(1)} %bitcast.4), channel_id=1, source_target_pairs={{0,1},{1,2},{2,3},{3,4},{4,5},{5,6},{6,7},{7,0},{8,9},{9,10},{10,1... | collective-permute-start | bytes 1572872 | tf_op jit(solution)/shard_map/s1/ppermute | solution.py:71
  13.8 18.6 %collective-permute-start.1 = (bf16[4,512,128]{2,1,0:T(8,128)(2,1)S(1)}, bf16[4,512,128]{2,1,0:T(8,128)(2,1)S(1)}, u32[]{:S(2)}, u32[]{:S(2)}) collective-permute-start(bf16[4,512,128]{2,1,0:T(8,128)(2,1)S(1)} %bitcast.5), channel_id=1, source_target_pairs={{0,8},{1,9},{2,10},{3,11},{4,12},{5,13},{6,14},{7,15},{8,0},{9,1},... | collective-permute-start | bytes 1572872 | tf_op jit(solution)/shard_map/q0/ppermute | solution.py:71
  15.4 17.2 %collective-permute-start.2 = (bf16[4,512,128]{2,1,0:T(8,128)(2,1)S(1)}, bf16[4,512,128]{2,1,0:T(8,128)(2,1)S(1)}, u32[]{:S(2)}, u32[]{:S(2)}) collective-permute-start(bf16[4,512,128]{2,1,0:T(8,128)(2,1)S(1)} %bitcast.6), channel_id=1, source_target_pairs={{0,24},{1,25},{2,26},{3,27},{4,28},{5,29},{6,30},{7,31},{8,16},{9,... | collective-permute-start | bytes 1572872 | tf_op jit(solution)/shard_map/u0/ppermute | solution.py:71
  17.6 15.1 %collective-permute-start.3 = (bf16[4,512,128]{2,1,0:T(8,128)(2,1)S(1)}, bf16[4,512,128]{2,1,0:T(8,128)(2,1)S(1)}, u32[]{:S(2)}, u32[]{:S(2)}) collective-permute-start(bf16[4,512,128]{2,1,0:T(8,128)(2,1)S(1)} %bitcast.7), channel_id=1, source_target_pairs={{0,7},{1,0},{2,1},{3,2},{4,3},{5,4},{6,5},{7,6},{8,15},{9,8},{10,9... | collective-permute-start | bytes 1572872 | tf_op jit(solution)/shard_map/s7/ppermute | solution.py:71
  24.4 10.4 %collective-permute-start.4 = (bf16[4,512,128]{2,1,0:T(8,128)(2,1)S(1)}, bf16[4,512,128]{2,1,0:T(8,128)(2,1)S(1)}, u32[]{:S(2)}, u32[]{:S(2)}) collective-permute-start(bf16[4,512,128]{2,1,0:T(8,128)(2,1)S(1)} %get-tuple-element.65.refs_6_), channel_id=1, source_target_pairs={{0,1},{1,2},{2,3},{3,4},{4,5},{5,6},{6,7},{7,0},{8,9},{9,10},{10,1... | collective-permute-start | bytes 1572872 | tf_op jit(solution)/shard_map/s2/ppermute | solution.py:71
  28.1 14.8 %collective-permute-start.5 = (bf16[4,512,128]{2,1,0:T(8,128)(2,1)S(1)}, bf16[4,512,128]{2,1,0:T(8,128)(2,1)S(1)}, u32[]{:S(2)}, u32[]{:S(2)}) collective-permute-start(bf16[4,512,128]{2,1,0:T(8,128)(2,1)S(1)} %get-tuple-element.65.refs_6_), channel_id=1, source_target_pairs={{0,24},{1,25},{2,26},{3,27},{4,28},{5,29},{6,30},{7,31},{8,16},{9,... | collective-permute-start | bytes 1572872 | tf_op jit(solution)/shard_map/u1/ppermute | solution.py:71
  32.4 10.4 %collective-permute-start.6 = (bf16[4,512,128]{2,1,0:T(8,128)(2,1)S(1)}, bf16[4,512,128]{2,1,0:T(8,128)(2,1)S(1)}, u32[]{:S(2)}, u32[]{:S(2)}) collective-permute-start(bf16[4,512,128]{2,1,0:T(8,128)(2,1)S(1)} %get-tuple-element.68.refs_3_.refs_6_), channel_id=1, source_target_pairs={{0,1},{1,2},{2,3},{3,4},{4,5},{5,6},{6,7},{7,0},{8,9},{9,10},{10,1... | collective-permute-start | bytes 1572872 | tf_op jit(solution)/shard_map/q1/ppermute | solution.py:71
  32.5 15.9 %collective-permute-start.7 = (bf16[4,512,128]{2,1,0:T(8,128)(2,1)S(1)}, bf16[4,512,128]{2,1,0:T(8,128)(2,1)S(1)}, u32[]{:S(2)}, u32[]{:S(2)}) collective-permute-start(bf16[4,512,128]{2,1,0:T(8,128)(2,1)S(1)} %get-tuple-element.68.refs_3_.refs_6_), channel_id=1, source_target_pairs={{0,24},{1,25},{2,26},{3,27},{4,28},{5,29},{6,30},{7,31},{8,16},{9,... | collective-permute-start | bytes 1572872 | tf_op jit(solution)/shard_map/v0/ppermute | solution.py:71
  34.8 13.7 %collective-permute-start.8 = (bf16[4,512,128]{2,1,0:T(8,128)(2,1)S(1)}, bf16[4,512,128]{2,1,0:T(8,128)(2,1)S(1)}, u32[]{:S(2)}, u32[]{:S(2)}) collective-permute-start(bf16[4,512,128]{2,1,0:T(8,128)(2,1)S(1)} %get-tuple-element.71.refs_10_), channel_id=1, source_target_pairs={{0,1},{1,2},{2,3},{3,4},{4,5},{5,6},{6,7},{7,0},{8,9},{9,10},{10,1... | collective-permute-start | bytes 1572872 | tf_op jit(solution)/shard_map/s3/ppermute | solution.py:71
  38.4 15.6 %collective-permute-start.9 = (bf16[4,512,128]{2,1,0:T(8,128)(2,1)S(1)}, bf16[4,512,128]{2,1,0:T(8,128)(2,1)S(1)}, u32[]{:S(2)}, u32[]{:S(2)}) collective-permute-start(bf16[4,512,128]{2,1,0:T(8,128)(2,1)S(1)} %get-tuple-element.71.refs_10_), channel_id=1, source_target_pairs={{0,24},{1,25},{2,26},{3,27},{4,28},{5,29},{6,30},{7,31},{8,16},{9,... | collective-permute-start | bytes 1572872 | tf_op jit(solution)/shard_map/u2/ppermute | solution.py:71
  42.9 11.2 %collective-permute-start.10 = (bf16[4,512,128]{2,1,0:T(8,128)(2,1)S(1)}, bf16[4,512,128]{2,1,0:T(8,128)(2,1)S(1)}, u32[]{:S(2)}, u32[]{:S(2)}) collective-permute-start(bf16[4,512,128]{2,1,0:T(8,128)(2,1)S(1)} %get-tuple-element.74.refs_7_), channel_id=1, source_target_pairs={{0,1},{1,2},{2,3},{3,4},{4,5},{5,6},{6,7},{7,0},{8,9},{9,10},{10,1... | collective-permute-start | bytes 1572872 | tf_op jit(solution)/shard_map/q2/ppermute | solution.py:71
  44.1 15.6 %collective-permute-start.11 = (bf16[4,512,128]{2,1,0:T(8,128)(2,1)S(1)}, bf16[4,512,128]{2,1,0:T(8,128)(2,1)S(1)}, u32[]{:S(2)}, u32[]{:S(2)}) collective-permute-start(bf16[4,512,128]{2,1,0:T(8,128)(2,1)S(1)} %get-tuple-element.74.refs_7_), channel_id=1, source_target_pairs={{0,24},{1,25},{2,26},{3,27},{4,28},{5,29},{6,30},{7,31},{8,16},{9,... | collective-permute-start | bytes 1572872 | tf_op jit(solution)/shard_map/v1/ppermute | solution.py:71
  48.5 11.2 %collective-permute-start.12 = (bf16[4,512,128]{2,1,0:T(8,128)(2,1)S(1)}, bf16[4,512,128]{2,1,0:T(8,128)(2,1)S(1)}, u32[]{:S(2)}, u32[]{:S(2)}) collective-permute-start(bf16[4,512,128]{2,1,0:T(8,128)(2,1)S(1)} %get-tuple-element.77.refs_3_), channel_id=1, source_target_pairs={{0,1},{1,2},{2,3},{3,4},{4,5},{5,6},{6,7},{7,0},{8,9},{9,10},{10,1... | collective-permute-start | bytes 1572872 | tf_op jit(solution)/shard_map/s4/ppermute | solution.py:71
  49.7 15.6 %collective-permute-start.13 = (bf16[4,512,128]{2,1,0:T(8,128)(2,1)S(1)}, bf16[4,512,128]{2,1,0:T(8,128)(2,1)S(1)}, u32[]{:S(2)}, u32[]{:S(2)}) collective-permute-start(bf16[4,512,128]{2,1,0:T(8,128)(2,1)S(1)} %get-tuple-element.77.refs_3_), channel_id=1, source_target_pairs={{0,24},{1,25},{2,26},{3,27},{4,28},{5,29},{6,30},{7,31},{8,16},{9,... | collective-permute-start | bytes 1572872 | tf_op jit(solution)/shard_map/u3/ppermute | solution.py:71
  54.1 11.2 %collective-permute-start.14 = (bf16[4,512,128]{2,1,0:T(8,128)(2,1)S(1)}, bf16[4,512,128]{2,1,0:T(8,128)(2,1)S(1)}, u32[]{:S(2)}, u32[]{:S(2)}) collective-permute-start(bf16[4,512,128]{2,1,0:T(8,128)(2,1)S(1)} %get-tuple-element.80.refs_11_), channel_id=1, source_target_pairs={{0,1},{1,2},{2,3},{3,4},{4,5},{5,6},{6,7},{7,0},{8,9},{9,10},{10,1... | collective-permute-start | bytes 1572872 | tf_op jit(solution)/shard_map/q3/ppermute | solution.py:71
  55.3 15.6 %collective-permute-start.15 = (bf16[4,512,128]{2,1,0:T(8,128)(2,1)S(1)}, bf16[4,512,128]{2,1,0:T(8,128)(2,1)S(1)}, u32[]{:S(2)}, u32[]{:S(2)}) collective-permute-start(bf16[4,512,128]{2,1,0:T(8,128)(2,1)S(1)} %get-tuple-element.80.refs_11_), channel_id=1, source_target_pairs={{0,24},{1,25},{2,26},{3,27},{4,28},{5,29},{6,30},{7,31},{8,16},{9,... | collective-permute-start | bytes 1572872 | tf_op jit(solution)/shard_map/v2/ppermute | solution.py:71
  59.7 11.2 %collective-permute-start.16 = (bf16[4,512,128]{2,1,0:T(8,128)(2,1)S(1)}, bf16[4,512,128]{2,1,0:T(8,128)(2,1)}, u32[]{:S(2)}, u32[]{:S(2)}) collective-permute-start(bf16[4,512,128]{2,1,0:T(8,128)(2,1)S(1)} %get-tuple-element.83.refs_7_), channel_id=1, source_target_pairs={{0,1},{1,2},{2,3},{3,4},{4,5},{5,6},{6,7},{7,0},{8,9},{9,10},{10,1... | collective-permute-start | bytes 1572872 | tf_op jit(solution)/shard_map/s5/ppermute | solution.py:71
  60.9 15.7 %collective-permute-start.17 = (bf16[4,512,128]{2,1,0:T(8,128)(2,1)S(1)}, bf16[4,512,128]{2,1,0:T(8,128)(2,1)S(1)}, u32[]{:S(2)}, u32[]{:S(2)}) collective-permute-start(bf16[4,512,128]{2,1,0:T(8,128)(2,1)S(1)} %get-tuple-element.83.refs_7_), channel_id=1, source_target_pairs={{0,24},{1,25},{2,26},{3,27},{4,28},{5,29},{6,30},{7,31},{8,16},{9,... | collective-permute-start | bytes 1572872 | tf_op jit(solution)/shard_map/u4/ppermute | solution.py:71
  65.3 11.3 %collective-permute-start.18 = (bf16[4,512,128]{2,1,0:T(8,128)(2,1)S(1)}, bf16[4,512,128]{2,1,0:T(8,128)(2,1)}, u32[]{:S(2)}, u32[]{:S(2)}) collective-permute-start(bf16[4,512,128]{2,1,0:T(8,128)(2,1)S(1)} %get-tuple-element.86.refs_4_), channel_id=1, source_target_pairs={{0,1},{1,2},{2,3},{3,4},{4,5},{5,6},{6,7},{7,0},{8,9},{9,10},{10,1... | collective-permute-start | bytes 1572872 | tf_op jit(solution)/shard_map/q4/ppermute | solution.py:71
  66.5 15.7 %collective-permute-start.19 = (bf16[4,512,128]{2,1,0:T(8,128)(2,1)S(1)}, bf16[4,512,128]{2,1,0:T(8,128)(2,1)S(1)}, u32[]{:S(2)}, u32[]{:S(2)}) collective-permute-start(bf16[4,512,128]{2,1,0:T(8,128)(2,1)S(1)} %get-tuple-element.86.refs_4_), channel_id=1, source_target_pairs={{0,24},{1,25},{2,26},{3,27},{4,28},{5,29},{6,30},{7,31},{8,16},{9,... | collective-permute-start | bytes 1572872 | tf_op jit(solution)/shard_map/v3/ppermute | solution.py:71
  71.0 16.8 %collective-permute-start.20 = (bf16[4,512,128]{2,1,0:T(8,128)(2,1)}, bf16[4,512,128]{2,1,0:T(8,128)(2,1)S(1)}, u32[]{:S(2)}, u32[]{:S(2)}) collective-permute-start(bf16[4,512,128]{2,1,0:T(8,128)(2,1)} %get-tuple-element.89.refs_11_), channel_id=1, source_target_pairs={{0,1},{1,2},{2,3},{3,4},{4,5},{5,6},{6,7},{7,0},{8,9},{9,10},{10,1... | collective-permute-start | bytes 1572872 | tf_op jit(solution)/shard_map/s6/ppermute | solution.py:71
  72.3 16.7 %collective-permute-start.21 = (bf16[4,512,128]{2,1,0:T(8,128)(2,1)}, bf16[4,512,128]{2,1,0:T(8,128)(2,1)S(1)}, u32[]{:S(2)}, u32[]{:S(2)}) collective-permute-start(bf16[4,512,128]{2,1,0:T(8,128)(2,1)} %get-tuple-element.89.refs_11_), channel_id=1, source_target_pairs={{0,24},{1,25},{2,26},{3,27},{4,28},{5,29},{6,30},{7,31},{8,16},{9,... | collective-permute-start | bytes 1572872 | tf_op jit(solution)/shard_map/u5/ppermute | solution.py:71
  76.7 12.3 %collective-permute-start.22 = (bf16[4,512,128]{2,1,0:T(8,128)(2,1)}, bf16[4,512,128]{2,1,0:T(8,128)(2,1)}, u32[]{:S(2)}, u32[]{:S(2)}) collective-permute-start(bf16[4,512,128]{2,1,0:T(8,128)(2,1)} %get-tuple-element.93.refs_8_), channel_id=1, source_target_pairs={{0,1},{1,2},{2,3},{3,4},{4,5},{5,6},{6,7},{7,0},{8,9},{9,10},{10,1... | collective-permute-start | bytes 1572872 | tf_op jit(solution)/shard_map/q5/ppermute | solution.py:71
  77.9 23.9 %collective-permute-start.23 = (bf16[4,512,128]{2,1,0:T(8,128)(2,1)}, bf16[4,512,128]{2,1,0:T(8,128)(2,1)}, u32[]{:S(2)}, u32[]{:S(2)}) collective-permute-start(bf16[4,512,128]{2,1,0:T(8,128)(2,1)} %get-tuple-element.93.refs_8_), channel_id=1, source_target_pairs={{0,24},{1,25},{2,26},{3,27},{4,28},{5,29},{6,30},{7,31},{8,16},{9,... | collective-permute-start | bytes 1572872 | tf_op jit(solution)/shard_map/v4/ppermute | solution.py:71
  87.8 14.0 %collective-permute-start.24 = (bf16[4,512,128]{2,1,0:T(8,128)(2,1)S(1)}, bf16[4,512,128]{2,1,0:T(8,128)(2,1)S(1)}, u32[]{:S(2)}, u32[]{:S(2)}) collective-permute-start(bf16[4,512,128]{2,1,0:T(8,128)(2,1)S(1)} %get-tuple-element.95.refs_4_), channel_id=1, source_target_pairs={{0,24},{1,25},{2,26},{3,27},{4,28},{5,29},{6,30},{7,31},{8,16},{9,... | collective-permute-start | bytes 1572872 | tf_op jit(solution)/shard_map/u6/ppermute | solution.py:71
  89.1 14.4 %collective-permute-start.25 = (bf16[4,512,128]{2,1,0:T(8,128)(2,1)}, bf16[4,512,128]{2,1,0:T(8,128)(2,1)S(1)}, u32[]{:S(2)}, u32[]{:S(2)}) collective-permute-start(bf16[4,512,128]{2,1,0:T(8,128)(2,1)} %get-tuple-element.108.refs_12_), channel_id=1, source_target_pairs={{0,1},{1,2},{2,3},{3,4},{4,5},{5,6},{6,7},{7,0},{8,9},{9,10},{10,1... | collective-permute-start | bytes 1572872 | tf_op jit(solution)/shard_map/q6/ppermute | solution.py:71
  91.9 12.0 %collective-permute-start.26 = (bf16[4,512,128]{2,1,0:T(8,128)(2,1)}, bf16[4,512,128]{2,1,0:T(8,128)(2,1)S(1)}, u32[]{:S(2)}, u32[]{:S(2)}) collective-permute-start(bf16[4,512,128]{2,1,0:T(8,128)(2,1)} %get-tuple-element.108.refs_12_), channel_id=1, source_target_pairs={{0,24},{1,25},{2,26},{3,27},{4,28},{5,29},{6,30},{7,31},{8,16},{9,... | collective-permute-start | bytes 1572872 | tf_op jit(solution)/shard_map/v5/ppermute | solution.py:71
  101.8 10.5 %collective-permute-start.27 = (bf16[4,512,128]{2,1,0:T(8,128)(2,1)S(1)}, bf16[4,512,128]{2,1,0:T(8,128)(2,1)S(1)}, u32[]{:S(2)}, u32[]{:S(2)}) collective-permute-start(bf16[4,512,128]{2,1,0:T(8,128)(2,1)S(1)} %get-tuple-element.114.refs_7_), channel_id=1, source_target_pairs={{0,24},{1,25},{2,26},{3,27},{4,28},{5,29},{6,30},{7,31},{8,16},{9,... | collective-permute-start | bytes 1572872 | tf_op jit(solution)/shard_map/u7/ppermute | solution.py:71
  103.4 10.4 %collective-permute-start.28 = (bf16[4,512,128]{2,1,0:T(8,128)(2,1)S(1)}, bf16[4,512,128]{2,1,0:T(8,128)(2,1)S(1)}, u32[]{:S(2)}, u32[]{:S(2)}) collective-permute-start(bf16[4,512,128]{2,1,0:T(8,128)(2,1)S(1)} %get-tuple-element.115), channel_id=1, source_target_pairs={{0,7},{1,0},{2,1},{3,2},{4,3},{5,4},{6,5},{7,6},{8,15},{9,8},{10,9... | collective-permute-start | bytes 1572872 | tf_op jit(solution)/shard_map/v7/ppermute | solution.py:71
  103.9 14.0 %collective-permute-start.30 = (bf16[4,512,128]{2,1,0:T(8,128)(2,1)S(1)}, bf16[4,512,128]{2,1,0:T(8,128)(2,1)S(1)}, u32[]{:S(2)}, u32[]{:S(2)}) collective-permute-start(bf16[4,512,128]{2,1,0:T(8,128)(2,1)S(1)} %get-tuple-element.112.refs_5_), channel_id=1, source_target_pairs={{0,24},{1,25},{2,26},{3,27},{4,28},{5,29},{6,30},{7,31},{8,16},{9,... | collective-permute-start | bytes 1572872 | tf_op jit(solution)/shard_map/v6/ppermute | solution.py:71
  105.2 14.2 %collective-permute-start.29 = (bf16[4,512,128]{2,1,0:T(8,128)(2,1)S(1)}, bf16[4,512,128]{2,1,0:T(8,128)(2,1)S(1)}, u32[]{:S(2)}, u32[]{:S(2)}) collective-permute-start(bf16[4,512,128]{2,1,0:T(8,128)(2,1)S(1)} %get-tuple-element.116), channel_id=1, source_target_pairs={{0,7},{1,0},{2,1},{3,2},{4,3},{5,4},{6,5},{7,6},{8,15},{9,8},{10,9... | collective-permute-start | bytes 1572872 | tf_op jit(solution)/shard_map/q7/ppermute | solution.py:71
  (32 other events, 545.5 us)
Sparse Core Ops, SparseCore 0:
  9.6 71.8 all-gather.1
